TPU v7x, 32 devices: a whole 2x2x4 slice. The times are simulated.
32 devices in a mesh: dp: 8 (over y, x, core), mp: 4 (over z).
Axes of the slice: x: 2, y: 2, z: 4, core: 2. Of those that a mesh axis runs over, the one named last changes fastest.
Arguments:
- patches: bfloat16 [16384, 768], P('dp'), may hold values from -6 to 6
- segment: int32 [16384], P('dp'), may hold values from 0 to 16, as said below
- keep: int32 [16384], P('dp'), may hold values 0 or 1
- pos_y: int32 [16384], P('dp'), may hold values from 0 to 31
- pos_x: int32 [16384], P('dp'), may hold values from 0 to 31
- labels: int32 [128], P('dp'), may hold values from 0 to 999
- bucket: int32 [8], P('dp'), may hold values from 0 to 3
- attend_in: float32 [768, 2304], P('dp', 'mp'), may hold values from -0.21875 to 0.21875
- attend_in_first: float32 [768, 2304], P('dp', 'mp'), may hold values from -2.2888184e-05 to 2.2888184e-05
- attend_in_second: float32 [768, 2304], P('dp', 'mp'), may hold values from 5.890625e-12 to 8.246875e-11
- attend_out: float32 [768, 768], P('mp', 'dp'), may hold values from -0.625 to 0.625
- attend_out_first: float32 [768, 768], P('mp', 'dp'), may hold values from -2.2888184e-05 to 2.2888184e-05
- attend_out_second: float32 [768, 768], P('mp', 'dp'), may hold values from 5.890625e-12 to 8.246875e-11
- expand: float32 [768, 3072], P('dp', 'mp'), may hold values from -0.21875 to 0.21875
- expand_first: float32 [768, 3072], P('dp', 'mp'), may hold values from -2.2888184e-05 to 2.2888184e-05
- expand_second: float32 [768, 3072], P('dp', 'mp'), may hold values from 5.890625e-12 to 8.246875e-11
- contract: float32 [3072, 768], P('mp', 'dp'), may hold values from -0.109375 to 0.109375
- contract_first: float32 [3072, 768], P('mp', 'dp'), may hold values from -2.2888184e-05 to 2.2888184e-05
- contract_second: float32 [3072, 768], P('mp', 'dp'), may hold values from 5.890625e-12 to 8.246875e-11
- patch_embed: float32 [768, 768], P('dp'), may hold values from -0.21875 to 0.21875
- patch_embed_first: float32 [768, 768], P('dp'), may hold values from -2.2888184e-05 to 2.2888184e-05
- patch_embed_second: float32 [768, 768], P('dp'), may hold values from 5.890625e-12 to 8.246875e-11
- position_table: float32 [64, 768], P(None, 'dp'), may hold values from -1.5 to 1.5
- position_table_first: float32 [64, 768], P(None, 'dp'), may hold values from -2.2888184e-05 to 2.2888184e-05
- position_table_second: float32 [64, 768], P(None, 'dp'), may hold values from 5.890625e-12 to 8.246875e-11
- class_head: float32 [768, 1000], P('dp'), may hold values from -0.21875 to 0.21875
- class_head_first: float32 [768, 1000], P('dp'), may hold values from -2.2888184e-05 to 2.2888184e-05
- class_head_second: float32 [768, 1000], P('dp'), may hold values from 5.890625e-12 to 8.246875e-11
- norm_gains: float32 [4, 768], P(None, 'dp'), may hold values from 0.5 to 1.5
- norm_gains_first: float32 [4, 768], P(None, 'dp'), may hold values from -9.1552734e-05 to 9.1552734e-05
- norm_gains_second: float32 [4, 768], P(None, 'dp'), may hold values from 9.425e-11 to 1.2959375e-09
- query_gains: float32 [2, 64], P(None, 'dp'), may hold values from 0.5 to 1.5
- query_gains_first: float32 [2, 64], P(None, 'dp'), may hold values from -9.1552734e-05 to 9.1552734e-05
- query_gains_second: float32 [2, 64], P(None, 'dp'), may hold values from 9.425e-11 to 1.2959375e-09
Outputs:
- bucket_loss: float32 [4], replicated
- bucket_count: float32 [4], replicated
- grad_norm: float32 [], replicated
- attend_in_new: float32 [768, 2304], P('dp', 'mp')
- attend_in_first_new: float32 [768, 2304], P('dp', 'mp')
- attend_in_second_new: float32 [768, 2304], P('dp', 'mp')
- attend_out_new: float32 [768, 768], P('mp', 'dp')
- attend_out_first_new: float32 [768, 768], P('mp', 'dp')
- attend_out_second_new: float32 [768, 768], P('mp', 'dp')
- expand_new: float32 [768, 3072], P('dp', 'mp')
- expand_first_new: float32 [768, 3072], P('dp', 'mp')
- expand_second_new: float32 [768, 3072], P('dp', 'mp')
- contract_new: float32 [3072, 768], P('mp', 'dp')
- contract_first_new: float32 [3072, 768], P('mp', 'dp')
- contract_second_new: float32 [3072, 768], P('mp', 'dp')
- patch_embed_new: float32 [768, 768], P('dp')
- patch_embed_first_new: float32 [768, 768], P('dp')
- patch_embed_second_new: float32 [768, 768], P('dp')
- position_table_new: float32 [64, 768], P(None, 'dp')
- position_table_first_new: float32 [64, 768], P(None, 'dp')
- position_table_second_new: float32 [64, 768], P(None, 'dp')
- class_head_new: float32 [768, 1000], P('dp')
- class_head_first_new: float32 [768, 1000], P('dp')
- class_head_second_new: float32 [768, 1000], P('dp')
- norm_gains_new: float32 [4, 768], P(None, 'dp')
- norm_gains_first_new: float32 [4, 768], P(None, 'dp')
- norm_gains_second_new: float32 [4, 768], P(None, 'dp')
- query_gains_new: float32 [2, 64], P(None, 'dp')
- query_gains_first_new: float32 [2, 64], P(None, 'dp')
- query_gains_second_new: float32 [2, 64], P(None, 'dp')
Inputs may be any that keep to these rules, and one draw needn't show every extreme that they name: `segment`: within each sequence the image numbers never fall along the slots, images 0 to n - 1 hold one or more slots each, images n to 15 hold none, and the slots after them are padding with number 16.
All inputs are finite; a program needn't handle non-finite values. No bound on the sum of `keep` on one device may be relied on, other than what follows from the above.
Results may differ from a plain program's by a relative error of at most 0.017.
Values may be sent and summed in bfloat16 or wider, within the bound.
No kernel may reach another device: no remote copies, remote signals or barrier semaphores. Data moves between devices by JAX's collectives and lax.ppermute only.
A program may use at most 192 MiB of HBM per device.

v0:
```python
import jax
import jax.numpy as jnp
from jax import lax
from jax.sharding import PartitionSpec as P

D = 768
HD = 64
CLASSES = 1000
GRID = 32
IMG = 16
NB = 4
STEP = 10


HIGH = lax.Precision.HIGHEST
NORM_EPS = 1e-06
CLIP = 0.1
BETA_ONE = 0.9
BETA_TWO = 0.95
RATE_MATRIX = 0.05
RATE_SMALL = 0.2
DECAY = 0.05
ADAM_EPS = 1e-08
NEG = -1e30


def layer_norm(values, gain):
    center = values - jnp.mean(values, axis=-1, keepdims=True)
    inv_std = lax.rsqrt(jnp.mean(center * center, axis=-1, keepdims=True) + NORM_EPS)
    scaled = center * inv_std
    return (scaled * gain, scaled, inv_std)


def norm_back(grad_out, scaled, inv_std, gain):
    grad_scaled = grad_out * gain
    grad_in = inv_std * (
        grad_scaled
        - jnp.mean(grad_scaled, axis=-1, keepdims=True)
        - scaled * jnp.mean(grad_scaled * scaled, axis=-1, keepdims=True)
    )
    return (grad_in, grad_out * scaled)


def allowed_mask(seg_rows, segment, kept, row_ids, col_ids):
    same = (seg_rows[:, None] == segment[None, :]) & kept[None, :]
    return same | (row_ids[:, None] == col_ids[None, :])


def local(
    patches,
    segment,
    keep,
    pos_y,
    pos_x,
    labels,
    bucket,
    attend_in,
    attend_in_first,
    attend_in_second,
    attend_out,
    attend_out_first,
    attend_out_second,
    expand,
    expand_first,
    expand_second,
    contract,
    contract_first,
    contract_second,
    patch_embed,
    patch_embed_first,
    patch_embed_second,
    position_table,
    position_table_first,
    position_table_second,
    class_head,
    class_head_first,
    class_head_second,
    norm_gains,
    norm_gains_first,
    norm_gains_second,
    query_gains,
    query_gains_first,
    query_gains_second,
):
    bf16 = jnp.bfloat16
    f32 = jnp.float32
    masters = (
        attend_in,
        attend_out,
        expand,
        contract,
        patch_embed,
        position_table,
        class_head,
        norm_gains,
        query_gains,
    )
    firsts = (
        attend_in_first,
        attend_out_first,
        expand_first,
        contract_first,
        patch_embed_first,
        position_table_first,
        class_head_first,
        norm_gains_first,
        query_gains_first,
    )
    seconds = (
        attend_in_second,
        attend_out_second,
        expand_second,
        contract_second,
        patch_embed_second,
        position_table_second,
        class_head_second,
        norm_gains_second,
        query_gains_second,
    )
    (
        in_proj,
        out_proj,
        up_proj,
        down_proj,
        patch_proj,
        pos_rows,
        head_proj,
        gain_rows,
        qgain_rows,
    ) = (
        lax.all_gather(attend_in.astype(bf16), "dp", axis=0, tiled=True),
        lax.all_gather(attend_out.astype(bf16), "dp", axis=1, tiled=True),
        lax.all_gather(expand.astype(bf16), "dp", axis=0, tiled=True),
        lax.all_gather(contract.astype(bf16), "dp", axis=1, tiled=True),
        lax.all_gather(patch_embed.astype(bf16), "dp", axis=0, tiled=True),
        lax.all_gather(position_table.astype(bf16), "dp", axis=1, tiled=True),
        lax.all_gather(class_head.astype(bf16), "dp", axis=0, tiled=True),
        lax.all_gather(norm_gains.astype(bf16), "dp", axis=1, tiled=True),
        lax.all_gather(query_gains.astype(bf16), "dp", axis=1, tiled=True),
    )
    gain_f = gain_rows.astype(f32)
    qgain_f = qgain_rows.astype(f32)
    length = patches.shape[0]
    heads_local = in_proj.shape[1] // (3 * HD)
    heads_all = D // HD
    block = min(512, length)
    count_blocks = length // block
    only_first = (lax.axis_index("mp") == 0).astype(f32)
    row_ids = jnp.arange(length)
    kept = (keep == 1) & (segment < IMG)
    onehot_y = (pos_y[:, None] == jnp.arange(GRID)[None, :]).astype(bf16)
    onehot_x = (pos_x[:, None] == jnp.arange(GRID)[None, :]).astype(bf16)
    embed = (
        jnp.dot(patches, patch_proj, preferred_element_type=f32)
        + jnp.dot(onehot_y, pos_rows[:GRID], preferred_element_type=f32)
        + jnp.dot(onehot_x, pos_rows[GRID:], preferred_element_type=f32)
    )
    normed_a, scaled_a, inv_a = layer_norm(embed, gain_f[0])
    normed_a_low = normed_a.astype(bf16)
    mixed = jnp.dot(normed_a_low, in_proj, preferred_element_type=f32).reshape(
        length, heads_local, 3, HD
    )
    query_n, query_s, query_i = layer_norm(mixed[:, :, 0], qgain_f[0])
    key_n, key_s, key_i = layer_norm(mixed[:, :, 1], qgain_f[1])
    query_low = (query_n * 0.125).astype(bf16)
    key_low = key_n.astype(bf16)
    value_low = mixed[:, :, 2].astype(bf16)
    query_blocks = query_low.reshape(count_blocks, block, heads_local, HD)
    seg_blocks = segment.reshape(count_blocks, block)
    id_blocks = row_ids.reshape(count_blocks, block)

    def attend_block(inputs):
        query_blk, seg_blk, ids_blk = inputs
        scores = jnp.einsum("thd,uhd->htu", query_blk, key_low, preferred_element_type=f32)
        allowed = allowed_mask(seg_blk, segment, kept, ids_blk, row_ids)
        scores = jnp.where(allowed[None], scores, NEG)
        top = jnp.max(scores, axis=-1, keepdims=True)
        expo = jnp.exp(scores - top)
        total = jnp.sum(expo, axis=-1, keepdims=True)
        probs = (expo / total).astype(bf16)
        out = jnp.einsum("htu,uhd->thd", probs, value_low, preferred_element_type=f32)
        return (out, top[..., 0] + jnp.log(total[..., 0]))

    attended, log_total = lax.map(attend_block, (query_blocks, seg_blocks, id_blocks))
    att_low = attended.reshape(length, heads_local * HD).astype(bf16)
    attn_term = jnp.dot(att_low, out_proj, preferred_element_type=f32)
    resid_mid = embed + lax.psum(attn_term.astype(jnp.bfloat16), "mp").astype(jnp.float32)
    normed_b, scaled_b, inv_b = layer_norm(resid_mid, gain_f[1])
    normed_b_low = normed_b.astype(bf16)
    upper = jnp.dot(normed_b_low, up_proj, preferred_element_type=f32)
    hidden_low = jax.nn.gelu(upper).astype(bf16)
    mlp_term = jnp.dot(hidden_low, down_proj, preferred_element_type=f32)
    resid_out = resid_mid + lax.psum(mlp_term.astype(jnp.bfloat16), "mp").astype(jnp.float32)
    final, scaled_f, inv_f = layer_norm(resid_out, gain_f[2])
    member = (segment[None, :] == jnp.arange(IMG)[:, None]) & kept[None, :]
    valid = jnp.any(member, axis=1).astype(f32)
    final_heads = final.reshape(length, heads_all, HD)
    probe = gain_f[3].reshape(heads_all, HD)
    tok_score = jnp.sum(final_heads * probe[None], axis=-1) * 0.125
    masked = jnp.where(member[:, :, None], tok_score[None], NEG)
    top = jnp.max(masked, axis=1, keepdims=True)
    weights_pool = jnp.where(member[:, :, None], jnp.exp(masked - top), 0.0)
    total = jnp.sum(weights_pool, axis=1) + (1.0 - valid)[:, None]
    attn_pool = weights_pool / total[:, None, :]
    pooled = jnp.einsum("ith,thd->ihd", attn_pool, final_heads, precision=HIGH)
    pooled_low = pooled.reshape(IMG, D).astype(bf16)
    logits = jnp.dot(pooled_low, head_proj, preferred_element_type=f32)
    label_hot = (labels[:, None] == jnp.arange(CLASSES)[None, :]).astype(f32)
    per_image = jnp.sum(jax.nn.softplus(logits), axis=1) - jnp.sum(logits * label_hot, axis=1)
    bucket_hot = (bucket[0] == jnp.arange(NB)).astype(f32)
    bucket_loss, bucket_count = lax.psum(
        (bucket_hot * jnp.sum(per_image * valid), bucket_hot * jnp.sum(valid)), "dp"
    )
    image_total = jnp.sum(bucket_count)
    grad_logits = ((valid / image_total)[:, None] * (jax.nn.sigmoid(logits) - label_hot)).astype(
        bf16
    )
    grad_head = jnp.dot(pooled_low.T, grad_logits, preferred_element_type=f32)
    grad_pooled = jnp.dot(grad_logits, head_proj.T, preferred_element_type=f32).reshape(
        IMG, heads_all, HD
    )
    grad_attn = jnp.einsum("ihd,thd->ith", grad_pooled, final_heads, precision=HIGH)
    grad_score = attn_pool * (grad_attn - jnp.sum(grad_pooled * pooled, axis=-1)[:, None, :])
    tok_grad = jnp.sum(grad_score, axis=0)
    grad_final = (
        jnp.einsum("ith,ihd->thd", attn_pool, grad_pooled, precision=HIGH)
        + tok_grad[:, :, None] * probe[None] * 0.125
    )
    grad_probe = 0.125 * jnp.sum(tok_grad[:, :, None] * final_heads, axis=0).reshape(D)
    grad_resid, gain_part_f = norm_back(grad_final.reshape(length, D), scaled_f, inv_f, gain_f[2])
    grad_out_low = grad_resid.astype(bf16)
    grad_down = jnp.dot(hidden_low.T, grad_out_low, preferred_element_type=f32)
    grad_hidden = jnp.dot(grad_out_low, down_proj.T, preferred_element_type=f32)
    grad_upper = jax.vjp(jax.nn.gelu, upper)[1](grad_hidden)[0].astype(bf16)
    grad_up = jnp.dot(normed_b_low.T, grad_upper, preferred_element_type=f32)
    back_term = jnp.dot(grad_upper, up_proj.T, preferred_element_type=f32)
    grad_normed_b = lax.psum(back_term.astype(jnp.bfloat16), "mp").astype(jnp.float32)
    grad_in_b, gain_part_b = norm_back(grad_normed_b, scaled_b, inv_b, gain_f[1])
    grad_mid = grad_resid + grad_in_b
    gain_b_term = only_first * jnp.sum(gain_part_b, axis=0)
    grad_mid_low = grad_mid.astype(bf16)
    grad_out_proj = jnp.dot(att_low.T, grad_mid_low, preferred_element_type=f32)
    grad_att = (
        jnp.dot(grad_mid_low, out_proj.T, preferred_element_type=f32)
        .astype(bf16)
        .reshape(count_blocks, block, heads_local, HD)
    )

    def back_block(carry, inputs):
        grad_key, grad_value = carry
        query_blk, grad_blk, total_blk, seg_blk, ids_blk = inputs
        scores = jnp.einsum("thd,uhd->htu", query_blk, key_low, preferred_element_type=f32)
        allowed = allowed_mask(seg_blk, segment, kept, ids_blk, row_ids)
        probs = jnp.where(allowed[None], jnp.exp(scores - total_blk[:, :, None]), 0.0)
        grad_value = grad_value + jnp.einsum(
            "htu,thd->uhd", probs.astype(bf16), grad_blk, preferred_element_type=f32
        )
        grad_prob = jnp.einsum("thd,uhd->htu", grad_blk, value_low, preferred_element_type=f32)
        grad_scores = (
            probs * (grad_prob - jnp.sum(probs * grad_prob, axis=-1, keepdims=True))
        ).astype(bf16)
        grad_query = jnp.einsum("htu,uhd->thd", grad_scores, key_low, preferred_element_type=f32)
        grad_key = grad_key + jnp.einsum(
            "htu,thd->uhd", grad_scores, query_blk, preferred_element_type=f32
        )
        return ((grad_key, grad_value), grad_query)

    zeros = jnp.zeros((length, heads_local, HD), f32)
    (grad_key, grad_value), grad_query = lax.scan(
        back_block, (zeros, zeros), (query_blocks, grad_att, log_total, seg_blocks, id_blocks)
    )
    grad_query = grad_query.reshape(length, heads_local, HD)
    grad_q_raw, qgain_part = norm_back(grad_query * 0.125, query_s, query_i, qgain_f[0])
    grad_k_raw, kgain_part = norm_back(grad_key, key_s, key_i, qgain_f[1])
    grad_mixed = (
        jnp.stack([grad_q_raw, grad_k_raw, grad_value], axis=2)
        .reshape(length, heads_local * 3 * HD)
        .astype(bf16)
    )
    grad_in = jnp.dot(normed_a_low.T, grad_mixed, preferred_element_type=f32)
    qgain_local = jnp.stack([jnp.sum(qgain_part, axis=(0, 1)), jnp.sum(kgain_part, axis=(0, 1))])
    grad_normed_a, grad_qgains, grad_gain_b = (
        lax.psum(
            jnp.dot(grad_mixed, in_proj.T, preferred_element_type=f32).astype(jnp.bfloat16), "mp"
        ).astype(jnp.float32),
        lax.psum(qgain_local.astype(jnp.bfloat16), "mp").astype(jnp.float32),
        lax.psum(gain_b_term.astype(jnp.bfloat16), "mp").astype(jnp.float32),
    )
    grad_in_a, gain_part_a = norm_back(grad_normed_a, scaled_a, inv_a, gain_f[0])
    grad_embed = (grad_mid + grad_in_a).astype(bf16)
    grad_patch = jnp.dot(patches.T, grad_embed, preferred_element_type=f32)
    grad_pos = jnp.concatenate(
        [
            jnp.dot(onehot_y.T, grad_embed, preferred_element_type=f32),
            jnp.dot(onehot_x.T, grad_embed, preferred_element_type=f32),
        ],
        axis=0,
    )
    grad_gains = jnp.stack(
        [jnp.sum(gain_part_a, axis=0), grad_gain_b, jnp.sum(gain_part_f, axis=0), grad_probe]
    )
    shares = (
        lax.psum_scatter(
            grad_in.astype(jnp.bfloat16), "dp", scatter_dimension=0, tiled=True
        ).astype(jnp.float32),
        lax.psum_scatter(
            grad_out_proj.astype(jnp.bfloat16), "dp", scatter_dimension=1, tiled=True
        ).astype(jnp.float32),
        lax.psum_scatter(
            grad_up.astype(jnp.bfloat16), "dp", scatter_dimension=0, tiled=True
        ).astype(jnp.float32),
        lax.psum_scatter(
            grad_down.astype(jnp.bfloat16), "dp", scatter_dimension=1, tiled=True
        ).astype(jnp.float32),
        lax.psum_scatter(
            grad_patch.astype(jnp.bfloat16), "dp", scatter_dimension=0, tiled=True
        ).astype(jnp.float32),
        lax.psum_scatter(
            grad_pos.astype(jnp.bfloat16), "dp", scatter_dimension=1, tiled=True
        ).astype(jnp.float32),
        lax.psum_scatter(
            grad_head.astype(jnp.bfloat16), "dp", scatter_dimension=0, tiled=True
        ).astype(jnp.float32),
        lax.psum_scatter(
            grad_gains.astype(jnp.bfloat16), "dp", scatter_dimension=1, tiled=True
        ).astype(jnp.float32),
        lax.psum_scatter(
            grad_qgains.astype(jnp.bfloat16), "dp", scatter_dimension=1, tiled=True
        ).astype(jnp.float32),
    )
    layer_squares = sum((jnp.sum(share * share) for share in shares[:4]))
    other_squares = sum((jnp.sum(share * share) for share in shares[4:]))
    squares = lax.psum(layer_squares + only_first * other_squares, ("dp", "mp"))
    grad_norm = jnp.sqrt(squares)
    factor = jnp.minimum(1.0, CLIP / (grad_norm + 1e-06))
    results = [bucket_loss, bucket_count, grad_norm]
    for index in range(9):
        clipped = shares[index] * factor
        first_new = BETA_ONE * firsts[index] + (1.0 - BETA_ONE) * clipped
        second_new = BETA_TWO * seconds[index] + (1.0 - BETA_TWO) * clipped * clipped
        matrix = index in (0, 1, 2, 3, 4, 6)
        rate = RATE_MATRIX if matrix else RATE_SMALL
        decay = DECAY if matrix else 0.0
        ratio = (
            first_new
            / (1.0 - BETA_ONE**STEP)
            / (jnp.sqrt(second_new / (1.0 - BETA_TWO**STEP)) + ADAM_EPS)
        )
        results += [masters[index] - rate * (ratio + decay * masters[index]), first_new, second_new]
    return tuple(results)


def solution(mesh):
    in_specs = (
        P("dp", None),
        P("dp"),
        P("dp"),
        P("dp"),
        P("dp"),
        P("dp"),
        P("dp"),
        P("dp", "mp"),
        P("dp", "mp"),
        P("dp", "mp"),
        P("mp", "dp"),
        P("mp", "dp"),
        P("mp", "dp"),
        P("dp", "mp"),
        P("dp", "mp"),
        P("dp", "mp"),
        P("mp", "dp"),
        P("mp", "dp"),
        P("mp", "dp"),
        P("dp", None),
        P("dp", None),
        P("dp", None),
        P(None, "dp"),
        P(None, "dp"),
        P(None, "dp"),
        P("dp", None),
        P("dp", None),
        P("dp", None),
        P(None, "dp"),
        P(None, "dp"),
        P(None, "dp"),
        P(None, "dp"),
        P(None, "dp"),
        P(None, "dp"),
    )
    out_specs = (
        P(),
        P(),
        P(),
        P("dp", "mp"),
        P("dp", "mp"),
        P("dp", "mp"),
        P("mp", "dp"),
        P("mp", "dp"),
        P("mp", "dp"),
        P("dp", "mp"),
        P("dp", "mp"),
        P("dp", "mp"),
        P("mp", "dp"),
        P("mp", "dp"),
        P("mp", "dp"),
        P("dp", None),
        P("dp", None),
        P("dp", None),
        P(None, "dp"),
        P(None, "dp"),
        P(None, "dp"),
        P("dp", None),
        P("dp", None),
        P("dp", None),
        P(None, "dp"),
        P(None, "dp"),
        P(None, "dp"),
        P(None, "dp"),
        P(None, "dp"),
        P(None, "dp"),
    )
    return jax.shard_map(local, mesh=mesh, in_specs=in_specs, out_specs=out_specs, check_vma=False)
```

profile of v0, /device:TPU:0, one launch (start us, length us, event | category | flops | bytes accessed | tf_op | source)
XLA Modules:
  0.0 1410.9 jit_solution(2651911913564201122)
XLA Ops:
  9.8 10.2 all-gather.2
  22.1 8.9 all-gather.1
  32.8 8.3 all-gather
  42.2 10.5 all_gather.32
  54.0 12.2 all_gather.30
  97.4 101.2 %while.28 = (s32[]{:T(128)}, bf16[4,512,3,64]{1,3,2,0:T(8,128)(2,1)}, f32[4,3,512]{2,1,0:T(4,128)}, s32[4,512]{1,0:T(4,128)}, s32[2048]{0:T(1024)S(1)}, /*index=...) while((s32[]{:T(128)}, ...), condition=%wide.region_10.11_spmd.clone, body=%wide.region_7.0_spmd.clone.sunk | while | flops 837810688 | bytes 53620952 | solution.py:184
  99.6 8.0 select_reduce_fusion.5
  107.6 7.9 fusion.232
  124.8 8.0 select_reduce_fusion.5
  132.8 7.9 fusion.232
  150.1 8.0 select_reduce_fusion.5
  158.0 7.9 fusion.232
  175.3 8.0 select_reduce_fusion.5
  183.3 7.9 fusion.232
  207.7 117.8 %all-reduce.8.cloned.1.call-done = bf16[2048,768]{0,1:T(8,128)(2,1)} async-done(((bf16[2048,768]{0,1:T(8,128)(2,1)}), bf16[2048,768]{0,1:T(8,128)(2,1)}) %all-reduce.8.cloned.1.call-update) | async-done | bytes 3145744 | tf_op jit(solution)/shard_map/psum | solution.py:187
  334.3 16.8 %all-gather.10.cloned.1.call-done = bf16[768,768]{1,0:T(8,128)(2,1)} async-done(((bf16[96,768]{1,0:T(8,128)(2,1)}), bf16[768,768]{1,0:T(8,128)(2,1)}) %all-gather.10.cloned.1.call-update) | async-done | bytes 1179664 | tf_op jit(solution)/shard_map/all_gather | solution.py:133
  351.1 8.6 fusion.148
  359.8 17.8 %all-gather.12.cloned.1.call-done = bf16[768,768]{0,1:T(8,128)(2,1)} async-done(((bf16[768,96]{0,1:T(8,128)(2,1)}), bf16[768,768]{0,1:T(8,128)(2,1)}) %all-gather.12.cloned.1.call-update) | async-done | bytes 1179664 | tf_op jit(solution)/shard_map/all_gather | solution.py:134
  377.5 7.5 convolution_convert_fusion.2
  391.0 115.2 %all-reduce.10.cloned.1.call-done = bf16[2048,768]{0,1:T(8,128)(2,1)} async-done(((bf16[2048,768]{0,1:T(8,128)(2,1)}), bf16[2048,768]{0,1:T(8,128)(2,1)}) %all-reduce.10.cloned.1.call-update) | async-done | bytes 3145744 | tf_op jit(solution)/shard_map/psum | solution.py:193
  540.8 13.9 all-reduce.1
  581.4 6.9 fusion.67
  595.3 120.0 %all-reduce.12.cloned.1.call-done = bf16[2048,768]{0,1:T(8,128)(2,1)} async-done(((bf16[2048,768]{0,1:T(8,128)(2,1)}), bf16[2048,768]{0,1:T(8,128)(2,1)}) %all-reduce.12.cloned.1.call-update) | async-done | bytes 3145744 | tf_op jit(solution)/shard_map/psum | solution.py:237
  738.2 156.0 %while.29 = (s32[]{:T(128)}, f32[2048,3,64]{0,2,1:T(8,128)}, f32[2048,3,64]{0,2,1:T(8,128)}, f32[4,512,3,64]{1,0,3,2:T(4,128)}, bf16[4,512,3,64]{1,3,2,0:T(8,128...) while((s32[]{:T(128)}, f32[2048,3,64]{0,2,1:T(8,128)}, ...), condition=%wide.region_36.37_spmd.clone, body=%wide.region_34.36_spmd.clone.sunk | while | flops 2056780288 | bytes 132059472 | solution.py:269
  748.2 6.8 multiply_reduce_fusion.16
  767.8 8.6 dynamic_update_slice.21
  787.5 6.8 multiply_reduce_fusion.16
  807.0 8.6 dynamic_update_slice.21
  826.7 6.8 multiply_reduce_fusion.16
  846.3 8.6 dynamic_update_slice.21
  866.0 6.8 multiply_reduce_fusion.16
  885.6 8.6 dynamic_update_slice.21
  910.7 7.5 convolution_convert_fusion.6
  918.4 7.4 convolution_convert_fusion.8
  937.7 14.4 %all-reduce = bf16[2,64]{1,0:T(2,128)(2,1)S(1)} all-reduce(bf16[2,64]{1,0:T(2,128)(2,1)S(1)} %pad_maximum_fusion.3), channel_id=10, replica_groups=mesh['dp'=8,'mp'=4] {'dp'}, use_global_device_ids=true, to_apply=%region_68.69.clone | all-reduce | flops 128 | bytes 512
  952.2 10.7 all-reduce.2
  962.9 7.1 convolution_convert_fusion.9
  970.1 61.0 %all-reduce.14.cloned.1.call-done = bf16[2048,768]{0,1:T(8,128)(2,1)} async-done(((bf16[2048,768]{0,1:T(8,128)(2,1)}), bf16[2048,768]{0,1:T(8,128)(2,1)}) %all-reduce.14.cloned.1.call-update) | async-done | bytes 3145744 | tf_op jit(solution)/shard_map/psum | solution.py:283
  1037.1 7.2 fusion.58
  1054.3 15.8 %reduce-scatter.20.cloned.1.call-done = bf16[768,96]{0,1:T(8,128)(2,1)} async-done(((bf16[768,768]{0,1:T(8,128)(2,1)}), bf16[768,96]{0,1:T(8,128)(2,1)}) %reduce-scatter.20.cloned.1.call-update) | async-done | bytes 147472 | tf_op jit(solution)/shard_map/reduce_scatter | solution.py:312
  1071.7 38.6 %reduce-scatter.18.cloned.1.call-done = bf16[96,768]{1,0:T(8,128)(2,1)} async-done(((bf16[768,768]{1,0:T(8,128)(2,1)}), bf16[96,768]{1,0:T(8,128)(2,1)}) %reduce-scatter.18.cloned.1.call-update) | async-done | bytes 147472 | tf_op jit(solution)/shard_map/reduce_scatter | solution.py:309
  1112.0 40.2 %reduce-scatter.24.cloned.1.call-done = bf16[96,1000]{1,0:T(8,128)(2,1)} async-done(((bf16[768,1000]{1,0:T(8,128)(2,1)}), bf16[96,1000]{1,0:T(8,128)(2,1)}) %reduce-scatter.24.cloned.1.call-update) | async-done | bytes 192016 | tf_op jit(solution)/shard_map/reduce_scatter | solution.py:321
  1154.4 35.1 %reduce-scatter.26.cloned.1.call-done = bf16[96,192]{1,0:T(8,128)(2,1)} async-done(((bf16[768,192]{1,0:T(8,128)(2,1)}), bf16[96,192]{1,0:T(8,128)(2,1)}) %reduce-scatter.26.cloned.1.call-update) | async-done | bytes 36880
  1192.4 36.0 %reduce-scatter.16.cloned.1.call-done = bf16[96,576]{1,0:T(8,128)(2,1)} async-done(((bf16[768,576]{1,0:T(8,128)(2,1)}), bf16[96,576]{1,0:T(8,128)(2,1)}) %reduce-scatter.16.cloned.1.call-update) | async-done | bytes 110608 | tf_op jit(solution)/shard_map/reduce_scatter | solution.py:303
  1232.6 33.1 %reduce-scatter.30.cloned.1.call-done = bf16[96,4]{1,0:T(8,128)(2,1)} async-done(((bf16[768,4]{1,0:T(8,128)(2,1)}), bf16[96,4]{1,0:T(8,128)(2,1)}) %reduce-scatter.30.cloned.1.call-update) | async-done | bytes 784
  1267.1 35.5 %reduce-scatter.28.cloned.1.call-done = bf16[96,64]{1,0:T(8,128)(2,1)} async-done(((bf16[768,64]{1,0:T(8,128)(2,1)}), bf16[96,64]{1,0:T(8,128)(2,1)}) %reduce-scatter.28.cloned.1.call-update) | async-done | bytes 12304
  1304.1 38.8 %reduce-scatter.22.cloned.1.call-done = bf16[96,768]{1,0:T(8,128)(2,1)} async-done(((bf16[768,768]{1,0:T(8,128)(2,1)}), bf16[96,768]{1,0:T(8,128)(2,1)}) %reduce-scatter.22.cloned.1.call-update) | async-done | bytes 147472 | tf_op jit(solution)/shard_map/reduce_scatter | solution.py:315
  1347.8 39.3 %psum.71 = f32[]{:T(128)} all-reduce(f32[]{:T(128)S(6)} %add.331), channel_id=1, replica_groups=mesh['dp'=8,'mp'=4] {'dp','mp'}, use_global_device_ids=true, to_apply=%region_70.71 | all-reduce | flops 1 | bytes 8 | tf_op jit(solution)/shard_map/psum | solution.py:333
  (522 shorter events, 356.7 us)
Async XLA Ops:
  7.2 63.7 %copy-start = (bf16[2048,768]{1,0:T(8,128)(2,1)S(1)}, bf16[2048,768]{1,0:T(8,128)(2,1)}, u32[]{:S(2)}) copy-start(bf16[2048,768]{1,0:T(8,128)(2,1)} %param.38) | copy-start | bytes 9437188
  7.2 63.7 %all-gather.8.cloned.1.call-start = ((), (), s32[]{:S(2)}) async-start(), calls=%async_computation.8 | async-start | bytes 1327104 | tf_op jit(solution)/shard_map/all_gather | solution.py:135
  9.1 316.5 %all-reduce.8.cloned.1.call-start = ((), (), s32[]{:S(2)}) async-start(), calls=%async_computation.9 | async-start | bytes 6291456 | tf_op jit(solution)/shard_map/psum | solution.py:187
  20.1 50.8 %copy-start.100 = (f32[64,2]{0,1:T(2,128)}, f32[64,2]{0,1:T(2,128)S(1)}, u32[]{:S(2)}) copy-start(f32[64,2]{0,1:T(2,128)S(1)} %reshape.521) | copy-start | bytes 1540
  54.0 23.2 %copy-start.85 = (f32[768]{0:T(1024)}, f32[768]{0:T(1024)S(1)}, u32[]{:S(2)}) copy-start(f32[768]{0:T(1024)S(1)} %get-tuple-element.334) | copy-start | bytes 9220
  66.2 21.7 %copy-start.94 = (f32[64]{0:T(128)}, f32[64]{0:T(128)S(1)}, u32[]{:S(2)}) copy-start(f32[64]{0:T(128)S(1)} %get-tuple-element.428) | copy-start | bytes 772
  84.5 11.8 copy-start.47
  84.6 11.7 copy-start.57
  86.2 11.2 copy-start.31
  97.3 104.0 %copy-start.27 = (bf16[192,768]{0,1:T(8,128)(2,1)S(1)}, bf16[192,768]{0,1:T(8,128)(2,1)}, u32[]{:S(2)}) copy-start(bf16[192,768]{0,1:T(8,128)(2,1)} %all_gather.32) | copy-start | bytes 884740
  198.5 188.7 %copy-start.51 = (pred[2048]{0:T(1024)(128)(4,1)}, pred[2048]{0:T(1024)(128)(4,1)S(1)}, u32[]{:S(2)}) copy-start(pred[2048]{0:T(1024)(128)(4,1)S(1)} %get-tuple-element.737) | copy-start | bytes 6148
  204.0 147.1 %all-gather.10.cloned.1.call-start = ((), (), s32[]{:S(2)}) async-start(), calls=%async_computation.10 | async-start | bytes 1327104 | tf_op jit(solution)/shard_map/all_gather | solution.py:133
  205.8 171.8 %all-gather.12.cloned.1.call-start = ((), (), s32[]{:S(2)}) async-start(), calls=%async_computation.11 | async-start | bytes 1327104 | tf_op jit(solution)/shard_map/all_gather | solution.py:134
  207.5 298.8 %all-reduce.10.cloned.1.call-start = ((), (), s32[]{:S(2)}) async-start(), calls=%async_computation.12 | async-start | bytes 6291456 | tf_op jit(solution)/shard_map/psum | solution.py:193
  330.4 20.7 %copy-start.82 = (f32[768]{0:T(1024)S(1)}, f32[768]{0:T(1024)}, u32[]{:S(2)}) copy-start(f32[768]{0:T(1024)} %get-tuple-element.333) | copy-start | bytes 9220
  359.8 29.4 %copy-start.93 = (f32[768]{0:T(1024)S(1)}, f32[768]{0:T(1024)}, u32[]{:S(2)}) copy-start(f32[768]{0:T(1024)} %get-tuple-element.331) | copy-start | bytes 9220
  385.0 148.3 %all-gather.14.cloned.1.call-start = ((), (), s32[]{:S(2)}) async-start(), calls=%async_computation.13 | async-start | bytes 1769472 | tf_op jit(solution)/shard_map/all_gather | solution.py:137
  386.8 328.5 %all-reduce.12.cloned.1.call-start = ((), (), s32[]{:S(2)}) async-start(), calls=%async_computation.14 | async-start | bytes 6291456 | tf_op jit(solution)/shard_map/psum | solution.py:237
  506.2 8.9 slice-start
  563.2 12.2 slice-start.2
  581.3 8.7 copy-start.106
  594.0 437.0 %all-reduce.14.cloned.1.call-start = ((), (), s32[]{:S(2)}) async-start(), calls=%async_computation.18 | async-start | bytes 6291456 | tf_op jit(solution)/shard_map/psum | solution.py:283
  738.2 159.3 %copy-start.103 = (f32[64]{0:T(128)S(1)}, f32[64]{0:T(128)}, u32[]{:S(2)}) copy-start(f32[64]{0:T(128)} %broadcast_multiply_fusion.14) | copy-start | bytes 772
  894.2 8.6 copy-start.95
  910.6 159.5 %reduce-scatter.20.cloned.1.call-start = ((), (), s32[]{:S(2)}) async-start(), calls=%async_computation.17 | async-start | bytes 1327104 | tf_op jit(solution)/shard_map/reduce_scatter | solution.py:312
  918.3 9.8 copy-start.108
  918.3 11.0 copy-start.46
  918.3 192.1 %reduce-scatter.18.cloned.1.call-start = ((), (), s32[]{:S(2)}) async-start(), calls=%async_computation.16 | async-start | bytes 1327104 | tf_op jit(solution)/shard_map/reduce_scatter | solution.py:309
  925.8 226.3 %reduce-scatter.24.cloned.1.call-start = ((), (), s32[]{:S(2)}) async-start(), calls=%async_computation.20 | async-start | bytes 1769472 | tf_op jit(solution)/shard_map/reduce_scatter | solution.py:321
  927.8 261.7 %reduce-scatter.26.cloned.1.call-start = ((), (), s32[]{:S(2)}) async-start(), calls=%async_computation.21 | async-start | bytes 442368
  929.3 33.6 %copy-start.67 = (f32[2048]{0:T(1024)S(1)}, f32[2048]{0:T(1024)}, u32[]{:S(2)}) copy-start(f32[2048]{0:T(1024)} %copy-done.66) | copy-start | bytes 24580
  929.3 33.6 %copy-start.73 = (f32[2048]{0:T(1024)S(1)}, f32[2048]{0:T(1024)}, u32[]{:S(2)}) copy-start(f32[2048]{0:T(1024)} %copy-done.72) | copy-start | bytes 24580
  929.3 33.6 %copy-start.86 = (f32[768]{0:T(1024)S(1)}, f32[768]{0:T(1024)}, u32[]{:S(2)}) copy-start(f32[768]{0:T(1024)} %copy-done.85) | copy-start | bytes 9220
  952.1 276.4 %reduce-scatter.16.cloned.1.call-start = ((), (), s32[]{:S(2)}) async-start(), calls=%async_computation.15 | async-start | bytes 1105920 | tf_op jit(solution)/shard_map/reduce_scatter | solution.py:303
  962.9 190.9 %copy-start.104 = (bf16[2,8]{1,0:T(2,128)(2,1)}, bf16[2,8]{1,0:T(2,128)(2,1)S(1)}, u32[]{:S(2)}) copy-start(bf16[2,8]{1,0:T(2,128)(2,1)S(1)} %get-tuple-element.386) | copy-start | bytes 100
  970.1 295.6 %reduce-scatter.30.cloned.1.call-start = ((), (), s32[]{:S(2)}) async-start(), calls=%async_computation.23 | async-start | bytes 221184
  1037.1 8.9 copy-start.68
  1047.5 255.2 %reduce-scatter.28.cloned.1.call-start = ((), (), s32[]{:S(2)}) async-start(), calls=%async_computation.22 | async-start | bytes 221184
  1048.4 294.5 %reduce-scatter.22.cloned.1.call-start = ((), (), s32[]{:S(2)}) async-start(), calls=%async_computation.19 | async-start | bytes 1327104 | tf_op jit(solution)/shard_map/reduce_scatter | solution.py:315
  1054.3 347.5 %copy-start.30 = (f32[96,1000]{1,0:T(8,128)S(1)}, f32[96,1000]{1,0:T(8,128)}, u32[]{:S(2)}) copy-start(f32[96,1000]{1,0:T(8,128)} %param.63) | copy-start | bytes 1152004
  1266.5 36.2 %copy-start.99 = (bf16[4,96]{1,0:T(4,128)(2,1)}, bf16[4,96]{1,0:T(4,128)(2,1)S(1)}, u32[]{:S(2)}) copy-start(bf16[4,96]{1,0:T(4,128)(2,1)S(1)} %copy.155) | copy-start | bytes 2308
  1387.9 12.8 copy-start.32
  1387.9 12.8 copy-start.41
  1387.9 12.8 copy-start.55
  1387.9 12.8 copy-start.56
  1387.9 13.8 copy-start.40
  1387.9 13.8 copy-start.49
  1387.9 13.8 copy-start.50
  (108 other events, 527.9 us)
Sparse Core Ops, SparseCore 0:
  10.5 26.7 all-gather.7
  204.2 121.3 all-reduce.7
  328.0 23.0 all-gather.9
  353.4 24.0 all-gather.11
  385.1 121.0 all-reduce.9
  508.6 24.6 all-gather.13
  594.2 121.0 all-reduce.11
  910.7 120.3 all-reduce.13
  1034.3 35.7 reduce-scatter.19
  1073.6 36.7 reduce-scatter.17
  1113.7 38.4 reduce-scatter.23
  1155.6 33.7 reduce-scatter.25
  1192.7 35.7 reduce-scatter.15
  1232.2 33.4 reduce-scatter.29
  1269.2 33.4 reduce-scatter.27
  1306.1 36.7 reduce-scatter.21
where the time goes:
time: 1420 us; the launch traced here: 1410 us
  waiting for transfers between devices  728 us (51%)
  matrix products  241 us (17%)
  other arithmetic  188 us (13%)
  blocking collectives  128 us (9%)
  local copies, waits for them, and re-layouts  96.2 us (7%)
  between operations  25.6 us (2%)
    psum x1, waiting for transfers between devices, local(): lax.psum(back_term.astype(jnp.bfloat16), 'mp').astype(jnp.float32)  120 us
    psum x1, waiting for transfers between devices, local(): lax.psum(attn_term.astype(jnp.bfloat16), 'mp').astype(jnp.float32)  118 us
    psum x1, waiting for transfers between devices, local(): lax.psum(mlp_term.astype(jnp.bfloat16), 'mp').astype(jnp.float32)  115 us
    unnamed x19, waiting for transfers between devices  104 us
    psum x1, waiting for transfers between devices, local(): lax.psum(jnp.dot(grad_mixed, in_proj.T, preferred_element_type=f32).astyp...  61 us
    reduce_scatter x1, waiting for transfers between devices, local(): lax.psum_scatter(grad_head.astype(jnp.bfloat16), 'dp', scatter_dimension=...  40.2 us
    psum x1, blocking collectives, local(): squares = lax.psum(layer_squares + only_first * other_squares, ('dp', 'mp'))  39.3 us
    reduce_scatter x1, waiting for transfers between devices, local(): lax.psum_scatter(grad_patch.astype(jnp.bfloat16), 'dp', scatter_dimension...  38.8 us
  transfers between devices with their start and end apart: 16, of which 15 were waited for; matrix products, arithmetic and copies ran while one was open for 9% of the time, Pallas kernels for 0%

commit v1 on v0

v1 whole, which is shorter than its diff:
```python
import jax
import jax.numpy as jnp
from jax import lax
from jax.experimental import pallas as pl
from jax.experimental.pallas import tpu as pltpu
from jax.sharding import PartitionSpec as P

D = 768
HD = 64
HID = 3072
CLASSES = 1000
CPAD = 1024
GRID = 32
IMG = 16
NB = 4
STEP = 10
BQ = 256
TOK = 512
NH = 3

HIGH = lax.Precision.HIGHEST
NORM_EPS = 1e-06
CLIP = 0.1
BETA_ONE = 0.9
BETA_TWO = 0.95
RATE_MATRIX = 0.05
RATE_SMALL = 0.2
DECAY = 0.05
ADAM_EPS = 1e-08
BIG = 128.0

bf16 = jnp.bfloat16
f32 = jnp.float32
VLIM = 56 * 1024 * 1024

NN = (((1,), (0,)), ((), ()))
NT = (((1,), (1,)), ((), ()))
TN = (((0,), (0,)), ((), ()))


def dot(a, b, dims=NN, precision=None):
    return lax.dot_general(a, b, dims, precision=precision, preferred_element_type=f32)


def norm_stats(values):
    center = values - jnp.mean(values, axis=-1, keepdims=True)
    inv_std = lax.rsqrt(jnp.mean(center * center, axis=-1, keepdims=True) + NORM_EPS)
    return center * inv_std, inv_std


def norm_back(grad_scaled, scaled, inv_std):
    return inv_std * (
        grad_scaled
        - jnp.mean(grad_scaled, axis=-1, keepdims=True)
        - scaled * jnp.mean(grad_scaled * scaled, axis=-1, keepdims=True)
    )


def split3(x):
    hi = x.astype(bf16).astype(f32)
    rest = x - hi
    mid = rest.astype(bf16).astype(f32)
    return hi, mid, rest - mid


def rows_at(index, size):
    return pl.ds(pl.multiple_of(index * size, size), size)


def load_rows(pieces, me, dst, sems):
    size = pieces[0].shape[0]
    copies = [
        pltpu.make_async_copy(piece, dst.at[rows_at(me ^ r, size), :], sems.at[r])
        for r, piece in enumerate(pieces)
    ]
    for copy in copies:
        copy.start()
    for copy in copies:
        copy.wait()


def x0_kernel(sc, own, other, hot, pos, gains, *rest):
    pieces = rest[:8]
    a_out, x0_out, w, sems = rest[8:]
    i = pl.program_id(0)

    @pl.when(i == 0)
    def _():
        load_rows(pieces, sc[0], w, sems)

    rows = jnp.where(sc[3] == 1, own[...], other[...])
    x0 = dot(rows, w[:, :D]) + dot(hot[...], pos[...])
    scaled, _ = norm_stats(x0)
    a_out[...] = (scaled * gains[0:1, :]).astype(bf16)

    @pl.when(i == sc[1])
    def _():
        x0_out[...] = x0


def qkv_kernel(sc, a, qaux, kaux, vaux, qg, *rest):
    pieces = rest[:4]
    qx, kx, vx, raw, w, sems = rest[4:]
    i = pl.program_id(0)

    @pl.when(i == 0)
    def _():
        load_rows(pieces, sc[4], w, sems)

    mixed = dot(a[...], w[...])
    qa, ka, va = qaux[...], kaux[...], vaux[...]
    for h in range(NH):
        q = mixed[:, h * 192 : h * 192 + 64]
        k = mixed[:, h * 192 + 64 : h * 192 + 128]
        v = mixed[:, h * 192 + 128 : h * 192 + 192]
        raw[2 * h] = q
        raw[2 * h + 1] = k
        qn = (norm_stats(q)[0] * qg[0:1, :] * 0.125).astype(bf16)
        kn = (norm_stats(k)[0] * qg[1:2, :]).astype(bf16)
        qx[h] = jnp.concatenate([qn, qa], axis=1)
        kx[h] = jnp.concatenate([kn, ka], axis=1)
        vx[h] = jnp.concatenate([v.astype(bf16), va], axis=1)


def attn_kernel(sc, qx, kx, vx, o_rel, o_full, ql, acc):
    i = pl.program_id(0)
    acc[...] = jnp.zeros_like(acc)

    def step(j, carry):
        ks = rows_at(j, BQ)
        for h in range(NH):
            s = dot(qx[h], kx[h, ks, :], NT)
            p = jnp.exp(s).astype(bf16)
            acc[h] += dot(p, vx[h, ks, :])
        return carry

    lax.fori_loop(sc[8 + i], sc[16 + i], step, 0)
    mine = rows_at(i, BQ)
    lane = lax.broadcasted_iota(jnp.int32, (BQ, 128), 1)
    outs = []
    for h in range(NH):
        q = qx[h].astype(f32)
        k = kx[h, mine, :].astype(f32)
        v = vx[h, mine, :].astype(f32)
        free = k[:, 84:85]
        diag = jnp.sum(jnp.where(lane < HD, q * k, 0.0), axis=1, keepdims=True)
        p = jnp.exp(diag) * free
        out = acc[h] + p.astype(bf16).astype(f32) * v
        total = out[:, 64:65]
        outs.append(out[:, :HD] / total)
        parts = split3(-jnp.log(total))
        for n, part in enumerate(parts):
            q = jnp.where(lane == 81 + n, part, q)
        ql[h] = q.astype(bf16)
    full = jnp.concatenate(outs, axis=1)
    o_full[...] = full
    o_rel[0] = full.astype(bf16)


def mid_kernel(sc, o, x0, gains, *rest):
    pieces = rest[:8]
    x1_out, b_out, w, sems = rest[8:]
    load_rows(pieces, sc[0], w, sems)
    x1 = x0[...] + dot(o[...], w[...], NT)
    x1_out[...] = x1
    b_out[...] = (norm_stats(x1)[0] * gains[1:2, :]).astype(bf16)


def tile_copies(pieces, me, z, j, dst, sems):
    size = pieces[0].shape[1]
    return [
        pltpu.make_async_copy(
            piece.at[z ^ j], dst.at[j, rows_at(me ^ r, size), :], sems.at[j, r]
        )
        for r, piece in enumerate(pieces)
    ]


def start_tiles(pieces, me, z, dst, sems):
    for j in range(4):
        for copy in tile_copies(pieces, me, z, j, dst, sems):
            copy.start()


def wait_tile(pieces, me, z, j, dst, sems):
    for copy in tile_copies(pieces, me, z, j, dst, sems):
        copy.wait()


GELU_C = 0.7978845608028654


def gelu_tanh(u):
    return jnp.tanh(GELU_C * (u + 0.044715 * u * u * u))


def up_kernel(sc, b, *rest):
    pieces = rest[:8]
    u_out, h_out, w, sems = rest[8:]
    j = pl.program_id(0)

    @pl.when(j == 0)
    def _():
        start_tiles(pieces, sc[0], sc[2], w, sems)

    wait_tile(pieces, sc[0], sc[2], j, w, sems)
    u = dot(b[...], w[j])
    u_out[...] = u
    h_out[...] = (0.5 * u * (1.0 + gelu_tanh(u))).astype(bf16)


def head_ones():
    row = lax.broadcasted_iota(jnp.int32, (D, 128), 0) // HD
    col = lax.broadcasted_iota(jnp.int32, (D, 128), 1)
    return (row == col).astype(f32)


def down_kernel(sc, h, x1, gains, mem, *rest):
    pieces = rest[:8]
    x2_out, ns_out, w, acc, sems = rest[8:]
    j = pl.program_id(0)

    @pl.when(j == 0)
    def _():
        start_tiles(pieces, sc[0], sc[2], w, sems)
        acc[...] = x1[...]

    wait_tile(pieces, sc[0], sc[2], j, w, sems)
    acc[...] += dot(h[...], w[j], NT)

    @pl.when(j == 3)
    def _():
        x2 = acc[...]
        x2_out[...] = x2
        f = norm_stats(x2)[0] * gains[2:3, :]
        ones = head_ones()
        e = jnp.exp(dot(f * gains[3:4, :], ones, NN, HIGH) * 0.125)
        eb = dot(e, ones, NT, HIGH)
        m = mem[...]
        ns_out[:, :D] = dot(m, eb * f, TN, HIGH)
        ns_out[:, D:] = dot(m, e, TN, HIGH)


def head_kernel(sc, ns, lab, vt, *rest):
    pieces = rest[:8]
    pooled_out, gp_out, sinv_out, loss_out, gh_out, gh_send, w, gw, sems = rest[8:]
    load_rows(pieces, sc[0], w, sems)
    valid = vt[:, 0:1]
    scale = vt[:, 1:2]
    total = jnp.where(valid > 0.0, ns[:, D:], 1.0)
    sinv = jnp.where(valid > 0.0, 1.0 / total, 0.0)
    lane = lax.broadcasted_iota(jnp.int32, (IMG, 128), 1)
    sinv = jnp.where(lane < D // HD, sinv, 0.0)
    pooled = ns[:, :D] * dot(sinv, head_ones(), NT, HIGH)
    low = pooled.astype(bf16)
    logits = dot(low, w[...])
    cls = lax.broadcasted_iota(jnp.int32, (IMG, CPAD), 1)
    real = (cls < CLASSES).astype(f32)
    hot = lab[...]
    ex = jnp.exp(-jnp.abs(logits))
    soft = jnp.maximum(logits, 0.0) + jnp.log1p(ex)
    per = jnp.sum(soft * real, axis=1, keepdims=True) - jnp.sum(
        logits * hot, axis=1, keepdims=True
    )
    loss_out[...] = jnp.broadcast_to(per * valid, (IMG, 128))
    sig = jnp.where(logits >= 0.0, 1.0, ex) / (1.0 + ex)
    gl = (scale * (sig * real - hot)).astype(bf16)
    pooled_out[...] = pooled
    sinv_out[...] = sinv
    gp_out[...] = dot(gl, w[...], NT)
    half = jnp.where(sc[2] % 2 == 1, gl[:, 512:].astype(f32), gl[:, :512].astype(f32))
    gw[...] = dot(low, half.astype(bf16), TN)
    size = D // 8
    for p in range(4):
        r = (p >> 1) * 2 + (p & 1) * 4
        gh_out[p] = gw[rows_at(sc[0] ^ r, size), :].astype(bf16)
        gh_send[p] = gw[rows_at(sc[0] ^ (r + 1), size), :].astype(bf16)


def back_kernel(sc, u, x2, x1, gains, mem, pooled, gp, sinv, *rest):
    ex_p, con_p, out_p = rest[:8], rest[8:16], rest[16:24]
    (gu_out, gr_out, gm_out, gmid_out, ga_out, small_out) = rest[24:30]
    wex, wcon, wout, grs, acc, sem_e, sem_c, sem_o = rest[30:]
    j = pl.program_id(0)
    size = D // 8

    @pl.when(j == 0)
    def _():
        start_tiles(con_p, sc[0], sc[2], wcon, sem_c)
        start_tiles(ex_p, sc[0], sc[2], wex, sem_e)
        for r, piece in enumerate(out_p):
            pltpu.make_async_copy(
                piece, wout.at[rows_at(sc[0] ^ r, size), :], sem_o.at[r]
            ).start()
        scaled, inv = norm_stats(x2[...])
        f = scaled * gains[2:3, :]
        probe = gains[3:4, :]
        ones = head_ones()
        e = jnp.exp(dot(f * probe, ones, NN, HIGH) * 0.125)
        m = mem[...]
        gt = dot(m, gp[...], NN, HIGH)
        at = e * dot(m, sinv[...], NN, HIGH)
        gpp = dot(gp[...] * pooled[...], ones, NN, HIGH)
        da = dot(gt * f, ones, NN, HIGH)
        dc = at * (da - dot(m, gpp, NN, HIGH))
        dcb = dot(dc, ones, NT, HIGH) * 0.125
        df = dot(at, ones, NT, HIGH) * gt + dcb * probe
        gr = norm_back(df * gains[2:3, :], scaled, inv)
        grs[...] = gr
        gr_out[...] = gr.astype(bf16)
        small_out[0:1, :] = jnp.sum(df * scaled, axis=0, keepdims=True)
        small_out[1:2, :] = jnp.sum(dcb * f, axis=0, keepdims=True)
        small_out[3:8, :] = jnp.zeros((5, D), f32)
        acc[...] = jnp.zeros_like(acc)

    wait_tile(con_p, sc[0], sc[2], j, wcon, sem_c)
    gh = dot(grs[...].astype(bf16), wcon[j])
    v = u[...]
    t = gelu_tanh(v)
    slope = 0.5 * (1.0 + t) + 0.5 * v * (1.0 - t * t) * GELU_C * (1.0 + 0.134145 * v * v)
    gu = (gh * slope).astype(bf16)
    gu_out[...] = gu
    wait_tile(ex_p, sc[0], sc[2], j, wex, sem_e)
    acc[...] += dot(gu, wex[j], NT)

    @pl.when(j == 3)
    def _():
        for r, piece in enumerate(out_p):
            pltpu.make_async_copy(
                piece, wout.at[rows_at(sc[0] ^ r, size), :], sem_o.at[r]
            ).wait()
        scaled, inv = norm_stats(x1[...])
        gb = acc[...]
        small_out[2:3, :] = jnp.sum(gb * scaled, axis=0, keepdims=True)
        gmid = grs[...] + norm_back(gb * gains[1:2, :], scaled, inv)
        gmid_out[...] = gmid
        low = gmid.astype(bf16)
        gm_out[...] = low
        ga_out[...] = dot(low, wout[...]).astype(bf16)


def rel_order(first):
    m1, m2 = (2, 4) if first == 2 else (4, 2)
    return [(p >> 1) * m1 + (p & 1) * m2 for p in range(4)]


def wgrad_kernel(sc, gr, h, b, gu, gm, o, ek, es, ck, cs, ok, os_, tile):
    j = pl.program_id(0)
    size = D // 8

    def emit(keep, send, first, lead):
        for p, r in enumerate(rel_order(first)):
            at = (p, 0) if lead else (p,)
            keep[at] = tile[rows_at(sc[0] ^ r, size), :].astype(bf16)
            send[at] = tile[rows_at(sc[0] ^ (r + 1), size), :].astype(bf16)

    tile[...] = dot(gr[...], h[...], TN)
    emit(ck, cs, 4, True)
    tile[...] = dot(b[...], gu[...], TN)
    emit(ek, es, 2, True)

    @pl.when(j == 3)
    def _():
        tile[...] = dot(gm[...], o[...], TN)
        emit(ok, os_, 2, False)


def attn_back_kernel(sc, ql, of, do, kx, vx, raw, a, qg, *rest):
    pieces = rest[:4]
    gna, gin_out, qg_out, dq, dk, dv, gin, w, sems = rest[4:]
    i = pl.program_id(0)
    nq = dk.shape[1] // BQ

    @pl.when(i == 0)
    def _():
        dk[...] = jnp.zeros_like(dk)
        dv[...] = jnp.zeros_like(dv)
        gin[...] = jnp.zeros_like(gin)
        qg_out[...] = jnp.zeros_like(qg_out)
        load_rows(pieces, sc[4], w, sems)

    @pl.when(i < nq)
    def _():
        mine = rows_at(i, BQ)
        lane = lax.broadcasted_iota(jnp.int32, (BQ, 128), 1)
        for h in range(NH):
            dof = do[0, :, h * HD : h * HD + HD].astype(f32)
            delta = jnp.sum(dof * of[:, h * HD : h * HD + HD], axis=1, keepdims=True)
            pad = jnp.zeros((BQ, HD), f32)
            dox = jnp.concatenate([dof, pad], axis=1)
            for n, part in enumerate(split3(-delta)):
                dox = jnp.where(lane == HD + n, part, dox)
            q = ql[h].astype(f32)
            k = kx[h, mine, :].astype(f32)
            v = vx[h, mine, :].astype(f32)
            free = k[:, 84:85]
            inner = (lane < HD) | ((lane >= 81) & (lane < 84))
            p = jnp.exp(jnp.sum(jnp.where(inner, q * k, 0.0), axis=1, keepdims=True)) * free
            ds = p * jnp.sum(jnp.where(lane < HD + 3, dox * v, 0.0), axis=1, keepdims=True)
            ds = ds.astype(bf16).astype(f32)
            dq[h, mine, :] = ds * k
            dk[h, mine, :] += ds * q
            dv[h, mine, :] += p.astype(bf16).astype(f32) * dox
            dob = dox.astype(bf16)
            qb = ql[h]

            def step(j, carry):
                ks = rows_at(j, BQ)
                kb = kx[h, ks, :]
                pt = jnp.exp(dot(kb, qb, NT))
                dpt = dot(vx[h, ks, :], dob, NT)
                dst = (pt * dpt).astype(bf16)
                dv[h, ks, :] += dot(pt.astype(bf16), dob)
                dk[h, ks, :] += dot(dst, qb)
                dq[h, mine, :] += dot(dst, kb, TN)
                return carry

            lax.fori_loop(sc[8 + i], sc[16 + i], step, 0)

    @pl.when(i >= nq)
    def _():
        rows = rows_at(i - nq, TOK)
        parts = []
        gq = jnp.zeros((1, HD), f32)
        gk = jnp.zeros((1, HD), f32)
        for h in range(NH):
            gradq = dq[h, rows, :][:, :HD] * 0.125
            gradk = dk[h, rows, :][:, :HD]
            qs, qi = norm_stats(raw[2 * h])
            ks, ki = norm_stats(raw[2 * h + 1])
            gq += jnp.sum(gradq * qs, axis=0, keepdims=True)
            gk += jnp.sum(gradk * ks, axis=0, keepdims=True)
            parts.append(norm_back(gradq * qg[0:1, :], qs, qi))
            parts.append(norm_back(gradk * qg[1:2, :], ks, ki))
            parts.append(dv[h, rows, :][:, :HD])
        qg_out[0:1, :] += gq
        qg_out[1:2, :] += gk
        mix = jnp.concatenate(parts, axis=1).astype(bf16)
        gna[0] = dot(mix, w[...], NT).astype(bf16)
        gin[...] += dot(a[...], mix, TN)

    @pl.when(i == pl.num_programs(0) - 1)
    def _():
        size = D // 4
        for p in range(4):
            r = (p >> 1) + (p & 1) * 2
            gin_out[p] = gin[rows_at(sc[4] ^ r, size), :].astype(bf16)


def tail_kernel(sc, gna, gna_in, gmid, x0, gains, own, other, hot, pk, ps, post, ga_out, tile):
    size = D // 8
    grad = gna[...].astype(f32) + gna_in[...].astype(f32)
    scaled, inv = norm_stats(x0[...])
    ga_out[0:1, :] = jnp.sum(grad * scaled, axis=0, keepdims=True)
    ga_out[1:8, :] = jnp.zeros((7, D), f32)
    ge = (gmid[...] + norm_back(grad * gains[0:1, :], scaled, inv)).astype(bf16)
    rows = jnp.where(sc[3] == 1, own[...], other[...])
    tile[...] = dot(rows, ge, TN)
    for p, r in enumerate(rel_order(2)):
        pk[p] = tile[rows_at(sc[0] ^ r, size), :].astype(bf16)
        ps[p] = tile[rows_at(sc[0] ^ (r + 1), size), :].astype(bf16)
    post[...] = dot(ge, hot[...], TN)


ANY = pl.BlockSpec(memory_space=pl.ANY)


def call(kernel, grid, sc, ins, specs, outs, out_specs, scratch, flops=0, nbytes=0):
    return pl.pallas_call(
        kernel,
        out_shape=outs,
        grid_spec=pltpu.PrefetchScalarGridSpec(
            num_scalar_prefetch=1,
            grid=grid,
            in_specs=specs,
            out_specs=out_specs,
            scratch_shapes=scratch,
        ),
        compiler_params=pltpu.CompilerParams(vmem_limit_bytes=VLIM),
        cost_estimate=pl.CostEstimate(flops=int(flops), bytes_accessed=int(nbytes), transcendentals=0),
    )(sc, *ins)


def whole(shape):
    return pl.BlockSpec(shape, lambda i, s: (0,) * len(shape))


def sds(shape, dtype):
    return jax.ShapeDtypeStruct(shape, dtype)


DMA = pltpu.SemaphoreType.DMA


def make_local(n_dp, n_mp):
    extra = n_dp // 8
    masks = [extra, 2 * extra, 4 * extra]
    low_bits = []
    m = 1
    while m < extra:
        low_bits.append(m)
        m *= 2
    cextra = n_dp // 8
    col_low = [2 * b for b in low_bits]
    col_masks = [2 * cextra, 4 * cextra]

    def pp(x, dmask, zmask=0):
        perm = [
            (d * n_mp + z, (d ^ dmask) * n_mp + (z ^ zmask))
            for d in range(n_dp)
            for z in range(n_mp)
        ]
        return lax.ppermute(x, ("dp", "mp"), perm)

    def local(
        patches, segment, keep, pos_y, pos_x, labels, bucket, *state
    ):
        masters, firsts, seconds = state[0::3], state[1::3], state[2::3]
        (attend_in, attend_out, expand, contract, patch_embed, pos_table, class_head,
         norm_gains, query_gains) = masters
        length = patches.shape[0]
        rows = patch_embed.shape[0]
        nq = length // BQ
        dp = lax.axis_index("dp")
        z = lax.axis_index("mp")
        core = dp % 2
        z1, z0 = z // 2, z % 2
        g = z0 + 2 * core
        me = dp // extra
        mecol = (dp // 2) // cextra
        mine = core == z1

        perm_core = [
            (d * n_mp + zz, (d ^ 1) * n_mp + zz)
            for d in range(n_dp)
            for zz in range(n_mp)
            if d % 2 == zz // 2
        ]
        patches_in = lax.ppermute(patches, ("dp", "mp"), perm_core)
        meta = jnp.stack([segment, keep, pos_y, pos_x])
        tag = jnp.concatenate([labels, bucket, jnp.zeros((length - IMG - 1,), jnp.int32)])
        meta = jnp.concatenate([meta, tag[None]], axis=0)
        meta = jnp.where(mine, meta, lax.ppermute(meta, ("dp", "mp"), perm_core))

        own_kept = (keep == 1) & (segment < IMG)
        own_valid = jnp.any(
            (segment[None, :] == jnp.arange(IMG)[:, None]) & own_kept[None, :], axis=1
        )
        own_hot = (bucket[0] == jnp.arange(128)).astype(f32)
        counts = jnp.broadcast_to(
            (own_hot * jnp.sum(own_valid.astype(f32)))[None, :], (8, 128)
        )

        def sum_dp(x):
            x = x + pp(x, 1)
            m = 2
            while m < n_dp:
                x = (x + pp(x, m)) + (pp(x, 2 * m) + pp(x, 3 * m))
                m *= 4
            return x

        def sum_z(x):
            return (x + pp(x, 0, 1)) + (pp(x, 0, 2) + pp(x, 0, 3))

        counts = sum_dp(counts)
        image_total = jnp.sum(counts[0])

        def bit_of(mask):
            return (dp // mask) % 2 == 1

        def swap(flag, x, y, axis):
            return jnp.where(
                flag, jnp.concatenate([y, x], axis=axis), jnp.concatenate([x, y], axis=axis)
            )

        def gather(x, low, order, unit):
            for b in low:
                x = swap(bit_of(b), x, pp(x, b), -2)
            got = {0: x}
            for m in order:
                for r in list(got):
                    got[r + m // unit] = pp(got[r], m)
            return [got[r] for r in range(len(got))]

        def gather_dp(x, first):
            a, b = (masks[1], masks[2]) if first == 2 else (masks[2], masks[1])
            return gather(x, low_bits, [a, b, masks[0]], extra)

        qcols = query_gains.shape[1]
        small = jnp.concatenate(
            [
                pos_table.T,
                norm_gains.T,
                jnp.pad(query_gains.reshape(2 * qcols, 1), ((0, rows - 2 * qcols), (0, 0))),
                jnp.zeros((rows, 59), f32),
            ],
            axis=1,
        )
        patch_p = gather_dp(
            jnp.concatenate([patch_embed, small], axis=1).astype(bf16), 2
        )

        perm_a, perm_b, back_b = [], [], []
        for d in range(n_dp):
            for zz in range(n_mp):
                c, a1, a0 = d % 2, zz // 2, zz % 2
                src = d * n_mp + zz
                perm_a.append((src, (d - c + a1) * n_mp + a0 + 2 * c))
                perm_b.append((src, (d - c + a1) * n_mp + a0 + 2 * (1 - c)))
                back_b.append((src, (d - c + 1 - a1) * n_mp + a0 + 2 * c))
        in_low = attend_in.astype(bf16)
        in_a = lax.ppermute(in_low, ("dp", "mp"), perm_a)
        in_b = lax.ppermute(in_low, ("dp", "mp"), perm_b)
        in_p = gather(swap(z1 == 1, in_a, in_b, 0), col_low, col_masks, 2 * cextra)

        def gather_z(x):
            return [x, pp(x, 0, 1), pp(x, 0, 2), pp(x, 0, 3)]

        def pick4(parts, index, axis):
            odd, high = index % 2 == 1, index // 2 == 1
            lo = swap(odd, parts[0], parts[1], axis)
            hi = swap(odd, parts[2], parts[3], axis)
            return swap(high, lo, hi, axis)

        out_p = gather_dp(pick4(gather_z(attend_out.T.astype(bf16)), z, 1), 2)
        head_p = gather_dp(
            jnp.pad(class_head, ((0, 0), (0, CPAD - CLASSES))).astype(bf16), 4
        )
        ex_p = gather_dp(jnp.stack(gather_z(expand.astype(bf16))), 2)
        con_p = gather_dp(jnp.stack(gather_z(contract.T.astype(bf16))), 4)

        size = D // 8

        def pick8(parts, axis):
            odd = me % 2 == 1
            pairs = [swap(odd, parts[2 * n], parts[2 * n + 1], axis) for n in range(4)]
            return pick4(pairs, me // 2, axis)

        small_all = pick8([p[:, D:] for p in patch_p], 0).T
        pos_rows = small_all[: 2 * GRID]
        gains = jnp.pad(small_all[2 * GRID : 2 * GRID + 4].astype(f32), ((0, 4), (0, 0)))
        qg = small_all[2 * GRID + 4].astype(f32).reshape(n_dp, rows)[:, : 2 * qcols]
        qg = qg.reshape(n_dp, 2, qcols).transpose(1, 0, 2).reshape(2, HD)
        qg = jnp.pad(qg, ((0, 6), (0, 0)))

        seg, kp, py, px = meta[0], meta[1], meta[2], meta[3]
        labs = meta[4, :IMG]
        buck = meta[4, IMG]
        kept = (kp == 1) & (seg < IMG)
        ids64 = jnp.arange(64)[None, :]
        hot_pos = ((py[:, None] == ids64) | (px[:, None] + GRID == ids64)).astype(bf16)
        same = seg[:, None] == ids64
        qaux = jnp.where((ids64 < IMG) & same, BIG, jnp.where(ids64 == IMG, 1.0, 0.0)).astype(bf16)
        kaux = jnp.where(
            (ids64 < IMG) & same & kept[:, None],
            1.0,
            jnp.where(
                ids64 == IMG,
                -BIG,
                jnp.where(
                    (ids64 > IMG) & (ids64 < IMG + 4),
                    1.0,
                    jnp.where((ids64 == IMG + 4) & ~kept[:, None], 1.0, 0.0),
                ),
            ),
        ).astype(bf16)
        vaux = jnp.broadcast_to(jnp.where(ids64 < 3, 1.0, 0.0).astype(bf16), (length, 64))
        first_seg, last_seg = seg[::BQ], jnp.minimum(seg[BQ - 1 :: BQ], IMG - 1)
        lo = jnp.sum((seg[None, :] < first_seg[:, None]).astype(jnp.int32), axis=1) // BQ
        hi = (jnp.sum((seg[None, :] <= last_seg[:, None]).astype(jnp.int32), axis=1) + BQ - 1) // BQ
        sc = jnp.concatenate(
            [
                jnp.stack([me, g, z, mine.astype(jnp.int32), mecol, mecol, mecol, mecol]),
                lo,
                hi,
            ]
        ).astype(jnp.int32)
        mem_all = ((seg[:, None] == jnp.arange(128)[None, :]) & kept[:, None]).astype(f32)
        mem_all = jnp.where(jnp.arange(128)[None, :] < IMG, mem_all, 0.0)[:, :IMG]
        valid = jnp.max(mem_all, axis=0)
        mem = lax.dynamic_slice_in_dim(mem_all, g * TOK, TOK, 0)
        hot_own = lax.dynamic_slice_in_dim(hot_pos, g * TOK, TOK, 0)
        vt = jnp.stack([valid, valid / image_total], axis=1)
        vt = jnp.pad(vt, ((0, 0), (0, 126)))
        lab_hot = (labs[:, None] == jnp.arange(CPAD)[None, :]).astype(f32)

        nt = length // TOK
        a, x0 = call(
            x0_kernel,
            (nt,),
            sc,
            [patches, patches_in, hot_pos, pos_rows, gains] + patch_p,
            [
                pl.BlockSpec((TOK, D), lambda i, s: (jnp.where(s[3] == 1, i, 0), 0)),
                pl.BlockSpec((TOK, D), lambda i, s: (jnp.where(s[3] == 1, 0, i), 0)),
                pl.BlockSpec((TOK, 64), lambda i, s: (i, 0)),
                whole((64, D)),
                whole((8, D)),
            ]
            + [ANY] * 8,
            (sds((length, D), bf16), sds((TOK, D), f32)),
            (pl.BlockSpec((TOK, D), lambda i, s: (i, 0)), whole((TOK, D))),
            [pltpu.VMEM((D, D + 128), bf16), DMA((8,))],
            2 * length * D * D,
            10e6,
        )
        qx, kx, vx, raw = call(
            qkv_kernel,
            (nt,),
            sc,
            [a, qaux, kaux, vaux, qg] + in_p,
            [
                pl.BlockSpec((TOK, D), lambda i, s: (i, 0)),
                pl.BlockSpec((TOK, 64), lambda i, s: (i, 0)),
                pl.BlockSpec((TOK, 64), lambda i, s: (i, 0)),
                pl.BlockSpec((TOK, 64), lambda i, s: (i, 0)),
                whole((8, HD)),
            ]
            + [ANY] * 4,
            tuple([sds((NH, length, 128), bf16)] * 3 + [sds((2 * NH, length, HD), f32)]),
            tuple(
                [pl.BlockSpec((NH, TOK, 128), lambda i, s: (0, i, 0))] * 3
                + [pl.BlockSpec((2 * NH, TOK, HD), lambda i, s: (0, i, 0))]
            ),
            [pltpu.VMEM((D, 576), bf16), DMA((4,))],
            2 * length * D * 576,
            10e6,
        )
        per_tok = TOK // BQ
        o_rel, o_full, ql = call(
            attn_kernel,
            (nq,),
            sc,
            [qx, kx, vx],
            [
                pl.BlockSpec((NH, BQ, 128), lambda i, s: (0, i, 0)),
                whole((NH, length, 128)),
                whole((NH, length, 128)),
            ],
            (
                sds((4, TOK, NH * HD), bf16),
                sds((length, NH * HD), f32),
                sds((NH, length, 128), bf16),
            ),
            (
                pl.BlockSpec(
                    (1, BQ, NH * HD), lambda i, s: (s[1] ^ (i // per_tok), i % per_tok, 0)
                ),
                pl.BlockSpec((BQ, NH * HD), lambda i, s: (i, 0)),
                pl.BlockSpec((NH, BQ, 128), lambda i, s: (0, i, 0)),
            ),
            [pltpu.VMEM((NH, BQ, 128), f32)],
            8e9,
            8e6,
        )

        def trade(parts):
            return [
                parts[0],
                pp(parts[1], 0, 1),
                pp(parts[2], 1, 0),
                pp(parts[3], 1, 1),
            ]

        o_cat = pick4(trade([o_rel[r] for r in range(4)]), g, 1)
        x1, b = call(
            mid_kernel,
            (1,),
            sc,
            [o_cat, x0, gains] + out_p,
            [whole((TOK, D)), whole((TOK, D)), whole((8, D))] + [ANY] * 8,
            (sds((TOK, D), f32), sds((TOK, D), bf16)),
            (whole((TOK, D)), whole((TOK, D))),
            [pltpu.VMEM((D, D), bf16), DMA((8,))],
            2 * TOK * D * D,
            6e6,
        )
        tile_spec = pl.BlockSpec((TOK, D), lambda j, s: (0, j))
        u, h = call(
            up_kernel,
            (4,),
            sc,
            [b] + ex_p,
            [whole((TOK, D))] + [ANY] * 8,
            (sds((TOK, HID), f32), sds((TOK, HID), bf16)),
            (tile_spec, tile_spec),
            [pltpu.VMEM((4, D, D), bf16), DMA((4, 8))],
            2 * TOK * D * HID,
            14e6,
        )
        x2, ns = call(
            down_kernel,
            (4,),
            sc,
            [h, x1, gains, mem] + con_p,
            [tile_spec, whole((TOK, D)), whole((8, D)), whole((TOK, IMG))] + [ANY] * 8,
            (sds((TOK, D), f32), sds((IMG, D + 128), f32)),
            (whole((TOK, D)), whole((IMG, D + 128))),
            [pltpu.VMEM((4, D, D), bf16), pltpu.VMEM((TOK, D), f32), DMA((4, 8))],
            2 * TOK * D * HID,
            12e6,
        )
        ns = ns + pp(ns, 1, 0)
        ns = ns + pp(ns, 0, 1)
        pooled, gp, sinv, loss, gh, gh_send = call(
            head_kernel,
            (1,),
            sc,
            [ns, lab_hot, vt] + head_p,
            [whole((IMG, D + 128)), whole((IMG, CPAD)), whole((IMG, 128))] + [ANY] * 8,
            (
                sds((IMG, D), f32),
                sds((IMG, D), f32),
                sds((IMG, 128), f32),
                sds((IMG, 128), f32),
                sds((4, size, CPAD // 2), bf16),
                sds((4, size, CPAD // 2), bf16),
            ),
            (
                whole((IMG, D)),
                whole((IMG, D)),
                whole((IMG, 128)),
                whole((IMG, 128)),
                whole((4, size, CPAD // 2)),
                whole((4, size, CPAD // 2)),
            ),
            [pltpu.VMEM((D, CPAD), bf16), pltpu.VMEM((D, CPAD // 2), f32), DMA((8,))],
            1e8,
            3e6,
        )

        gu, gr, gm, gmid, ga, small_b = call(
            back_kernel,
            (4,),
            sc,
            [u, x2, x1, gains, mem, pooled, gp, sinv] + ex_p + con_p + out_p,
            [
                tile_spec,
                whole((TOK, D)),
                whole((TOK, D)),
                whole((8, D)),
                whole((TOK, IMG)),
                whole((IMG, D)),
                whole((IMG, D)),
                whole((IMG, 128)),
            ]
            + [ANY] * 24,
            (
                sds((TOK, HID), bf16),
                sds((TOK, D), bf16),
                sds((TOK, D), bf16),
                sds((TOK, D), f32),
                sds((TOK, D), bf16),
                sds((8, D), f32),
            ),
            (
                tile_spec,
                whole((TOK, D)),
                whole((TOK, D)),
                whole((TOK, D)),
                whole((TOK, D)),
                whole((8, D)),
            ),
            [
                pltpu.VMEM((4, D, D), bf16),
                pltpu.VMEM((4, D, D), bf16),
                pltpu.VMEM((D, D), bf16),
                pltpu.VMEM((TOK, D), f32),
                pltpu.VMEM((TOK, D), f32),
                DMA((4, 8)),
                DMA((4, 8)),
                DMA((8,)),
            ],
            4 * TOK * D * HID,
            24e6,
        )
        ga4 = ga.reshape(TOK, 4, NH * HD).transpose(1, 0, 2)
        ga_rel = pick4([ga4[n : n + 1] for n in range(4)], g, 0)
        do = pick4([t[None] for t in trade([ga_rel[r] for r in range(4)])], g, 0)

        wide = pl.BlockSpec((4, 1, size, D), lambda j, s: (0, s[2] ^ j, 0, 0))
        ek, es, ck, cs, ok, os_ = call(
            wgrad_kernel,
            (4,),
            sc,
            [gr, h, b, gu, gm, o_cat],
            [whole((TOK, D)), tile_spec, whole((TOK, D)), tile_spec, whole((TOK, D)), whole((TOK, D))],
            tuple([sds((4, 4, size, D), bf16)] * 4 + [sds((4, size, D), bf16)] * 2),
            tuple([wide] * 4 + [whole((4, size, D))] * 2),
            [pltpu.VMEM((D, D), f32)],
            4 * TOK * D * HID,
            20e6,
        )

        def add(x, y):
            return x.astype(f32) + y.astype(f32)

        def low_rows(x, low):
            for b in reversed(low):
                half = x.shape[-2] // 2
                first, second = x[..., :half, :], x[..., half:, :]
                flag = bit_of(b)
                send = jnp.where(flag, first, second)
                stay = jnp.where(flag, second, first)
                x = add(stay, pp(send.astype(bf16), b))
            return x

        def scatter4(stay, low, m1, m2):
            x = add(stay[:2], pp(stay[2:].astype(bf16), m1))
            x = add(x[0].astype(bf16), pp(x[1].astype(bf16), m2))
            return low_rows(x, low)

        def scatter8(stay, send, first):
            x = add(stay, pp(send, masks[0])).astype(bf16)
            m1, m2 = (masks[1], masks[2]) if first == 2 else (masks[2], masks[1])
            return scatter4(x, low_bits, m1, m2)

        def scatter_z(parts):
            return (parts[0].astype(f32) + pp(parts[1], 0, 1)) + (
                pp(parts[2], 0, 2).astype(f32) + pp(parts[3], 0, 3)
            )

        def split_z(x):
            return scatter_z([x[r].astype(bf16) for r in range(4)])

        if extra == 1:
            gh = scatter4(gh, low_bits, masks[1], masks[2])
        else:
            gh = 0.5 * scatter8(gh, gh_send, 2)
        gh = add(gh.astype(bf16), pp(gh.astype(bf16), 0, 2))
        gh = swap(z0 == 1, gh, pp(gh, 0, 1), 1)[:, :CLASSES]

        share_ex = split_z(scatter8(ek, es, 2))
        share_con = split_z(scatter8(ck, cs, 4)).T
        go = scatter8(ok, os_, 2)
        go4 = go.reshape(rows, 4, NH * HD).transpose(1, 0, 2)
        share_out = split_z(pick4([go4[n : n + 1] for n in range(4)], z, 0)).T

        nsteps = nq + nt
        gna, gin, qgrad = call(
            attn_back_kernel,
            (nsteps,),
            sc,
            [ql, o_full, do, kx, vx, raw, a, qg] + in_p,
            [
                pl.BlockSpec((NH, BQ, 128), lambda i, s: (0, jnp.minimum(i, nq - 1), 0)),
                pl.BlockSpec((BQ, NH * HD), lambda i, s: (jnp.minimum(i, nq - 1), 0)),
                pl.BlockSpec(
                    (1, BQ, NH * HD),
                    lambda i, s: (
                        jnp.minimum(i, nq - 1) // per_tok,
                        jnp.minimum(i, nq - 1) % per_tok,
                        0,
                    ),
                ),
                whole((NH, length, 128)),
                whole((NH, length, 128)),
                pl.BlockSpec((2 * NH, TOK, HD), lambda i, s: (0, jnp.maximum(i - nq, 0), 0)),
                pl.BlockSpec((TOK, D), lambda i, s: (jnp.maximum(i - nq, 0), 0)),
                whole((8, HD)),
            ]
            + [ANY] * 4,
            (sds((4, TOK, D), bf16), sds((4, D // 4, 576), bf16), sds((8, HD), f32)),
            (
                pl.BlockSpec((1, TOK, D), lambda i, s: (s[1] ^ jnp.maximum(i - nq, 0), 0, 0)),
                whole((4, D // 4, 576)),
                whole((8, HD)),
            ),
            [
                pltpu.VMEM((NH, length, 128), f32),
                pltpu.VMEM((NH, length, 128), f32),
                pltpu.VMEM((NH, length, 128), f32),
                pltpu.VMEM((D, 576), f32),
                pltpu.VMEM((D, 576), bf16),
                DMA((4,)),
            ],
            20e9,
            20e6,
        )
        part = add(gna[:2], pp(gna[2:], 1)).astype(bf16)
        gna_in = pp(part[1], 0, 1)

        gin = scatter4(gin, col_low, col_masks[0], col_masks[1])
        gin = gin.astype(bf16).reshape(2, rows, 3 * NH * HD)
        share_in = add(
            lax.ppermute(jnp.where(z1 == 1, gin[1], gin[0]), ("dp", "mp"), perm_a),
            lax.ppermute(jnp.where(z1 == 1, gin[0], gin[1]), ("dp", "mp"), back_b),
        )

        own_rows = pl.BlockSpec((TOK, D), lambda i, s: (s[1], 0))
        pk, ps, post, gain_a = call(
            tail_kernel,
            (1,),
            sc,
            [part[0], gna_in, gmid, x0, gains, patches, patches_in, hot_own],
            [
                whole((TOK, D)),
                whole((TOK, D)),
                whole((TOK, D)),
                whole((TOK, D)),
                whole((8, D)),
                own_rows,
                own_rows,
                whole((TOK, 64)),
            ],
            (
                sds((4, size, D), bf16),
                sds((4, size, D), bf16),
                sds((D, 64), f32),
                sds((8, D), f32),
            ),
            (whole((4, size, D)), whole((4, size, D)), whole((D, 64)), whole((8, D))),
            [pltpu.VMEM((D, D), f32)],
            2 * TOK * D * D,
            8e6,
        )
        qg_cols = qgrad[:2].reshape(2, n_dp, qcols).transpose(1, 0, 2).reshape(n_dp, 2 * qcols)
        qg_cols = jnp.pad(qg_cols, ((0, 0), (0, rows - 2 * qcols))).reshape(D, 1)
        gain_cols = jnp.stack([gain_a[0], small_b[2], small_b[0], small_b[1]], axis=1)
        tiny = jnp.concatenate(
            [post, gain_cols, qg_cols, jnp.zeros((D, 59), f32)], axis=1
        ).astype(bf16)
        tiny = tiny.reshape(8, 1, size, 128)
        tiny = pick8([tiny[n] for n in range(8)], 0)
        order = rel_order(2)
        tk = jnp.stack([tiny[r] for r in order])
        ts = jnp.stack([tiny[r + 1] for r in order])
        gpatch = scatter8(pk, ps, 2).astype(bf16)
        gtiny = scatter8(tk, ts, 2).astype(bf16)
        quarter = rows // 4

        def z_rows(x):
            x4 = x.reshape(4, quarter, x.shape[-1])
            rel = pick4([x4[n : n + 1] for n in range(4)], z, 0)
            return scatter_z([rel[r] for r in range(4)])

        qpatch, qtiny = z_rows(gpatch), z_rows(gtiny)

        once = (z == 0).astype(f32)
        squares = (
            jnp.sum(share_in * share_in)
            + jnp.sum(share_out * share_out)
            + jnp.sum(share_ex * share_ex)
            + jnp.sum(share_con * share_con)
            + once * jnp.sum(gh * gh)
            + jnp.sum(qpatch * qpatch)
            + jnp.sum(qtiny * qtiny)
        )
        lane = jnp.arange(128)
        buck_hot = (lane == buck + 1).astype(f32) * (g == 0).astype(f32)
        stats = jnp.where(lane == 0, squares, 0.0) + buck_hot * jnp.sum(loss[:, 0])
        stats = sum_z(sum_dp(jnp.broadcast_to(stats[None, :], (8, 128))))
        grad_norm = jnp.sqrt(stats[0, 0])
        bucket_loss = stats[0, 1 : 1 + NB]
        factor = jnp.minimum(1.0, CLIP / (grad_norm + 1e-06))

        share_patch = pick4(gather_z(qpatch), z, 0)
        share_tiny = pick4(gather_z(qtiny), z, 0)
        shares = (
            share_in,
            share_out,
            share_ex,
            share_con,
            share_patch,
            share_tiny[:, : 2 * GRID].T,
            gh,
            share_tiny[:, 2 * GRID : 2 * GRID + 4].T,
            share_tiny[: 2 * qcols, 2 * GRID + 4].reshape(2, qcols),
        )
        results = [bucket_loss, counts[0, :NB], grad_norm]
        for index in range(9):
            clipped = shares[index] * factor
            first_new = BETA_ONE * firsts[index] + (1.0 - BETA_ONE) * clipped
            second_new = BETA_TWO * seconds[index] + (1.0 - BETA_TWO) * clipped * clipped
            matrix = index in (0, 1, 2, 3, 4, 6)
            rate = RATE_MATRIX if matrix else RATE_SMALL
            decay = DECAY if matrix else 0.0
            ratio = (
                first_new
                / (1.0 - BETA_ONE**STEP)
                / (jnp.sqrt(second_new / (1.0 - BETA_TWO**STEP)) + ADAM_EPS)
            )
            results += [
                masters[index] - rate * (ratio + decay * masters[index]),
                first_new,
                second_new,
            ]
        return tuple(results)

    return local


def solution(mesh):
    shard = {
        "in": P("dp", "mp"),
        "out": P("mp", "dp"),
        "row": P("dp", None),
        "col": P(None, "dp"),
    }
    kinds = ["in", "out", "in", "out", "row", "col", "row", "col", "col"]
    triples = tuple(shard[k] for k in kinds for _ in range(3))
    in_specs = (P("dp", None),) + (P("dp"),) * 6 + triples
    out_specs = (P(), P(), P()) + triples
    return jax.shard_map(
        make_local(mesh.shape["dp"], mesh.shape["mp"]),
        mesh=mesh,
        in_specs=in_specs,
        out_specs=out_specs,
        check_vma=False,
    )
```

time: 1420 us -> 605 us (0.43); the launches traced: 1410 us -> 610 us
  waiting for transfers between devices: 728 us -> 118 us
  matrix products: 241 us -> 0 us
  Pallas kernels: 0 us -> 236 us
  other arithmetic: 188 us -> 59 us
  blocking collectives: 128 us -> 0 us
  starting transfers between devices: 1.75 us -> 120 us
  local copies, waits for them, and re-layouts: 96.2 us -> 67.1 us
  between operations: 25.6 us -> 10.7 us
    psum x4 -> x0, waiting for transfers between devices: 414 us -> none  [the longest x1 120 us: local(): lax.psum(back_term.astype(jnp.bfloat16), 'mp').astype(jnp.float32)]
    dot_general x52 -> x0, matrix products: 241 us -> none  [the longest x4 31.8 us: attend_block(): jnp.einsum('thd,uhd->htu', query_blk, key_low, preferred_element_type=f32)]
    pallas_call x0 -> x11, Pallas kernels: none -> 236 us  [call(): pl.pallas_call(kernel, out_shape=outs, grid_spec=pltpu.PrefetchScalarGrid...]
    reduce_scatter x5 -> x0, waiting for transfers between devices: 169 us -> none  [the longest x1 40.2 us: local(): lax.psum_scatter(grad_head.astype(jnp.bfloat16), 'dp', scatter_dimension=...]
    ppermute x0 -> x116, starting transfers between devices: none -> 120 us  [the longest x110 108 us: pp(): return lax.ppermute(x, ('dp', 'mp'), perm)]
    ppermute x0 -> x116, waiting for transfers between devices: none -> 118 us  [the longest x110 117 us: pp(): return lax.ppermute(x, ('dp', 'mp'), perm)]
    unnamed x19 -> x0, waiting for transfers between devices: 104 us -> none
    reduce_sum x32 -> x11, other arithmetic: 90.9 us -> 6.65 us  [the longest x1 0.71 us: local(): jnp.sum(gh * gh)]
  transfers between devices with their start and end apart: 16 -> 116, of which waited for: 15 -> 36; matrix products, arithmetic and copies ran while one was open for 9% -> 15% of each run, Pallas kernels for 0% -> 33%
where the time goes in v1:
time: 605 us; the launch traced here: 610 us
  Pallas kernels  236 us (39%)
  starting transfers between devices  120 us (20%)
  waiting for transfers between devices  118 us (20%)
  local copies, waits for them, and re-layouts  67.1 us (11%)
  other arithmetic  59 us (10%)
  between operations  10.7 us (2%)
    pallas_call x11, Pallas kernels, call(): pl.pallas_call(kernel, out_shape=outs, grid_spec=pltpu.PrefetchScalarGrid...  236 us
    ppermute x110, waiting for transfers between devices, pp(): return lax.ppermute(x, ('dp', 'mp'), perm)  117 us
    ppermute x110, starting transfers between devices, pp(): return lax.ppermute(x, ('dp', 'mp'), perm)  108 us
    unnamed x227, local copies, waits for them, and re-layouts  18.2 us
    ppermute x7, local copies, waits for them, and re-layouts, pp(): return lax.ppermute(x, ('dp', 'mp'), perm)  12.2 us
  transfers between devices with their start and end apart: 116, of which 36 were waited for; matrix products, arithmetic and copies ran while one was open for 15% of the time, Pallas kernels for 33%

profile of v1, /device:TPU:0, one launch (start us, length us, event | category | flops | bytes accessed | tf_op | source)
XLA Modules:
  0.0 610.5 jit_solution(11747840392980605091)
XLA Ops:
  2.4 5.4 collective-permute-start.9
  29.0 2.6 collective-permute-start.18
  33.0 3.6 collective-permute-start.29
  40.3 4.3 collective-permute-start.1
  47.9 2.1 fusion.3.hot
  50.0 2.6 select_convert_fusion.kaux
  52.9 5.7 collective-permute-start.27
  66.7 3.7 collective-permute-start.37
  98.0 2.5 collective-permute-done.23.rest_4_.rest_20_
  102.1 2.7 collective-permute-done.56.rest_4_
  106.4 3.7 collective-permute-done.12.rest_2_
  117.3 10.4 %shard_map.553 = (bf16[2048,768]{1,0:T(8,128)(2,1)}, f32[512,768]{1,0:T(8,128)}) custom-call(s32[24]{0:T(128)} %concatenate.280.sc, bf16[2048,768]{1,0:T(8,128)(2,1)} %own.3, bf16[2048,768]{1,0:T(8,128)(2,1)} %collective-permute-done.1.other, bf16[2048,64]{1,0:T(8,128)(2,1)} %fusion.3.hot, bf16[64,768]{1,0:T(8,128)(2,1)} %slice.604.pos, ...), custom_call_target="tpu_custom_call" | custom-call | flops 2415919104 | bytes 10000000 | tf_op jit(solution)/shard_map/pallas_call | solution.py:469
  128.0 2.7 collective-permute-done.13.rest_3_
  131.5 20.1 %shard_map.554 = (bf16[3,2048,128]{2,1,0:T(8,128)(2,1)}, bf16[3,2048,128]{2,1,0:T(8,128)(2,1)}, bf16[3,2048,128]{2,1,0:T(8,128)(2,1)}, f32[6,2048,64]{2,1,0:T(8,128)}) custom-call(s32[24]{0:T(128)} %concatenate.280.sc, bf16[2048,768]{1,0:T(8,128)(2,1)} %get-tuple-element.69.a, bf16[2048,64]{1,0:T(8,128)(2,1)} %select_convert_fusion.1.qaux, ...), custom_call_target="tpu_custom_call" | custom-call | flops 1811939328 | bytes 10000000 | tf_op jit(solution)/shard_map/pallas_call | solution.py:469
  155.0 34.1 %shard_map.555 = (bf16[4,512,192]{2,1,0:T(8,128)(2,1)}, f32[2048,192]{1,0:T(8,128)}, bf16[3,2048,128]{2,1,0:T(8,128)(2,1)}) custom-call(s32[24]{0:T(128)} %concatenate.280.sc, bf16[3,2048,128]{2,1,0:T(8,128)(2,1)} %get-tuple-element.70.qx, bf16[3,2048,128]{2,1,0:T(8,128)(2,1)} %get-tuple-element.71.kx, bf16[3,2048,128]{2,1,0:T(8,128)(2,1)} %get-tuple-element.72.vx), custom_call_target="tpu_custom_call" | custom-call | flops 8000000000 | bytes 8000000 | tf_op jit(solution)/shard_map/pallas_call | solution.py:469
  194.7 10.1 %collective-permute-done.45.rest_6_.rest_14_ = bf16[4,96,768]{2,1,0:T(8,128)(2,1)S(1)} collective-permute-done((bf16[4,96,768]{2,1,0:T(8,128)(2,1)S(1)}, bf16[4,96,768]{2,1,0:T(8,128)(2,1)S(1)}, u32[]{:S(2)}, u32[]{:S(2)}) %collective-permute-start.45) | collective-permute-done | bytes 589856 | tf_op jit(solution)/shard_map/ppermute | solution.py:513
  207.6 6.0 shard_map.556
  214.9 9.3 %shard_map.557 = (f32[512,3072]{1,0:T(8,128)}, bf16[512,3072]{1,0:T(8,128)(2,1)}) custom-call(s32[24]{0:T(128)} %concatenate.280.sc, bf16[512,768]{1,0:T(8,128)(2,1)} %get-tuple-element.77.b, bf16[4,96,768]{2,1,0:T(8,128)(2,1)} %copy-done.10, bf16[4,96,768]{2,1,0:T(8,128)(2,1)} %collective-permute-done.30.rest_1_, ...), custom_call_target="tpu_custom_call" | custom-call | flops 2415919104 | bytes 14000000 | tf_op jit(solution)/shard_map/pallas_call | solution.py:469
  226.2 14.6 %shard_map.558 = (f32[512,768]{1,0:T(8,128)}, f32[16,896]{1,0:T(8,128)}) custom-call(s32[24]{0:T(128)} %concatenate.280.sc, bf16[512,3072]{1,0:T(8,128)(2,1)} %get-tuple-element.79.h, f32[512,768]{1,0:T(8,128)} %get-tuple-element.80.x1, f32[8,768]{1,0:T(8,128)} %pad_convert_fusion.gains, f32[512,16]{1,0:T(8,128)} %constant_dynamic-slice_fusion.1.mem, ...), custom_call_target="tpu_custom_call" | custom-call | flops 2415919104 | bytes 12000000 | tf_op jit(solution)/shard_map/pallas_call | solution.py:469
  251.0 5.5 shard_map.559
  256.5 27.6 %shard_map.560 = (bf16[512,3072]{1,0:T(8,128)(2,1)}, bf16[512,768]{1,0:T(8,128)(2,1)}, bf16[512,768]{1,0:T(8,128)(2,1)}, f32[512,768]{1,0:T(8,128)}, bf16[512,768]{1,0:T(8,128)(2,1)}, /*index=5*/f32[8,768]{1,0:T(8,128)}) custom-call(s32[24]{0:T(128)} %concatenate.280.sc, f32[512,3072]{1,0:T(8,128)} %get-tuple-element.78.u, f32[512,768]{1,0:T(8,128)} %get-tuple-element.81.x2, ...), custom_call_target="tpu_custom_call" | custom-call | flops 4831838208 | bytes 24000000 | tf_op jit(solution)/shard_map/pallas_call | solution.py:469
  289.1 13.3 %shard_map.562 = (bf16[4,4,96,768]{3,2,1,0:T(8,128)(2,1)}, bf16[4,4,96,768]{3,2,1,0:T(8,128)(2,1)}, bf16[4,4,96,768]{3,2,1,0:T(8,128)(2,1)}, bf16[4,4,96,768]{3,...) custom-call(s32[24]{0:T(128)} %concatenate.280.sc, bf16[512,768]{1,0:T(8,128)(2,1)} %get-tuple-element.89.gr, ...), custom_call_target="tpu_custom_call" | custom-call | flops 4831838208 | bytes 20000000 | tf_op jit(solution)/shard_map/pallas_call | solution.py:469
  306.5 3.3 collective-permute-done.85
  311.6 87.9 %shard_map.561 = (bf16[4,512,768]{2,1,0:T(8,128)(2,1)}, bf16[4,192,576]{2,1,0:T(8,128)(2,1)}, f32[8,64]{1,0:T(8,128)}) custom-call(s32[24]{0:T(128)} %concatenate.280.sc, bf16[3,2048,128]{2,1,0:T(8,128)(2,1)} %get-tuple-element.73.ql, f32[2048,192]{1,0:T(8,128)} %get-tuple-element.74.of, bf16[4,512,192]{2,1,0:T(8,128)(2,1)} %maximum_select_fusion.1.do, ...), custom_call_target="tpu_custom_call" | custom-call | flops 20000000000 | bytes 20000000 | tf_op jit(solution)/shard_map/pallas_call | solution.py:469
  401.3 2.8 slice.530
  405.3 3.7 collective-permute-done.87
  410.0 4.3 collective-permute-done.63
  418.6 2.2 collective-permute-done.88
  425.7 3.3 collective-permute-done.68
  437.8 16.2 %collective-permute-done.90.gna_in = bf16[512,768]{1,0:T(8,128)(2,1)S(1)} collective-permute-done((bf16[512,768]{1,0:T(8,128)(2,1)S(1)}, bf16[512,768]{1,0:T(8,128)(2,1)S(1)}, u32[]{:S(2)}, u32[]{:S(2)}) %collective-permute-start.90) | collective-permute-done | bytes 786464 | tf_op jit(solution)/shard_map/ppermute | solution.py:513
  454.9 6.9 %shard_map.563 = (bf16[4,96,768]{2,1,0:T(8,128)(2,1)}, bf16[4,96,768]{2,1,0:T(8,128)(2,1)}, f32[768,64]{1,0:T(8,128)}, f32[8,768]{1,0:T(8,128)}) custom-call(s32[24]{0:T(128)} %concatenate.280.sc, bf16[512,768]{1,0:T(8,128)(2,1)} %get-tuple-element.295.gna, bf16[512,768]{1,0:T(8,128)(2,1)} %copy-done.25, f32[512,768]{1,0:T(8,128)} %get-tuple-element.100.gmid, ...), custom_call_target="tpu_custom_call" | custom-call | flops 603979776 | bytes 8000000 | tf_op jit(solution)/shard_map/pallas_call | solution.py:469
  466.8 2.4 collective-permute-start.71
  479.7 3.1 collective-permute-start.100
  482.8 2.3 add_convert_fusion.1
  488.9 2.4 add_convert_fusion
  493.8 2.1 collective-permute-start.113
  496.7 2.6 collective-permute-done.113
  499.3 19.9 %collective-permute-done.92 = bf16[2,96,768]{2,1,0:T(8,128)(2,1)S(1)} collective-permute-done((bf16[2,96,768]{2,1,0:T(8,128)(2,1)S(1)}, bf16[2,96,768]{2,1,0:T(8,128)(2,1)S(1)}, u32[]{:S(2)}, u32[]{:S(2)}) %collective-permute-start.92) | collective-permute-done | bytes 294944 | tf_op jit(solution)/shard_map/ppermute | solution.py:513
  523.8 2.4 collective-permute-done.93
  528.1 2.6 collective-permute-start.94
  530.7 5.8 collective-permute-done.75
  539.8 2.3 collective-permute-start.76
  545.3 7.1 %collective-permute-start.82 = (bf16[96,768]{1,0:T(8,128)(2,1)}, bf16[96,768]{1,0:T(8,128)(2,1)S(1)}, u32[]{:S(2)}, u32[]{:S(2)}) collective-permute-start(bf16[96,768]{1,0:T(8,128)(2,1)} %get-tuple-element.310), channel_id=1, source_target_pairs={{0,1},{1,0},{2,3},{3,2},{4,5},{5,4},{6,7},{7,6},{8,9},{9,8},{10,11... | collective-permute-start | bytes 442376 | tf_op jit(solution)/shard_map/ppermute | solution.py:513
  553.1 5.0 collective-permute-done.77
  559.4 3.4 collective-permute-done.83
  570.4 2.4 collective-permute-start.106
  572.8 2.5 collective-permute-done.112
  601.0 2.1 multiply_subtract_fusion.1
  (652 shorter events, 206.3 us)
Async XLA Ops:
  1.8 51.2 %collective-permute-start.10 = (bf16[96,576]{1,0:T(8,128)(2,1)S(1)}, bf16[96,576]{1,0:T(8,128)(2,1)S(1)}, u32[]{:S(2)}, u32[]{:S(2)}) collective-permute-start(bf16[96,576]{1,0:T(8,128)(2,1)S(1)} %convert_element_type.428), channel_id=1, source_target_pairs={{0,0},{1,1},{2,4},{3,5},{4,2},{5,3},{6,6},{7,7},{8,8},{9,9},{10,12... | collective-permute-start | bytes 331784 | tf_op jit(solution)/shard_map/ppermute | solution.py:612
  2.4 56.2 %collective-permute-start.9 = (bf16[96,576]{1,0:T(8,128)(2,1)S(1)}, bf16[96,576]{1,0:T(8,128)(2,1)S(1)}, u32[]{:S(2)}, u32[]{:S(2)}) collective-permute-start(bf16[96,576]{1,0:T(8,128)(2,1)S(1)} %convert_element_type.428), channel_id=1, source_target_pairs={{0,2},{1,3},{2,6},{3,7},{4,0},{5,1},{6,4},{7,5},{8,10},{9,11},{10,... | collective-permute-start | bytes 331784 | tf_op jit(solution)/shard_map/ppermute | solution.py:613
  33.0 25.7 %collective-permute-start.29 = (bf16[96,768]{1,0:T(8,128)(2,1)S(1)}, bf16[96,768]{1,0:T(8,128)(2,1)S(1)}, u32[]{:S(2)}, u32[]{:S(2)}) collective-permute-start(bf16[96,768]{1,0:T(8,128)(2,1)S(1)} %convert_element_type.431), channel_id=1, source_target_pairs={{0,3},{1,2},{2,1},{3,0},{4,7},{5,6},{6,5},{7,4},{8,11},{9,10},{10,... | collective-permute-start | bytes 442376 | tf_op jit(solution)/shard_map/ppermute | solution.py:513
  36.7 24.1 %collective-permute-start.28 = (bf16[96,768]{1,0:T(8,128)(2,1)S(1)}, bf16[96,768]{1,0:T(8,128)(2,1)S(1)}, u32[]{:S(2)}, u32[]{:S(2)}) collective-permute-start(bf16[96,768]{1,0:T(8,128)(2,1)S(1)} %convert_element_type.431), channel_id=1, source_target_pairs={{0,2},{1,3},{2,0},{3,1},{4,6},{5,7},{6,4},{7,5},{8,10},{9,11},{10,... | collective-permute-start | bytes 442376 | tf_op jit(solution)/shard_map/ppermute | solution.py:513
  40.3 75.4 %collective-permute-start.1 = (bf16[2048,768]{1,0:T(8,128)(2,1)}, bf16[2048,768]{1,0:T(8,128)(2,1)}, u32[]{:S(2)}, u32[]{:S(2)}) collective-permute-start(bf16[2048,768]{1,0:T(8,128)(2,1)} %own.3), channel_id=1, source_target_pairs={{0,4},{1,5},{6,2},{7,3},{8,12},{9,13},{14,10},{15,11},{16,20},{17,... | collective-permute-start | bytes 9437192 | tf_op jit(solution)/shard_map/ppermute | solution.py:539
  77.8 24.2 %collective-permute-start.54 = (bf16[96,1024]{1,0:T(8,128)(2,1)S(1)}, bf16[96,1024]{1,0:T(8,128)(2,1)}, u32[]{:S(2)}, u32[]{:S(2)}) collective-permute-start(bf16[96,1024]{1,0:T(8,128)(2,1)S(1)} %pad.37.rest_0_), channel_id=1, source_target_pairs={{0,8},{1,9},{2,10},{3,11},{4,12},{5,13},{6,14},{7,15},{8,0},{9,1},... | collective-permute-start | bytes 589832 | tf_op jit(solution)/shard_map/ppermute | solution.py:513
  102.0 51.3 %collective-permute-start.30 = (bf16[4,96,768]{2,1,0:T(8,128)(2,1)S(1)}, bf16[4,96,768]{2,1,0:T(8,128)(2,1)}, u32[]{:S(2)}, u32[]{:S(2)}) collective-permute-start(bf16[4,96,768]{2,1,0:T(8,128)(2,1)S(1)} %pad_maximum_fusion.rest_0_), channel_id=1, source_target_pairs={{0,4},{1,5},{2,6},{3,7},{4,0},{5,1},{6,2},{7,3},{8,12},{9,13},{10,... | collective-permute-start | bytes 1769480 | tf_op jit(solution)/shard_map/ppermute | solution.py:513
  104.8 48.5 %collective-permute-start.31 = (bf16[4,96,768]{2,1,0:T(8,128)(2,1)S(1)}, bf16[4,96,768]{2,1,0:T(8,128)(2,1)}, u32[]{:S(2)}, u32[]{:S(2)}) collective-permute-start(bf16[4,96,768]{2,1,0:T(8,128)(2,1)S(1)} %pad_maximum_fusion.rest_0_), channel_id=1, source_target_pairs={{0,8},{1,9},{2,10},{3,11},{4,12},{5,13},{6,14},{7,15},{8,0},{9,1},... | collective-permute-start | bytes 1769480 | tf_op jit(solution)/shard_map/ppermute | solution.py:513
  105.9 49.0 %collective-permute-start.33 = (bf16[4,96,768]{2,1,0:T(8,128)(2,1)S(1)}, bf16[4,96,768]{2,1,0:T(8,128)(2,1)}, u32[]{:S(2)}, u32[]{:S(2)}) collective-permute-start(bf16[4,96,768]{2,1,0:T(8,128)(2,1)S(1)} %pad_maximum_fusion.rest_0_), channel_id=1, source_target_pairs={{0,16},{1,17},{2,18},{3,19},{4,20},{5,21},{6,22},{7,23},{8,24},{9,... | collective-permute-start | bytes 1769480 | tf_op jit(solution)/shard_map/ppermute | solution.py:513
  127.8 23.9 %collective-permute-start.24 = (bf16[96,768]{1,0:T(8,128)(2,1)S(1)}, bf16[96,768]{1,0:T(8,128)(2,1)S(1)}, u32[]{:S(2)}, u32[]{:S(2)}) collective-permute-start(bf16[96,768]{1,0:T(8,128)(2,1)S(1)} %collective-permute-done.23.rest_4_.rest_20_), channel_id=1, source_target_pairs={{0,4},{1,5},{2,6},{3,7},{4,0},{5,1},{6,2},{7,3},{8,12},{9,13},{10,... | collective-permute-start | bytes 442376 | tf_op jit(solution)/shard_map/ppermute | solution.py:513
  130.6 22.1 %collective-permute-start.26 = (bf16[96,768]{1,0:T(8,128)(2,1)S(1)}, bf16[96,768]{1,0:T(8,128)(2,1)S(1)}, u32[]{:S(2)}, u32[]{:S(2)}) collective-permute-start(bf16[96,768]{1,0:T(8,128)(2,1)S(1)} %collective-permute-done.25.rest_6_.rest_22_), channel_id=1, source_target_pairs={{0,4},{1,5},{2,6},{3,7},{4,0},{5,1},{6,2},{7,3},{8,12},{9,13},{10,... | collective-permute-start | bytes 442376 | tf_op jit(solution)/shard_map/ppermute | solution.py:513
  151.6 39.4 %collective-permute-start.41 = (bf16[4,96,768]{2,1,0:T(8,128)(2,1)S(1)}, bf16[4,96,768]{2,1,0:T(8,128)(2,1)S(1)}, u32[]{:S(2)}, u32[]{:S(2)}) collective-permute-start(bf16[4,96,768]{2,1,0:T(8,128)(2,1)S(1)} %pad_maximum_fusion.1.rest_0_.rest_8_), channel_id=1, source_target_pairs={{0,8},{1,9},{2,10},{3,11},{4,12},{5,13},{6,14},{7,15},{8,0},{9,1},... | collective-permute-start | bytes 1769480 | tf_op jit(solution)/shard_map/ppermute | solution.py:513
  152.8 36.4 %collective-permute-start.43 = (bf16[4,96,768]{2,1,0:T(8,128)(2,1)S(1)}, bf16[4,96,768]{2,1,0:T(8,128)(2,1)S(1)}, u32[]{:S(2)}, u32[]{:S(2)}) collective-permute-start(bf16[4,96,768]{2,1,0:T(8,128)(2,1)S(1)} %pad_maximum_fusion.1.rest_0_.rest_8_), channel_id=1, source_target_pairs={{0,16},{1,17},{2,18},{3,19},{4,20},{5,21},{6,22},{7,23},{8,24},{9,... | collective-permute-start | bytes 1769480 | tf_op jit(solution)/shard_map/ppermute | solution.py:513
  153.3 39.8 %collective-permute-start.32 = (bf16[4,96,768]{2,1,0:T(8,128)(2,1)}, bf16[4,96,768]{2,1,0:T(8,128)(2,1)S(1)}, u32[]{:S(2)}, u32[]{:S(2)}) collective-permute-start(bf16[4,96,768]{2,1,0:T(8,128)(2,1)} %collective-permute-done.31.rest_2_), channel_id=1, source_target_pairs={{0,4},{1,5},{2,6},{3,7},{4,0},{5,1},{6,2},{7,3},{8,12},{9,13},{10,... | collective-permute-start | bytes 1769480 | tf_op jit(solution)/shard_map/ppermute | solution.py:513
  153.3 37.4 %collective-permute-start.35 = (bf16[4,96,768]{2,1,0:T(8,128)(2,1)}, bf16[4,96,768]{2,1,0:T(8,128)(2,1)}, u32[]{:S(2)}, u32[]{:S(2)}) collective-permute-start(bf16[4,96,768]{2,1,0:T(8,128)(2,1)} %collective-permute-done.31.rest_2_), channel_id=1, source_target_pairs={{0,16},{1,17},{2,18},{3,19},{4,20},{5,21},{6,22},{7,23},{8,24},{9,... | collective-permute-start | bytes 1769480 | tf_op jit(solution)/shard_map/ppermute | solution.py:513
  154.9 38.2 %collective-permute-start.34 = (bf16[4,96,768]{2,1,0:T(8,128)(2,1)}, bf16[4,96,768]{2,1,0:T(8,128)(2,1)S(1)}, u32[]{:S(2)}, u32[]{:S(2)}) collective-permute-start(bf16[4,96,768]{2,1,0:T(8,128)(2,1)} %collective-permute-done.33.rest_4_), channel_id=1, source_target_pairs={{0,4},{1,5},{2,6},{3,7},{4,0},{5,1},{6,2},{7,3},{8,12},{9,13},{10,... | collective-permute-start | bytes 1769480 | tf_op jit(solution)/shard_map/ppermute | solution.py:513
  189.2 15.6 %collective-permute-start.45 = (bf16[4,96,768]{2,1,0:T(8,128)(2,1)S(1)}, bf16[4,96,768]{2,1,0:T(8,128)(2,1)S(1)}, u32[]{:S(2)}, u32[]{:S(2)}) collective-permute-start(bf16[4,96,768]{2,1,0:T(8,128)(2,1)S(1)} %collective-permute-done.43.rest_4_.rest_12_), channel_id=1, source_target_pairs={{0,8},{1,9},{2,10},{3,11},{4,12},{5,13},{6,14},{7,15},{8,0},{9,1},... | collective-permute-start | bytes 1769480 | tf_op jit(solution)/shard_map/ppermute | solution.py:513
  190.7 22.9 %collective-permute-start.36 = (bf16[4,96,768]{2,1,0:T(8,128)(2,1)}, bf16[4,96,768]{2,1,0:T(8,128)(2,1)}, u32[]{:S(2)}, u32[]{:S(2)}) collective-permute-start(bf16[4,96,768]{2,1,0:T(8,128)(2,1)} %collective-permute-done.35.rest_6_), channel_id=1, source_target_pairs={{0,4},{1,5},{2,6},{3,7},{4,0},{5,1},{6,2},{7,3},{8,12},{9,13},{10,... | collective-permute-start | bytes 1769480 | tf_op jit(solution)/shard_map/ppermute | solution.py:513
  204.8 19.6 %collective-permute-start.40 = (bf16[4,96,768]{2,1,0:T(8,128)(2,1)S(1)}, bf16[4,96,768]{2,1,0:T(8,128)(2,1)S(1)}, u32[]{:S(2)}, u32[]{:S(2)}) collective-permute-start(bf16[4,96,768]{2,1,0:T(8,128)(2,1)S(1)} %pad_maximum_fusion.1.rest_0_.rest_8_), channel_id=1, source_target_pairs={{0,4},{1,5},{2,6},{3,7},{4,0},{5,1},{6,2},{7,3},{8,12},{9,13},{10,... | collective-permute-start | bytes 1769480 | tf_op jit(solution)/shard_map/ppermute | solution.py:513
  204.9 20.1 %collective-permute-start.44 = (bf16[4,96,768]{2,1,0:T(8,128)(2,1)S(1)}, bf16[4,96,768]{2,1,0:T(8,128)(2,1)S(1)}, u32[]{:S(2)}, u32[]{:S(2)}) collective-permute-start(bf16[4,96,768]{2,1,0:T(8,128)(2,1)S(1)} %collective-permute-done.43.rest_4_.rest_12_), channel_id=1, source_target_pairs={{0,4},{1,5},{2,6},{3,7},{4,0},{5,1},{6,2},{7,3},{8,12},{9,13},{10,... | collective-permute-start | bytes 1769480 | tf_op jit(solution)/shard_map/ppermute | solution.py:513
  205.3 19.5 %collective-permute-start.42 = (bf16[4,96,768]{2,1,0:T(8,128)(2,1)S(1)}, bf16[4,96,768]{2,1,0:T(8,128)(2,1)S(1)}, u32[]{:S(2)}, u32[]{:S(2)}) collective-permute-start(bf16[4,96,768]{2,1,0:T(8,128)(2,1)S(1)} %collective-permute-done.41.rest_2_.rest_10_), channel_id=1, source_target_pairs={{0,4},{1,5},{2,6},{3,7},{4,0},{5,1},{6,2},{7,3},{8,12},{9,13},{10,... | collective-permute-start | bytes 1769480 | tf_op jit(solution)/shard_map/ppermute | solution.py:513
  205.4 19.9 %collective-permute-start.46 = (bf16[4,96,768]{2,1,0:T(8,128)(2,1)S(1)}, bf16[4,96,768]{2,1,0:T(8,128)(2,1)S(1)}, u32[]{:S(2)}, u32[]{:S(2)}) collective-permute-start(bf16[4,96,768]{2,1,0:T(8,128)(2,1)S(1)} %collective-permute-done.45.rest_6_.rest_14_), channel_id=1, source_target_pairs={{0,4},{1,5},{2,6},{3,7},{4,0},{5,1},{6,2},{7,3},{8,12},{9,13},{10,... | collective-permute-start | bytes 1769480 | tf_op jit(solution)/shard_map/ppermute | solution.py:513
  224.2 25.3 %collective-permute-start.53 = (bf16[96,1024]{1,0:T(8,128)(2,1)S(1)}, bf16[96,1024]{1,0:T(8,128)(2,1)S(1)}, u32[]{:S(2)}, u32[]{:S(2)}) collective-permute-start(bf16[96,1024]{1,0:T(8,128)(2,1)S(1)} %pad.37.rest_0_), channel_id=1, source_target_pairs={{0,4},{1,5},{2,6},{3,7},{4,0},{5,1},{6,2},{7,3},{8,12},{9,13},{10,... | collective-permute-start | bytes 589832 | tf_op jit(solution)/shard_map/ppermute | solution.py:513
  224.4 25.2 %collective-permute-start.57 = (bf16[96,1024]{1,0:T(8,128)(2,1)}, bf16[96,1024]{1,0:T(8,128)(2,1)S(1)}, u32[]{:S(2)}, u32[]{:S(2)}) collective-permute-start(bf16[96,1024]{1,0:T(8,128)(2,1)} %collective-permute-done.56.rest_4_), channel_id=1, source_target_pairs={{0,4},{1,5},{2,6},{3,7},{4,0},{5,1},{6,2},{7,3},{8,12},{9,13},{10,... | collective-permute-start | bytes 589832 | tf_op jit(solution)/shard_map/ppermute | solution.py:513
  224.8 24.7 %collective-permute-start.55 = (bf16[96,1024]{1,0:T(8,128)(2,1)}, bf16[96,1024]{1,0:T(8,128)(2,1)S(1)}, u32[]{:S(2)}, u32[]{:S(2)}) collective-permute-start(bf16[96,1024]{1,0:T(8,128)(2,1)} %collective-permute-done.54.rest_2_), channel_id=1, source_target_pairs={{0,4},{1,5},{2,6},{3,7},{4,0},{5,1},{6,2},{7,3},{8,12},{9,13},{10,... | collective-permute-start | bytes 589832 | tf_op jit(solution)/shard_map/ppermute | solution.py:513
  224.9 24.7 %collective-permute-start.59 = (bf16[96,1024]{1,0:T(8,128)(2,1)S(1)}, bf16[96,1024]{1,0:T(8,128)(2,1)S(1)}, u32[]{:S(2)}, u32[]{:S(2)}) collective-permute-start(bf16[96,1024]{1,0:T(8,128)(2,1)S(1)} %collective-permute-done.58.rest_6_), channel_id=1, source_target_pairs={{0,4},{1,5},{2,6},{3,7},{4,0},{5,1},{6,2},{7,3},{8,12},{9,13},{10,... | collective-permute-start | bytes 589832 | tf_op jit(solution)/shard_map/ppermute | solution.py:513
  286.9 19.4 %collective-permute-start.62 = (bf16[512,192]{1,0:T(8,128)(2,1)S(1)}, bf16[512,192]{1,0:T(8,128)(2,1)S(1)}, u32[]{:S(2)}, u32[]{:S(2)}) collective-permute-start(bf16[512,192]{1,0:T(8,128)(2,1)S(1)} %get-tuple-element.298), channel_id=1, source_target_pairs={{0,1},{1,0},{2,3},{3,2},{4,5},{5,4},{6,7},{7,6},{8,9},{9,8},{10,11... | collective-permute-start | bytes 589832 | tf_op jit(solution)/shard_map/ppermute | solution.py:513
  288.7 21.3 %collective-permute-start.61 = (bf16[512,192]{1,0:T(8,128)(2,1)S(1)}, bf16[512,192]{1,0:T(8,128)(2,1)S(1)}, u32[]{:S(2)}, u32[]{:S(2)}) collective-permute-start(bf16[512,192]{1,0:T(8,128)(2,1)S(1)} %get-tuple-element.299), channel_id=1, source_target_pairs={{0,4},{1,5},{2,6},{3,7},{4,0},{5,1},{6,2},{7,3},{8,12},{9,13},{10,... | collective-permute-start | bytes 589832 | tf_op jit(solution)/shard_map/ppermute | solution.py:513
  288.7 21.4 %collective-permute-start.60 = (bf16[512,192]{1,0:T(8,128)(2,1)S(1)}, bf16[512,192]{1,0:T(8,128)(2,1)S(1)}, u32[]{:S(2)}, u32[]{:S(2)}) collective-permute-start(bf16[512,192]{1,0:T(8,128)(2,1)S(1)} %get-tuple-element.296), channel_id=1, source_target_pairs={{0,5},{1,4},{2,7},{3,6},{4,1},{5,0},{6,3},{7,2},{8,13},{9,12},{10,... | collective-permute-start | bytes 589832 | tf_op jit(solution)/shard_map/ppermute | solution.py:513
  302.4 114.4 %collective-permute-start.67 = (bf16[4,96,768]{2,1,0:T(8,128)(2,1)}, bf16[4,96,768]{2,1,0:T(8,128)(2,1)S(1)}, u32[]{:S(2)}, u32[]{:S(2)}) collective-permute-start(bf16[4,96,768]{2,1,0:T(8,128)(2,1)} %get-tuple-element.93), channel_id=1, source_target_pairs={{0,4},{1,5},{2,6},{3,7},{4,0},{5,1},{6,2},{7,3},{8,12},{9,13},{10,... | collective-permute-start | bytes 1769480 | tf_op jit(solution)/shard_map/ppermute | solution.py:513
  306.3 173.4 %collective-permute-start.73 = (bf16[4,4,96,768]{3,2,1,0:T(8,128)(2,1)}, bf16[4,4,96,768]{3,2,1,0:T(8,128)(2,1)}, u32[]{:S(2)}, u32[]{:S(2)}) collective-permute-start(bf16[4,4,96,768]{3,2,1,0:T(8,128)(2,1)} %get-tuple-element.95), channel_id=1, source_target_pairs={{0,4},{1,5},{2,6},{3,7},{4,0},{5,1},{6,2},{7,3},{8,12},{9,13},{10,... | collective-permute-start | bytes 7077896 | tf_op jit(solution)/shard_map/ppermute | solution.py:513
  309.9 179.0 %collective-permute-start.79 = (bf16[4,4,96,768]{3,2,1,0:T(8,128)(2,1)}, bf16[4,4,96,768]{3,2,1,0:T(8,128)(2,1)}, u32[]{:S(2)}, u32[]{:S(2)}) collective-permute-start(bf16[4,4,96,768]{3,2,1,0:T(8,128)(2,1)} %get-tuple-element.97), channel_id=1, source_target_pairs={{0,4},{1,5},{2,6},{3,7},{4,0},{5,1},{6,2},{7,3},{8,12},{9,13},{10,... | collective-permute-start | bytes 7077896 | tf_op jit(solution)/shard_map/ppermute | solution.py:513
  310.0 90.6 %collective-permute-start.86 = (bf16[96,512]{1,0:T(8,128)(2,1)S(1)}, bf16[96,512]{1,0:T(8,128)(2,1)S(1)}, u32[]{:S(2)}, u32[]{:S(2)}) collective-permute-start(bf16[96,512]{1,0:T(8,128)(2,1)S(1)} %slice_bitcast_fusion.27), channel_id=1, source_target_pairs={{0,16},{1,17},{2,18},{3,19},{4,20},{5,21},{6,22},{7,23},{8,24},{9,... | collective-permute-start | bytes 294920 | tf_op jit(solution)/shard_map/ppermute | solution.py:513
  409.0 21.7 %collective-permute-start.89 = (bf16[2,512,768]{2,1,0:T(8,128)(2,1)}, bf16[2,512,768]{2,1,0:T(8,128)(2,1)}, u32[]{:S(2)}, u32[]{:S(2)}) collective-permute-start(bf16[2,512,768]{2,1,0:T(8,128)(2,1)} %slice.530), channel_id=1, source_target_pairs={{0,4},{1,5},{2,6},{3,7},{4,0},{5,1},{6,2},{7,3},{8,12},{9,13},{10,... | collective-permute-start | bytes 4718600 | tf_op jit(solution)/shard_map/ppermute | solution.py:513
  433.6 20.4 %collective-permute-start.90 = (bf16[512,768]{1,0:T(8,128)(2,1)S(1)}, bf16[512,768]{1,0:T(8,128)(2,1)S(1)}, u32[]{:S(2)}, u32[]{:S(2)}) collective-permute-start(bf16[512,768]{1,0:T(8,128)(2,1)S(1)} %get-tuple-element.294), channel_id=1, source_target_pairs={{0,1},{1,0},{2,3},{3,2},{4,5},{5,4},{6,7},{7,6},{8,9},{9,8},{10,11... | collective-permute-start | bytes 2359304 | tf_op jit(solution)/shard_map/ppermute | solution.py:513
  485.3 34.7 %collective-permute-start.74 = (bf16[2,4,96,768]{3,2,1,0:T(8,128)(2,1)S(1)}, bf16[2,4,96,768]{3,2,1,0:T(8,128)(2,1)S(1)}, u32[]{:S(2)}, u32[]{:S(2)}) collective-permute-start(bf16[2,4,96,768]{3,2,1,0:T(8,128)(2,1)S(1)} %slice.635), channel_id=1, source_target_pairs={{0,8},{1,9},{2,10},{3,11},{4,12},{5,13},{6,14},{7,15},{8,0},{9,1},... | collective-permute-start | bytes 3538952 | tf_op jit(solution)/shard_map/ppermute | solution.py:513
  487.7 31.5 %collective-permute-start.92 = (bf16[2,96,768]{2,1,0:T(8,128)(2,1)S(1)}, bf16[2,96,768]{2,1,0:T(8,128)(2,1)S(1)}, u32[]{:S(2)}, u32[]{:S(2)}) collective-permute-start(bf16[2,96,768]{2,1,0:T(8,128)(2,1)S(1)} %slice.655), channel_id=1, source_target_pairs={{0,8},{1,9},{2,10},{3,11},{4,12},{5,13},{6,14},{7,15},{8,0},{9,1},... | collective-permute-start | bytes 884744 | tf_op jit(solution)/shard_map/ppermute | solution.py:513
  491.3 30.5 %collective-permute-start.80 = (bf16[2,4,96,768]{3,2,1,0:T(8,128)(2,1)S(1)}, bf16[2,4,96,768]{3,2,1,0:T(8,128)(2,1)S(1)}, u32[]{:S(2)}, u32[]{:S(2)}) collective-permute-start(bf16[2,4,96,768]{3,2,1,0:T(8,128)(2,1)S(1)} %slice.643), channel_id=1, source_target_pairs={{0,16},{1,17},{2,18},{3,19},{4,20},{5,21},{6,22},{7,23},{8,24},{9,... | collective-permute-start | bytes 3538952 | tf_op jit(solution)/shard_map/ppermute | solution.py:513
  520.4 16.2 %collective-permute-start.75 = (bf16[4,96,768]{2,1,0:T(8,128)(2,1)S(1)}, bf16[4,96,768]{2,1,0:T(8,128)(2,1)S(1)}, u32[]{:S(2)}, u32[]{:S(2)}) collective-permute-start(bf16[4,96,768]{2,1,0:T(8,128)(2,1)S(1)} %slice_bitcast_fusion.4), channel_id=1, source_target_pairs={{0,16},{1,17},{2,18},{3,19},{4,20},{5,21},{6,22},{7,23},{8,24},{9,... | collective-permute-start | bytes 1769480 | tf_op jit(solution)/shard_map/ppermute | solution.py:513
  522.2 15.6 %collective-permute-start.81 = (bf16[4,96,768]{2,1,0:T(8,128)(2,1)S(1)}, bf16[4,96,768]{2,1,0:T(8,128)(2,1)S(1)}, u32[]{:S(2)}, u32[]{:S(2)}) collective-permute-start(bf16[4,96,768]{2,1,0:T(8,128)(2,1)S(1)} %slice_bitcast_fusion.2), channel_id=1, source_target_pairs={{0,8},{1,9},{2,10},{3,11},{4,12},{5,13},{6,14},{7,15},{8,0},{9,1},... | collective-permute-start | bytes 1769480 | tf_op jit(solution)/shard_map/ppermute | solution.py:513
  527.0 15.1 %collective-permute-start.95 = (bf16[24,768]{1,0:T(8,128)(2,1)S(1)}, bf16[24,768]{1,0:T(8,128)(2,1)S(1)}, u32[]{:S(2)}, u32[]{:S(2)}) collective-permute-start(bf16[24,768]{1,0:T(8,128)(2,1)S(1)} %get-tuple-element.347), channel_id=1, source_target_pairs={{0,2},{1,3},{2,0},{3,1},{4,6},{5,7},{6,4},{7,5},{8,10},{9,11},{10,... | collective-permute-start | bytes 110600 | tf_op jit(solution)/shard_map/ppermute | solution.py:513
  537.7 20.4 %collective-permute-start.77 = (bf16[96,768]{1,0:T(8,128)(2,1)S(1)}, bf16[96,768]{1,0:T(8,128)(2,1)S(1)}, u32[]{:S(2)}, u32[]{:S(2)}) collective-permute-start(bf16[96,768]{1,0:T(8,128)(2,1)S(1)} %get-tuple-element.315), channel_id=1, source_target_pairs={{0,2},{1,3},{2,0},{3,1},{4,6},{5,7},{6,4},{7,5},{8,10},{9,11},{10,... | collective-permute-start | bytes 442376 | tf_op jit(solution)/shard_map/ppermute | solution.py:513
  539.8 18.3 %collective-permute-start.76 = (bf16[96,768]{1,0:T(8,128)(2,1)S(1)}, bf16[96,768]{1,0:T(8,128)(2,1)S(1)}, u32[]{:S(2)}, u32[]{:S(2)}) collective-permute-start(bf16[96,768]{1,0:T(8,128)(2,1)S(1)} %get-tuple-element.313), channel_id=1, source_target_pairs={{0,1},{1,0},{2,3},{3,2},{4,5},{5,4},{6,7},{7,6},{8,9},{9,8},{10,11... | collective-permute-start | bytes 442376 | tf_op jit(solution)/shard_map/ppermute | solution.py:513
  542.1 17.3 %collective-permute-start.84 = (bf16[96,768]{1,0:T(8,128)(2,1)}, bf16[96,768]{1,0:T(8,128)(2,1)S(1)}, u32[]{:S(2)}, u32[]{:S(2)}) collective-permute-start(bf16[96,768]{1,0:T(8,128)(2,1)} %get-tuple-element.311), channel_id=1, source_target_pairs={{0,3},{1,2},{2,1},{3,0},{4,7},{5,6},{6,5},{7,4},{8,11},{9,10},{10,... | collective-permute-start | bytes 442376 | tf_op jit(solution)/shard_map/ppermute | solution.py:513
  543.1 19.7 %collective-permute-start.83 = (bf16[96,768]{1,0:T(8,128)(2,1)}, bf16[96,768]{1,0:T(8,128)(2,1)S(1)}, u32[]{:S(2)}, u32[]{:S(2)}) collective-permute-start(bf16[96,768]{1,0:T(8,128)(2,1)} %get-tuple-element.312), channel_id=1, source_target_pairs={{0,2},{1,3},{2,0},{3,1},{4,6},{5,7},{6,4},{7,5},{8,10},{9,11},{10,... | collective-permute-start | bytes 442376 | tf_op jit(solution)/shard_map/ppermute | solution.py:513
  545.3 17.5 %collective-permute-start.82 = (bf16[96,768]{1,0:T(8,128)(2,1)}, bf16[96,768]{1,0:T(8,128)(2,1)S(1)}, u32[]{:S(2)}, u32[]{:S(2)}) collective-permute-start(bf16[96,768]{1,0:T(8,128)(2,1)} %get-tuple-element.310), channel_id=1, source_target_pairs={{0,1},{1,0},{2,3},{3,2},{4,5},{5,4},{6,7},{7,6},{8,9},{9,8},{10,11... | collective-permute-start | bytes 442376 | tf_op jit(solution)/shard_map/ppermute | solution.py:513
  566.2 16.2 %collective-permute-start.111 = (f32[24,768]{1,0:T(8,128)S(1)}, f32[24,768]{1,0:T(8,128)S(1)}, u32[]{:S(2)}, u32[]{:S(2)}) collective-permute-start(f32[24,768]{1,0:T(8,128)S(1)} %get-tuple-element.291), channel_id=1, source_target_pairs={{0,2},{1,3},{2,0},{3,1},{4,6},{5,7},{6,4},{7,5},{8,10},{9,11},{10,... | collective-permute-start | bytes 221192 | tf_op jit(solution)/shard_map/ppermute | solution.py:513
  566.3 16.1 %collective-permute-start.110 = (f32[24,768]{1,0:T(8,128)S(1)}, f32[24,768]{1,0:T(8,128)S(1)}, u32[]{:S(2)}, u32[]{:S(2)}) collective-permute-start(f32[24,768]{1,0:T(8,128)S(1)} %get-tuple-element.291), channel_id=1, source_target_pairs={{0,3},{1,2},{2,1},{3,0},{4,7},{5,6},{6,5},{7,4},{8,11},{9,10},{10,... | collective-permute-start | bytes 221192 | tf_op jit(solution)/shard_map/ppermute | solution.py:513
  (176 other events, 2314.2 us)

commit v2 on v1

v2 whole, which is shorter than its diff:
```python
import jax
import jax.numpy as jnp
from jax import lax
from jax.experimental import pallas as pl
from jax.experimental.pallas import tpu as pltpu
from jax.sharding import PartitionSpec as P

D = 768
HD = 64
HID = 3072
CLASSES = 1000
CPAD = 1024
GRID = 32
IMG = 16
NB = 4
STEP = 10
BQ = 256
TOK = 512
NH = 3
QK = 2 * NH * HD
SUB = D // 8
SMALL = 128
LANE_GAIN = 64
LANE_QG = 68
LANE_COUNT = 72

HIGH = lax.Precision.HIGHEST
NORM_EPS = 1e-06
CLIP = 0.1
BETA_ONE = 0.9
BETA_TWO = 0.95
RATE_MATRIX = 0.05
RATE_SMALL = 0.2
DECAY = 0.05
ADAM_EPS = 1e-08
BIG = 128.0

bf16 = jnp.bfloat16
f32 = jnp.float32
VLIM = 56 * 1024 * 1024

NN = (((1,), (0,)), ((), ()))
NT = (((1,), (1,)), ((), ()))
TN = (((0,), (0,)), ((), ()))


def dot(a, b, dims=NN, precision=None):
    return lax.dot_general(a, b, dims, precision=precision, preferred_element_type=f32)


def norm_stats(values):
    center = values - jnp.mean(values, axis=-1, keepdims=True)
    inv_std = lax.rsqrt(jnp.mean(center * center, axis=-1, keepdims=True) + NORM_EPS)
    return center * inv_std, inv_std


def norm_back(grad_scaled, scaled, inv_std):
    return inv_std * (
        grad_scaled
        - jnp.mean(grad_scaled, axis=-1, keepdims=True)
        - scaled * jnp.mean(grad_scaled * scaled, axis=-1, keepdims=True)
    )


def splits(x, n):
    out = []
    for _ in range(n - 1):
        part = x.astype(bf16)
        out.append(part)
        x = x - part.astype(f32)
    out.append(x.astype(bf16))
    return out


def dot_split(x, exact, n, dims=NN):
    total = None
    for part in splits(x, n):
        term = dot(part, exact, dims)
        total = term if total is None else total + term
    return total


def eye(rows, cols, offset=0):
    row = lax.broadcasted_iota(jnp.int32, (rows, cols), 0)
    col = lax.broadcasted_iota(jnp.int32, (rows, cols), 1)
    return (row + offset == col).astype(f32)


def rows_at(index, size):
    return pl.ds(pl.multiple_of(index * size, size), size)


def pack_kernel(w_in, w_out, w_up, w_down, w_patch, w_pos, w_gain, w_qg, cnt,
                patch_o, in_o, z_o, out_o):
    rows = w_patch.shape[0]
    patch_o[:, :D] = w_patch[...].astype(bf16)
    low = lambda ref: ref[...].astype(bf16).astype(f32)
    small = dot(low(w_pos), eye(64, SMALL), TN)
    small += dot(low(w_gain), eye(4, SMALL, LANE_GAIN), TN)
    qg = dot(low(w_qg), eye(2, SMALL, LANE_QG), TN)
    small += dot(eye(rows, qg.shape[0]), qg)
    small += dot(eye(rows, 8), cnt[...])
    patch_o[:, D:] = small.astype(bf16)
    w = w_in[...].astype(bf16)
    parts = [
        w[:, h * 192 + part * HD : h * 192 + part * HD + HD]
        for part in range(3)
        for h in range(NH)
    ]
    in_o[...] = jnp.concatenate(parts, axis=1)
    z_o[0] = w_up[...].astype(bf16)
    z_o[1] = w_down[...].astype(bf16)
    out_o[...] = dot(eye(rows, rows).astype(bf16), w_out[...].astype(bf16), NT).astype(bf16)


def ordered(flag, x, y):
    return jnp.where(flag, jnp.concatenate([y, x], axis=1), jnp.concatenate([x, y], axis=1))


def xor_columns(parts, index):
    odd, high = index % 2 == 1, index // 2 == 1
    return ordered(high, ordered(odd, parts[0], parts[1]), ordered(odd, parts[2], parts[3]))


def first_kernel(sc, z_w, o0, o1, o2, o3, head, f_out):
    f_out[:, :D] = z_w[0]
    f_out[:, D : 2 * D] = z_w[1]
    outs = [o[...].astype(f32) for o in (o0, o1, o2, o3)]
    f_out[:, 2 * D : 3 * D] = xor_columns(outs, sc[2]).astype(bf16)
    f_out[:, 3 * D :] = jnp.zeros_like(f_out[:, 3 * D :])
    f_out[:, 3 * D : 3 * D + CLASSES] = head[...].astype(bf16)


def second_kernel(z1, z2, z3, g_out):
    for n, ref in enumerate((z1, z2, z3)):
        g_out[2 * n] = ref[0]
        g_out[2 * n + 1] = ref[1]


REL = [0, 2, 4, 6, 1, 3, 5, 7]


def row_copies(refs, me, dst, sems, rel=REL):
    out = []
    for n, ref in enumerate(refs):
        size = ref.shape[0]
        out.append(pltpu.make_async_copy(ref, dst.at[rows_at(me ^ rel[n], size), :], sems.at[n]))
    return out


def columns(refs, lo, width):
    return [ref.at[:, pl.ds(lo, width)] for ref in refs]


def start(copies):
    for copy in copies:
        copy.start()


def wait(copies):
    for copy in copies:
        copy.wait()


def x0_kernel(sc, own, other, hot, *rest):
    refs = rest[:8]
    a_out, x0_out, gx_out, w, sems = rest[8:]
    i = pl.program_id(0)

    @pl.when(i == 0)
    def _():
        copies = row_copies(refs, sc[0], w, sems)
        start(copies)
        wait(copies)
        row = lax.broadcasted_iota(jnp.int32, (16, SMALL), 0)
        col = lax.broadcasted_iota(jnp.int32, (16, SMALL), 1)
        pick = (row + LANE_GAIN == col).astype(f32).astype(bf16)
        gx_out[...] = dot(pick, w[:, D:], NT)

    rows = jnp.where(sc[3] == 1, own[...], other[...])
    x0 = dot(rows, w[:, :D]) + dot(hot[...], w[:, D:], NT)
    scaled, _ = norm_stats(x0)
    a_out[...] = (scaled * gx_out[0:1, :]).astype(bf16)

    @pl.when(i == sc[1])
    def _():
        x0_out[...] = x0


IN_REL = [0, 1, 2, 3]


def qkv_kernel(sc, a, qaux, kaux, vaux, gain, avg, *rest):
    refs = rest[:4]
    qx, kx, vx, xh_out, inv_out, w, sems = rest[4:]
    i = pl.program_id(0)

    @pl.when(i == 0)
    def _():
        copies = row_copies(refs, sc[4], w, sems, IN_REL)
        start(copies)
        wait(copies)

    mixed = dot(a[...], w[...])
    qk = mixed[:, :QK]
    v = mixed[:, QK:].astype(bf16)
    ones = avg[...]
    center = qk - dot_split(qk, ones, 2)
    inv = lax.rsqrt(dot_split(center * center, ones, 2) + NORM_EPS)
    scaled = center * inv
    xh_out[...] = scaled
    inv_out[...] = inv
    low = (scaled * gain[0:1, :]).astype(bf16)
    qa, ka, va = qaux[...], kaux[...], vaux[...]
    for h in range(NH):
        qx[h] = jnp.concatenate([low[:, h * HD : h * HD + HD], qa], axis=1)
        kx[h] = jnp.concatenate([low[:, (NH + h) * HD : (NH + h) * HD + HD], ka], axis=1)
        vx[h] = jnp.concatenate([v[:, h * HD : h * HD + HD], va], axis=1)


def attn_kernel(sc, qx, kx, vx, o_rel, o_full, ql, acc):
    i = pl.program_id(0)
    acc[...] = jnp.zeros_like(acc)
    lo, hi = sc[8 + i], sc[16 + i]

    def tile(start_row, size):
        ks = pl.ds(pl.multiple_of(start_row, BQ), size)
        scores = [dot(qx[h], kx[h, ks, :], NT) for h in range(NH)]
        probs = [jnp.exp(s).astype(bf16) for s in scores]
        for h in range(NH):
            acc[h] += dot(probs[h], vx[h, ks, :])

    pairs = (hi - lo) // 2

    def step(j, carry):
        tile((lo + 2 * j) * BQ, 2 * BQ)
        return carry

    lax.fori_loop(0, pairs, step, 0)

    @pl.when((hi - lo) % 2 == 1)
    def _():
        tile((hi - 1) * BQ, BQ)

    mine = rows_at(i, BQ)
    lane = lax.broadcasted_iota(jnp.int32, (BQ, 128), 1)
    outs = []
    for h in range(NH):
        q = qx[h].astype(f32)
        k = kx[h, mine, :].astype(f32)
        v = vx[h, mine, :].astype(f32)
        free = k[:, 84:85]
        diag = jnp.sum(jnp.where(lane < HD, q * k, 0.0), axis=1, keepdims=True)
        p = jnp.exp(diag) * free
        out = acc[h] + p.astype(bf16).astype(f32) * v
        total = out[:, 64:65]
        outs.append(out[:, :HD] / total)
        for n, part in enumerate(splits(-jnp.log(total), 3)):
            q = jnp.where(lane == 81 + n, part.astype(f32), q)
        ql[h] = q.astype(bf16)
    full = jnp.concatenate(outs, axis=1)
    o_full[...] = full
    o_rel[0] = full.astype(bf16)


GELU_C = 0.7978845608028654


def gelu_tanh(u):
    return jnp.tanh(GELU_C * (u + 0.044715 * u * u * u))


def mlp_tile(b, w, u_out, h_out):
    u = dot(b, w[0])
    u_out[...] = u
    h = (0.5 * u * (1.0 + gelu_tanh(u))).astype(bf16)
    h_out[...] = h
    return dot(h, w[1], NT)


def first_tile(refs, me, dst, sems):
    return row_copies(columns(refs, 0, D), me, dst.at[0], sems.at[0]) + row_copies(
        columns(refs, D, D), me, dst.at[1], sems.at[1]
    )


def later_tile(refs, t, me, dst, sems):
    return row_copies([r.at[2 * t] for r in refs], me, dst.at[0], sems.at[0]) + row_copies(
        [r.at[2 * t + 1] for r in refs], me, dst.at[1], sems.at[1]
    )


def mlp_one_kernel(sc, o, x0, gx, *rest):
    refs = rest[:8]
    x1_out, b_out, u_out, h_out, acc, w_o, w_t, sem_o, sem_t = rest[8:]
    first = row_copies(columns(refs, 2 * D, D), sc[0], w_o, sem_o)
    tile = first_tile(refs, sc[0], w_t, sem_t)
    start(first)
    start(tile)
    wait(first)
    x1 = x0[...] + dot(o[...], w_o[...], NT)
    x1_out[...] = x1
    b_out[...] = (norm_stats(x1)[0] * gx[1:2, :]).astype(bf16)
    wait(tile)
    acc[...] = x1 + mlp_tile(b_out[...], w_t, u_out, h_out)


def mlp_two_kernel(sc, b, acc_in, gx, mem, heads, *rest):
    refs = rest[:8]
    u_out, h_out, x2, ns_out, w_t, sem_t = rest[8:]
    j = pl.program_id(0)

    @pl.when(j == 0)
    def _():
        for t in range(3):
            start(later_tile(refs, t, sc[0], w_t.at[t], sem_t.at[t]))
        x2[...] = acc_in[...]

    for t in range(3):

        @pl.when(j == t)
        def _():
            wait(later_tile(refs, t, sc[0], w_t.at[t], sem_t.at[t]))

    x2[...] += mlp_tile(b[...], w_t.at[j], u_out, h_out)

    @pl.when(j == 2)
    def _():
        f = norm_stats(x2[...])[0] * gx[2:3, :]
        ones = heads[...]
        e = jnp.exp(dot_split(f * gx[3:4, :], ones, 3) * 0.125)
        eb = dot_split(e, ones, 2, NT)
        m = mem[...]
        num = jnp.zeros((IMG, D), f32)
        for part in splits(eb * f, 3):
            num += dot(m, part, TN)
        den = jnp.zeros((IMG, 128), f32)
        for part in splits(e, 3):
            den += dot(m, part, TN)
        ns_out[:, :D] = num
        ns_out[:, D:] = den


def head_kernel(sc, ns_a, ns_b, lab, vt, heads, *rest):
    pooled_out, gp_out, sinv_out, loss_out, gh_out, gh_send, w, gw, sems = rest[8:]
    copies = row_copies(columns(rest[:8], 3 * D, CPAD), sc[0], w, sems)
    start(copies)
    ns = ns_a[...] + ns_b[...]
    valid = vt[:, 0:1]
    scale = vt[:, 1:2]
    total = jnp.where(valid > 0.0, ns[:, D:], 1.0)
    sinv = jnp.where(valid > 0.0, 1.0 / total, 0.0)
    lane = lax.broadcasted_iota(jnp.int32, (IMG, 128), 1)
    sinv = jnp.where(lane < D // HD, sinv, 0.0)
    pooled = ns[:, :D] * dot_split(sinv, heads[...], 3, NT)
    low = pooled.astype(bf16)
    wait(copies)
    logits = dot(low, w[...])
    cls = lax.broadcasted_iota(jnp.int32, (IMG, CPAD), 1)
    real = (cls < CLASSES).astype(f32)
    hot = lab[...]
    ex = jnp.exp(-jnp.abs(logits))
    soft = jnp.maximum(logits, 0.0) + jnp.log1p(ex)
    per = jnp.sum(soft * real, axis=1, keepdims=True) - jnp.sum(
        logits * hot, axis=1, keepdims=True
    )
    loss_out[...] = jnp.broadcast_to(per * valid, (IMG, 128))
    sig = jnp.where(logits >= 0.0, 1.0, ex) / (1.0 + ex)
    gl = (scale * (sig * real - hot)).astype(bf16)
    pooled_out[...] = pooled
    sinv_out[...] = sinv
    gp_out[...] = dot(gl, w[...], NT)
    half = jnp.where(sc[2] % 2 == 1, gl[:, 512:].astype(f32), gl[:, :512].astype(f32))
    gw[...] = dot(low, half.astype(bf16), TN)
    for p, r in enumerate(rel_order(2)):
        gh_out[p] = gw[rows_at(sc[0] ^ r, SUB), :].astype(bf16)
        gh_send[p] = gw[rows_at(sc[0] ^ (r + 1), SUB), :].astype(bf16)


def rel_order(first):
    m1, m2 = (2, 4) if first == 2 else (4, 2)
    return [(p >> 1) * m1 + (p & 1) * m2 for p in range(4)]


def back_kernel(sc, u_a, u_b, x2, x1, gx, mem, pooled, gp, sinv, heads, *rest):
    refs, later = rest[:8], rest[8:16]
    gu_out, gr_out, gm_out, gmid_out, ga_out, small_out = rest[16:22]
    w_t, w_o, grs, acc, sem_t, sem_o = rest[22:]
    j = pl.program_id(0)

    def tile(t):
        if t == 0:
            return first_tile(refs, sc[0], w_t.at[0], sem_t.at[0])
        return later_tile(later, t - 1, sc[0], w_t.at[t], sem_t.at[t])

    def out_rows():
        return row_copies(columns(refs, 2 * D, D), sc[0], w_o, sem_o)

    @pl.when(j == 0)
    def _():
        for t in range(4):
            start(tile(t))
        start(out_rows())
        scaled, inv = norm_stats(x2[...])
        f = scaled * gx[2:3, :]
        probe = gx[3:4, :]
        ones = heads[...]
        e = jnp.exp(dot_split(f * probe, ones, 3) * 0.125)
        m = mem[...]
        m3 = jnp.concatenate([m, m, m], axis=1)

        def spread(x):
            return dot(m3, jnp.concatenate(splits(x, 3), axis=0))

        gt = spread(gp[...])
        at = e * spread(sinv[...])
        gpp = dot_split(gp[...] * pooled[...], ones, 3)
        da = dot_split(gt * f, ones, 3)
        dc = at * (da - spread(gpp))
        dcb = dot_split(dc, ones, 2, NT) * 0.125
        df = dot_split(at, ones, 2, NT) * gt + dcb * probe
        gr = norm_back(df * gx[2:3, :], scaled, inv)
        grs[...] = gr
        gr_out[...] = gr.astype(bf16)
        small_out[2:3, :] = jnp.sum(df * scaled, axis=0, keepdims=True)
        small_out[3:4, :] = jnp.sum(dcb * f, axis=0, keepdims=True)
        small_out[0:1, :] = jnp.zeros((1, D), f32)
        small_out[4:8, :] = jnp.zeros((4, D), f32)
        acc[...] = jnp.zeros_like(acc)

    for t in range(4):

        @pl.when(j == t)
        def _():
            wait(tile(t))

    gh = dot(gr_out[...], w_t[j, 1])
    v = jnp.where(j < 1, u_a[...], u_b[...])
    t = gelu_tanh(v)
    slope = 0.5 * (1.0 + t) + 0.5 * v * (1.0 - t * t) * GELU_C * (1.0 + 0.134145 * v * v)
    gu = (gh * slope).astype(bf16)
    gu_out[...] = gu
    acc[...] += dot(gu, w_t[j, 0], NT)

    @pl.when(j == 3)
    def _():
        wait(out_rows())
        scaled, inv = norm_stats(x1[...])
        gb = acc[...]
        small_out[1:2, :] = jnp.sum(gb * scaled, axis=0, keepdims=True)
        gmid = grs[...] + norm_back(gb * gx[1:2, :], scaled, inv)
        gmid_out[...] = gmid
        low = gmid.astype(bf16)
        gm_out[...] = low
        ga_out[...] = dot(low, w_o[...]).astype(bf16)


def wgrad_kernel(sc, gr, h_a, h_b, b, gu, gm, o, ek, es, ck, cs, tile):
    j = pl.program_id(0)

    def emit(keep, send, first):
        for p, r in enumerate(rel_order(first)):
            keep[p, 0] = tile[rows_at(sc[0] ^ r, SUB), :].astype(bf16)
            send[p, 0] = tile[rows_at(sc[0] ^ (r + 1), SUB), :].astype(bf16)

    @pl.when(j < 4)
    def _():
        h = jnp.where(j < 1, h_a[...].astype(f32), h_b[...].astype(f32)).astype(bf16)
        tile[...] = dot(gr[...], h, TN)
        emit(ck, cs, 4)
        tile[...] = dot(b[...], gu[...], TN)
        emit(ek, es, 2)

    @pl.when(j == 4)
    def _():
        tile[...] = dot(gm[...], o[...], TN)
        emit(ek, es, 2)


def attn_back_kernel(sc, ql, of, do, kx, vx, g_out, dq, dk, dv):
    i = pl.program_id(0)
    nq = dk.shape[1] // BQ

    @pl.when(i == 0)
    def _():
        dk[...] = jnp.zeros_like(dk)
        dv[...] = jnp.zeros_like(dv)

    @pl.when(i < nq)
    def _():
        mine = rows_at(i, BQ)
        lane = lax.broadcasted_iota(jnp.int32, (BQ, 128), 1)
        dob, qb = [], []
        for h in range(NH):
            dof = do[0, :, h * HD : h * HD + HD].astype(f32)
            delta = jnp.sum(dof * of[:, h * HD : h * HD + HD], axis=1, keepdims=True)
            dox = jnp.concatenate([dof, jnp.zeros((BQ, HD), f32)], axis=1)
            for n, part in enumerate(splits(-delta, 3)):
                dox = jnp.where(lane == HD + n, part.astype(f32), dox)
            q = ql[h].astype(f32)
            k = kx[h, mine, :].astype(f32)
            v = vx[h, mine, :].astype(f32)
            free = k[:, 84:85]
            inner = (lane < HD) | ((lane >= 81) & (lane < 84))
            p = jnp.exp(jnp.sum(jnp.where(inner, q * k, 0.0), axis=1, keepdims=True)) * free
            ds = p * jnp.sum(jnp.where(lane < HD + 3, dox * v, 0.0), axis=1, keepdims=True)
            ds = ds.astype(bf16).astype(f32)
            dq[h, mine, :] = ds * k
            dk[h, mine, :] += ds * q
            dv[h, mine, :] += p.astype(bf16).astype(f32) * dox
            dob.append(dox.astype(bf16))
            qb.append(ql[h])

        def step(j, carry):
            ks = rows_at(j, BQ)
            pts = [jnp.exp(dot(kx[h, ks, :], qb[h], NT)) for h in range(NH)]
            dpts = [dot(vx[h, ks, :], dob[h], NT) for h in range(NH)]
            dsts = [(pts[h] * dpts[h]).astype(bf16) for h in range(NH)]
            for h in range(NH):
                dv[h, ks, :] += dot(pts[h].astype(bf16), dob[h])
                dk[h, ks, :] += dot(dsts[h], qb[h])
                dq[h, mine, :] += dot(dsts[h], kx[h, ks, :], TN)
            return carry

        lax.fori_loop(sc[8 + i], sc[16 + i], step, 0)

    @pl.when(i >= nq)
    def _():
        rows = rows_at(i - nq, TOK)
        g_out[...] = jnp.concatenate(
            [ref[h, rows, :][:, :HD] for ref in (dq, dk, dv) for h in range(NH)], axis=1
        )


def mix_kernel(sc, grad, xh, inv, a, gain, avg, *rest):
    refs = rest[:4]
    g_send, g_one, g_own, in_keep, in_send, qg_out, gin, w, sems = rest[4:]
    n = pl.program_id(0)

    @pl.when(n == 0)
    def _():
        copies = row_copies(refs, sc[4], w, sems, IN_REL)
        start(copies)
        gin[...] = jnp.zeros_like(gin)
        qg_out[...] = jnp.zeros_like(qg_out)
        wait(copies)

    grads = grad[:, :QK]
    scaled = xh[...]
    ones = avg[...]
    qg_out[0:1, :] += jnp.sum(grads * scaled, axis=0, keepdims=True)
    dg = grads * gain[0:1, :]
    back = inv[...] * (
        dg - dot_split(dg, ones, 2) - scaled * dot_split(dg * scaled, ones, 2)
    )
    mix = jnp.concatenate([back, grad[:, QK:]], axis=1).astype(bf16)
    out = dot(mix, w[...], NT).astype(bf16)
    gin[...] += dot(a[...], mix, TN)

    @pl.when(n < 2)
    def _():
        g_send[0] = out

    @pl.when(n == 2)
    def _():
        g_one[...] = out

    @pl.when(n == 3)
    def _():
        g_own[...] = out
        size = D // 4
        for p in range(2):
            in_keep[p] = gin[rows_at(sc[4] ^ (2 * p), size), :].astype(bf16)
            in_send[p] = gin[rows_at(sc[4] ^ (2 * p + 1), size), :].astype(bf16)


def add(x, y):
    return x.astype(f32) + y.astype(f32)


def split_kernel(count, *refs):
    ins, outs = refs[1 : 1 + 2 * count], refs[1 + 2 * count :]
    p = pl.program_id(0)
    total = pl.num_programs(0)
    for n in range(count):
        value = add(ins[2 * n][...], ins[2 * n + 1][...]).astype(bf16)

        @pl.when(p < total // 2)
        def _():
            outs[2 * n][...] = value

        @pl.when(p >= total // 2)
        def _():
            outs[2 * n + 1][...] = value


def z_parts_kernel(sc, up, up_r, down, down_r, z_out):
    for r in range(4):
        z_out[r, :, :D] = add(up[r], up_r[r]).astype(bf16)
        z_out[r, :, D : 2 * D] = add(down[r], down_r[r]).astype(bf16)
    out = add(up[4], up_r[4])
    width = D // 4
    out = xor_columns([out[:, n * width : (n + 1) * width] for n in range(4)], sc[2])
    for r in range(4):
        z_out[r, :, 2 * D :] = out[:, r * width : (r + 1) * width].astype(bf16)


def in_parts_kernel(sc, kept, got, a_out, b_out):
    half = a_out.shape[0]
    first = sc[5]
    mine, other = rows_at(first, half), rows_at(1 - first, half)
    a_out[...] = add(kept[mine, :], got[mine, :]).astype(bf16)
    b_out[...] = add(kept[other, :], got[other, :]).astype(bf16)


def share_kernel(sc, z0, z1, z2, z3, in_a, in_b, h_own, h_got,
                 up_o, down_o, out_o, in_o, head_o, sq_o):
    rows = up_o.shape[0]
    total = add(z0[0], z1[...]) + add(z2[...], z3[...])
    up_o[...] = total[:, :D]
    down_o[...] = total[:, D : 2 * D]
    out_o[...] = dot(total[:, 2 * D :], eye(rows, rows), TN, HIGH)
    grad = add(in_a[...], in_b[...])
    in_o[...] = jnp.concatenate(
        [
            grad[:, part * NH * HD + h * HD : part * NH * HD + h * HD + HD]
            for h in range(NH)
            for part in range(3)
        ],
        axis=1,
    )
    head = ordered(sc[2] % 2 == 1, h_own[...], h_got[...])
    head_o[...] = head[:, :CLASSES]
    squares = jnp.sum(total * total, keepdims=True) + jnp.sum(grad * grad, keepdims=True)
    once = jnp.where(sc[2] == 0, 1.0, 0.0)
    squares += once * jnp.sum(head * head, keepdims=True)
    sq_o[...] = jnp.broadcast_to(squares, sq_o.shape)


def patch_parts_kernel(sc, kept, got, out, tile):
    tile[...] = add(kept[0], got[0])
    size = out.shape[1]
    for r in range(4):
        out[r] = tile[rows_at(sc[2] ^ r, size), :].astype(bf16)


def patch_sum_kernel(sc, own, q1, q2, q3, sq, extra_row, out):
    size = own.shape[1]
    total = add(own[0], q1[...]) + add(q2[...], q3[...])
    out[...] = jnp.zeros_like(out)
    out[:size, :] = total
    squares = jnp.sum(total * total, keepdims=True) + sq[0:1, 0:1]
    lane = lax.broadcasted_iota(jnp.int32, (1, D + SMALL), 1)
    out[size : size + 1, :] = jnp.where(lane == 0, squares, extra_row[0:1, :])


def tail_kernel(n_dp, sc, g_own, g_core, g_z, gmid, x0, gx, own, other, hot, small_b, qgrad,
                pk, ps, tile):
    grad = g_own[...].astype(f32) + g_core[0].astype(f32) + g_z[...].astype(f32)
    scaled, inv = norm_stats(x0[...])
    gain_a = jnp.sum(grad * scaled, axis=0, keepdims=True)
    ge = (gmid[...] + norm_back(grad * gx[0:1, :], scaled, inv)).astype(bf16)
    rows = jnp.where(sc[3] == 1, own[...], other[...])
    tile[:, :D] = dot(rows, ge, TN)
    row8 = lax.broadcasted_iota(jnp.int32, (8, D), 0)
    gains = jnp.where(row8 == 0, gain_a, small_b[...])
    small = dot(ge, hot[...], TN) + dot(gains, eye(8, SMALL, LANE_GAIN), TN)
    part = HD // n_dp
    kk = lax.broadcasted_iota(jnp.int32, (HD, D), 0)
    rr = lax.broadcasted_iota(jnp.int32, (HD, D), 1)
    spot = ((kk // part) * (D // n_dp) + kk % part == rr).astype(f32)
    lane = lax.broadcasted_iota(jnp.int32, (8, SMALL), 1)
    row = lax.broadcasted_iota(jnp.int32, (8, SMALL), 0)
    q_lane = ((lane == LANE_QG + row) & (row < 2)).astype(f32)
    q_cols = dot(qgrad[...], q_lane, TN, HIGH)
    small += dot(spot, q_cols, TN)
    tile[:, D:] = small
    for p, r in enumerate(rel_order(2)):
        pk[p] = tile[rows_at(sc[0] ^ r, SUB), :].astype(bf16)
        ps[p] = tile[rows_at(sc[0] ^ (r + 1), SUB), :].astype(bf16)


def update_kernel(stats, *rest):
    shares = rest[:6]
    state = rest[6:33]
    head_out, outs = rest[33], rest[34:]
    total = stats[0:1, :]
    norm = jnp.sqrt(total)
    head_out[...] = jnp.where(
        lax.broadcasted_iota(jnp.int32, (8, 128), 1) == 0, norm, total
    )
    factor = jnp.minimum(1.0, CLIP / (norm[:, 0:1] + 1e-06))
    s_in, s_out, s_up, s_down, s_patch, s_head = shares
    rows = s_patch.shape[0]
    small = dot(eye(SMALL, SMALL), s_patch[:, D:], NT, HIGH)
    part = state[24].shape[1]
    grads = [
        s_in[...],
        s_out[...],
        s_up[...],
        s_down[...],
        s_patch[:, :D],
        small[: 2 * GRID, :],
        s_head[...],
        small[LANE_GAIN : LANE_GAIN + 4, :],
        small[LANE_QG : LANE_QG + 2, :part],
    ]
    for n in range(9):
        master, first, second = state[3 * n : 3 * n + 3]
        clipped = grads[n] * factor
        first_new = BETA_ONE * first[...] + (1.0 - BETA_ONE) * clipped
        second_new = BETA_TWO * second[...] + (1.0 - BETA_TWO) * clipped * clipped
        matrix = n in (0, 1, 2, 3, 4, 6)
        rate = RATE_MATRIX if matrix else RATE_SMALL
        decay = DECAY if matrix else 0.0
        ratio = (
            first_new
            / (1.0 - BETA_ONE**STEP)
            / (jnp.sqrt(second_new / (1.0 - BETA_TWO**STEP)) + ADAM_EPS)
        )
        value = master[...]
        outs[3 * n][...] = value - rate * (ratio + decay * value)
        outs[3 * n + 1][...] = first_new
        outs[3 * n + 2][...] = second_new


ANY = pl.BlockSpec(memory_space=pl.ANY)


def without(kernel, count, deps):
    if not deps:
        return kernel
    return lambda *refs: kernel(*refs[:count], *refs[count + len(deps) :])


def call(kernel, grid, sc, ins, specs, outs, out_specs, scratch, us=5, deps=()):
    return pl.pallas_call(
        without(kernel, 1 + len(ins), deps),
        out_shape=outs,
        grid_spec=pltpu.PrefetchScalarGridSpec(
            num_scalar_prefetch=1,
            grid=grid,
            in_specs=list(specs) + [ANY] * len(deps),
            out_specs=out_specs,
            scratch_shapes=scratch,
        ),
        compiler_params=pltpu.CompilerParams(vmem_limit_bytes=VLIM),
        cost_estimate=pl.CostEstimate(
            flops=int(us * 1.15e9), bytes_accessed=1000000, transcendentals=0
        ),
    )(sc, *ins, *deps)


def flat_call(kernel, sc, ins, outs, scratch=(), us=3, deps=()):
    return call(
        kernel,
        (1,),
        sc,
        ins,
        [whole(x.shape) for x in ins],
        outs,
        tuple(whole(o.shape) for o in outs),
        list(scratch),
        us,
        deps,
    )


def simple_call(kernel, ins, outs, us=3, deps=()):
    return pl.pallas_call(
        without(kernel, len(ins), deps),
        out_shape=outs,
        in_specs=[pl.BlockSpec(memory_space=pltpu.VMEM)] * len(ins) + [ANY] * len(deps),
        compiler_params=pltpu.CompilerParams(vmem_limit_bytes=VLIM),
        cost_estimate=pl.CostEstimate(
            flops=int(us * 1.15e9), bytes_accessed=1000000, transcendentals=0
        ),
    )(*ins, *deps)


def whole(shape):
    return pl.BlockSpec(shape, lambda i, s: (0,) * len(shape))


def sds(shape, dtype):
    return jax.ShapeDtypeStruct(shape, dtype)


DMA = pltpu.SemaphoreType.DMA


def make_local(n_dp, n_mp):
    extra = n_dp // 8
    masks = [extra, 2 * extra, 4 * extra]
    low_bits = [b for b in (1, 2, 4, 8, 16, 32) if b < extra]
    col_low = [2 * b for b in low_bits]
    col_masks = [2 * extra, 4 * extra]

    def pp(x, dmask, zmask=0):
        perm = [
            (d * n_mp + z, (d ^ dmask) * n_mp + (z ^ zmask))
            for d in range(n_dp)
            for z in range(n_mp)
        ]
        return lax.ppermute(x, ("dp", "mp"), perm)

    def local(patches, segment, keep, pos_y, pos_x, labels, bucket, *state):
        masters = state[0::3]
        (attend_in, attend_out, expand, contract, patch_embed, pos_table, class_head,
         norm_gains, query_gains) = masters
        length = patches.shape[0]
        rows = patch_embed.shape[0]
        nq = length // BQ
        dp = lax.axis_index("dp")
        z = lax.axis_index("mp")
        core = dp % 2
        z1, z0 = z // 2, z % 2
        g = z0 + 2 * core
        me = dp // extra
        mecol = (dp // 2) // extra
        mine = core == z1

        def bit_of(mask):
            return (dp // mask) % 2 == 1

        def swap(flag, x, y, axis):
            return jnp.where(
                flag, jnp.concatenate([y, x], axis=axis), jnp.concatenate([x, y], axis=axis)
            )

        def pick4(parts, index, axis):
            odd, high = index % 2 == 1, index // 2 == 1
            lo = swap(odd, parts[0], parts[1], axis)
            hi = swap(odd, parts[2], parts[3], axis)
            return swap(high, lo, hi, axis)

        own_kept = (keep == 1) & (segment < IMG)
        own_valid = jnp.any(
            (segment[None, :] == jnp.arange(IMG)[:, None]) & own_kept[None, :], axis=1
        )
        lanes = jnp.arange(SMALL)
        cnt = jnp.where(lanes == bucket[0] + LANE_COUNT, jnp.sum(own_valid.astype(f32)), 0.0)
        cnt = jnp.pad(cnt[None, :], ((0, 7), (0, 0)))
        patch_w, in_w, z_w, out_w = simple_call(
            pack_kernel,
            [attend_in, attend_out, expand, contract.T, patch_embed, pos_table, norm_gains,
             query_gains, cnt],
            (
                sds((rows, D + SMALL), bf16),
                sds((rows, 576), bf16),
                sds((2, rows, D), bf16),
                sds((rows, 192), bf16),
            ),
        )

        perm_core = [
            (d * n_mp + zz, (d ^ 1) * n_mp + zz)
            for d in range(n_dp)
            for zz in range(n_mp)
            if d % 2 == zz // 2
        ]
        patches_in = lax.ppermute(patches, ("dp", "mp"), perm_core)
        meta = jnp.stack([segment, keep, pos_y, pos_x])
        tag = jnp.concatenate([labels, bucket, jnp.zeros((length - IMG - 1,), jnp.int32)])
        meta = jnp.concatenate([meta, tag[None]], axis=0)
        meta = jnp.where(mine, meta, lax.ppermute(meta, ("dp", "mp"), perm_core))

        def widen(x, low):
            for b in low:
                x = swap(bit_of(b), x, pp(x, b), -2)
            return x

        def direct8(x):
            chips = [x] + [pp(x, m) for m in (masks[1], masks[2], masks[1] | masks[2])]
            return chips + [pp(y, masks[0]) for y in chips]

        patch_p = direct8(widen(patch_w, low_bits))

        perm_a, perm_b, back_b = [], [], []
        for d in range(n_dp):
            for zz in range(n_mp):
                c, a1, a0 = d % 2, zz // 2, zz % 2
                src = d * n_mp + zz
                perm_a.append((src, (d - c + a1) * n_mp + a0 + 2 * c))
                perm_b.append((src, (d - c + a1) * n_mp + a0 + 2 * (1 - c)))
                back_b.append((src, (d - c + 1 - a1) * n_mp + a0 + 2 * c))
        in_a = lax.ppermute(in_w, ("dp", "mp"), perm_a)
        in_b = lax.ppermute(in_w, ("dp", "mp"), perm_b)
        in_own = widen(swap(z1 == 1, in_a, in_b, 0), col_low)
        in_p = [in_own] + [pp(in_own, m) for m in (col_masks[0], col_masks[1], col_masks[0] | col_masks[1])]
        out_z = [out_w, pp(out_w, 0, 1), pp(out_w, 0, 2), pp(out_w, 0, 3)]
        z_in = [pp(z_w, 0, r) for r in (1, 2, 3)]

        seg, kp, py, px = meta[0], meta[1], meta[2], meta[3]
        labs = meta[4, :IMG]
        buck = meta[4, IMG]
        kept = (kp == 1) & (seg < IMG)
        ids = jnp.arange(128)[None, :]
        ids64 = ids[:, :64]
        hot_pos = ((py[:, None] == ids) | (px[:, None] + GRID == ids)).astype(bf16)
        match = seg[:, None] == ids64
        qaux = jnp.where((ids64 < IMG) & match, BIG, jnp.where(ids64 == IMG, 1.0, 0.0)).astype(bf16)
        kaux = jnp.where(
            (ids64 < IMG) & match & kept[:, None],
            1.0,
            jnp.where(
                ids64 == IMG,
                -BIG,
                jnp.where(
                    (ids64 > IMG) & (ids64 < IMG + 4),
                    1.0,
                    jnp.where((ids64 == IMG + 4) & ~kept[:, None], 1.0, 0.0),
                ),
            ),
        ).astype(bf16)
        vaux = jnp.broadcast_to(jnp.where(jnp.arange(64) < 3, 1.0, 0.0).astype(bf16), (TOK, 64))
        first_seg, last_seg = seg[::BQ], jnp.minimum(seg[BQ - 1 :: BQ], IMG - 1)
        lo = jnp.sum((seg[None, :] < first_seg[:, None]).astype(jnp.int32), axis=1) // BQ
        hi = (jnp.sum((seg[None, :] <= last_seg[:, None]).astype(jnp.int32), axis=1) + BQ - 1) // BQ
        sc = jnp.concatenate(
            [
                jnp.stack([me, g, z, mine.astype(jnp.int32), mecol, z1, z1, z1]),
                lo,
                hi,
            ]
        ).astype(jnp.int32)
        own_seg = lax.dynamic_slice_in_dim(seg, g * TOK, TOK, 0)
        own_kp = lax.dynamic_slice_in_dim(kept, g * TOK, TOK, 0)
        mem = (
            (own_seg[:, None] == jnp.arange(IMG)[None, :]) & own_kp[:, None]
        ).astype(bf16)
        valid = jnp.max(
            ((seg[None, :] == jnp.arange(IMG)[:, None]) & kept[None, :]).astype(f32), axis=1
        )
        lab_hot = (labs[:, None] == jnp.arange(CPAD)[None, :]).astype(f32)
        block = jnp.arange(QK) // HD
        avg = jnp.where(block[:, None] == block[None, :], 1.0 / HD, 0.0).astype(bf16)
        heads = (jnp.arange(D)[:, None] // HD == ids).astype(bf16)

        nt = length // TOK
        f_w = flat_call(
            first_kernel,
            sc,
            [z_w] + out_z + [class_head],
            (sds((rows, 3 * D + CPAD), bf16),),
            us=2,
            deps=patch_p[1:4],
        )[0]
        f_p = direct8(widen(f_w, low_bits))
        a, x0, gx = call(
            x0_kernel,
            (nt,),
            sc,
            [patches, patches_in, hot_pos] + patch_p,
            [
                pl.BlockSpec((TOK, D), lambda i, s: (jnp.where(s[3] == 1, i, 0), 0)),
                pl.BlockSpec((TOK, D), lambda i, s: (jnp.where(s[3] == 1, 0, i), 0)),
                pl.BlockSpec((TOK, 128), lambda i, s: (i, 0)),
            ]
            + [ANY] * 8,
            (sds((length, D), bf16), sds((TOK, D), f32), sds((16, D), f32)),
            (pl.BlockSpec((TOK, D), lambda i, s: (i, 0)), whole((TOK, D)), whole((16, D))),
            [pltpu.VMEM((D, D + SMALL), bf16), DMA((8,))],
            10,
            deps=[f_w],
        )
        g_w = simple_call(
            second_kernel, z_in, sds((6, rows, D), bf16), 2, deps=[a]
        )
        g_p = direct8(widen(g_w, low_bits))
        qcols = query_gains.shape[1]
        counts = jnp.sum(gx[LANE_COUNT - LANE_GAIN : LANE_COUNT - LANE_GAIN + NB], axis=1)
        image_total = jnp.sum(counts)
        qg = gx[4:6].reshape(2, n_dp, rows)[:, :, :qcols].reshape(2, 1, HD)
        gain = jnp.tile(qg * jnp.array([0.125, 1.0], f32)[:, None, None], (1, NH, 1))
        gain = jnp.pad(gain.reshape(1, QK), ((0, 7), (0, 0)))
        vt = jnp.stack([valid, valid / image_total], axis=1)
        vt = jnp.pad(vt, ((0, 0), (0, 126)))

        row_block = lambda width: pl.BlockSpec((TOK, width), lambda i, s: (i, 0))
        head_block = pl.BlockSpec((NH, TOK, 128), lambda i, s: (0, i, 0))
        qx, kx, vx, xh, inv = call(
            qkv_kernel,
            (nt,),
            sc,
            [a, qaux, kaux, vaux, gain, avg] + in_p,
            [row_block(D), row_block(64), row_block(64), whole((TOK, 64)), whole((8, QK)),
             whole((QK, QK))]
            + [ANY] * 4,
            tuple([sds((NH, length, 128), bf16)] * 3 + [sds((length, QK), f32)] * 2),
            tuple([head_block] * 3 + [row_block(QK)] * 2),
            [pltpu.VMEM((D, 576), bf16), DMA((4,))],
            10,
            deps=[g_w],
        )
        per_tok = TOK // BQ
        o_rel, o_full, ql = call(
            attn_kernel,
            (nq,),
            sc,
            [qx, kx, vx],
            [
                pl.BlockSpec((NH, BQ, 128), lambda i, s: (0, i, 0)),
                whole((NH, length, 128)),
                whole((NH, length, 128)),
            ],
            (
                sds((4, TOK, NH * HD), bf16),
                sds((length, NH * HD), f32),
                sds((NH, length, 128), bf16),
            ),
            (
                pl.BlockSpec(
                    (1, BQ, NH * HD), lambda i, s: (s[1] ^ (i // per_tok), i % per_tok, 0)
                ),
                pl.BlockSpec((BQ, NH * HD), lambda i, s: (i, 0)),
                pl.BlockSpec((NH, BQ, 128), lambda i, s: (0, i, 0)),
            ),
            [pltpu.VMEM((NH, BQ, 128), f32)],
            20,
        )

        def trade(parts):
            return [parts[0], pp(parts[1], 0, 1), pp(parts[2], 1, 0), pp(parts[3], 1, 1)]

        o_cat = pick4(trade([o_rel[r] for r in range(4)]), g, 1)
        tile_spec = pl.BlockSpec((TOK, D), lambda j, s: (0, j))
        x1, b, u_a, h_a, acc = call(
            mlp_one_kernel,
            (1,),
            sc,
            [o_cat, x0, gx] + f_p,
            [whole((TOK, D)), whole((TOK, D)), whole((16, D))] + [ANY] * 8,
            (
                sds((TOK, D), f32),
                sds((TOK, D), bf16),
                sds((TOK, D), f32),
                sds((TOK, D), bf16),
                sds((TOK, D), f32),
            ),
            tuple([whole((TOK, D))] * 5),
            [pltpu.VMEM((D, D), bf16), pltpu.VMEM((2, D, D), bf16), DMA((8,)), DMA((2, 8))],
            10,
        )
        u_b, h_b, x2, ns = call(
            mlp_two_kernel,
            (3,),
            sc,
            [b, acc, gx, mem, heads] + g_p,
            [whole((TOK, D)), whole((TOK, D)), whole((16, D)), whole((TOK, IMG)), whole((D, 128))]
            + [ANY] * 8,
            (
                sds((TOK, 3 * D), f32),
                sds((TOK, 3 * D), bf16),
                sds((TOK, D), f32),
                sds((IMG, D + 128), f32),
            ),
            (tile_spec, tile_spec, whole((TOK, D)), whole((IMG, D + 128))),
            [pltpu.VMEM((3, 2, D, D), bf16), DMA((3, 2, 8))],
            13,
        )
        ns = ns + pp(ns, 1, 0)
        half_shape = (4, SUB, CPAD // 2)
        pooled, gp, sinv, loss, gh, gh_send = call(
            head_kernel,
            (1,),
            sc,
            [ns, pp(ns, 0, 1), lab_hot, vt, heads] + f_p,
            [whole((IMG, D + 128))] * 2
            + [whole((IMG, CPAD)), whole((IMG, 128)), whole((D, 128))]
            + [ANY] * 8,
            (
                sds((IMG, D), f32),
                sds((IMG, D), f32),
                sds((IMG, 128), f32),
                sds((IMG, 128), f32),
                sds(half_shape, bf16),
                sds(half_shape, bf16),
            ),
            (
                whole((IMG, D)),
                whole((IMG, D)),
                whole((IMG, 128)),
                whole((IMG, 128)),
                whole(half_shape),
                whole(half_shape),
            ),
            [pltpu.VMEM((D, CPAD), bf16), pltpu.VMEM((D, CPAD // 2), f32), DMA((8,))],
            5,
        )

        low_spec = whole((TOK, D))
        high_spec = pl.BlockSpec((TOK, D), lambda j, s: (0, jnp.clip(j - 1, 0, 2)))
        gu, gr, gm, gmid, ga, small_b = call(
            back_kernel,
            (4,),
            sc,
            [u_a, u_b, x2, x1, gx, mem, pooled, gp, sinv, heads]
            + f_p + g_p,
            [
                low_spec,
                high_spec,
                whole((TOK, D)),
                whole((TOK, D)),
                whole((16, D)),
                whole((TOK, IMG)),
                whole((IMG, D)),
                whole((IMG, D)),
                whole((IMG, 128)),
                whole((D, 128)),
            ]
            + [ANY] * 16,
            (
                sds((TOK, HID), bf16),
                sds((TOK, D), bf16),
                sds((TOK, D), bf16),
                sds((TOK, D), f32),
                sds((TOK, D), bf16),
                sds((8, D), f32),
            ),
            (
                tile_spec,
                whole((TOK, D)),
                whole((TOK, D)),
                whole((TOK, D)),
                whole((TOK, D)),
                whole((8, D)),
            ),
            [
                pltpu.VMEM((4, 2, D, D), bf16),
                pltpu.VMEM((D, D), bf16),
                pltpu.VMEM((TOK, D), f32),
                pltpu.VMEM((TOK, D), f32),
                DMA((4, 2, 8)),
                DMA((8,)),
            ],
            20,
        )
        ga4 = [ga[:, n * NH * HD : (n + 1) * NH * HD][None] for n in range(4)]
        ga_rel = pick4(ga4, g, 0)
        do = pick4([t[None] for t in trade([ga_rel[r] for r in range(4)])], g, 0)

        up_block = pl.BlockSpec((4, 1, SUB, D), lambda j, s: (0, j, 0, 0))
        down_block = pl.BlockSpec((4, 1, SUB, D), lambda j, s: (0, jnp.minimum(j, 3), 0, 0))
        ek, es, ck, cs = call(
            wgrad_kernel,
            (5,),
            sc,
            [gr, h_a, h_b, b, gu, gm, o_cat],
            [
                whole((TOK, D)),
                low_spec,
                high_spec,
                whole((TOK, D)),
                pl.BlockSpec((TOK, D), lambda j, s: (0, jnp.minimum(j, 3))),
                whole((TOK, D)),
                whole((TOK, D)),
            ],
            tuple([sds((4, 5, SUB, D), bf16)] * 2 + [sds((4, 4, SUB, D), bf16)] * 2),
            (up_block, up_block, down_block, down_block),
            [pltpu.VMEM((D, D), f32)],
            14,
        )

        def low_rows(x, low):
            for b in reversed(low):
                half = x.shape[-2] // 2
                first, second = x[..., :half, :], x[..., half:, :]
                flag = bit_of(b)
                send = jnp.where(flag, first, second)
                stay = jnp.where(flag, second, first)
                x = add(stay, pp(send.astype(bf16), b))
            return x

        def scatter4(stay, low, m1, m2):
            x = add(stay[:2], pp(stay[2:].astype(bf16), m1))
            x = add(x[0].astype(bf16), pp(x[1].astype(bf16), m2))
            return low_rows(x, low)

        def core_sum(stay, send):
            return add(stay, pp(send, masks[0])).astype(bf16)

        def chip_sum(x, first):
            m1, m2 = (masks[1], masks[2]) if first == 2 else (masks[2], masks[1])
            return scatter4(x, low_bits, m1, m2)

        if extra == 1:
            gh = chip_sum(gh, 2)
        else:
            gh = 0.5 * chip_sum(core_sum(gh, gh_send), 2)
        gh = add(gh.astype(bf16), pp(gh.astype(bf16), 0, 2))

        def halves(pairs, us, deps=()):
            count = pairs[0][0].shape[0]
            half = count // 2
            ins, specs, outs, out_specs = [], [], [], []
            for kept, got in pairs:
                shape = kept.shape[1:]
                block = (1,) + shape
                tail = (0,) * len(shape)
                ins += [kept, got]
                specs += [pl.BlockSpec(block, lambda p, s, tail=tail: (p,) + tail)] * 2
                outs += [sds((half,) + shape, bf16)] * 2
                out_specs += [
                    pl.BlockSpec(block, lambda p, s, tail=tail: (jnp.minimum(p, half - 1),) + tail),
                    pl.BlockSpec(block, lambda p, s, tail=tail: (jnp.maximum(p - half, 0),) + tail),
                ]
            n = len(pairs)
            out = call(
                lambda *refs: split_kernel(n, *refs), (count,), sc, ins, specs, tuple(outs),
                tuple(out_specs), [], us, deps,
            )
            return [(out[2 * i], out[2 * i + 1]) for i in range(n)]

        (uk, us_), (vk, vs) = halves([(ek, pp(es, masks[0])), (ck, pp(cs, masks[0]))], 5)
        us_got, vs_got = pp(us_, masks[1]), pp(vs, masks[2])

        last = nq - 1
        grads = call(
            attn_back_kernel,
            (nq + nt,),
            sc,
            [ql, o_full, do, kx, vx],
            [
                pl.BlockSpec((NH, BQ, 128), lambda i, s: (0, jnp.minimum(i, last), 0)),
                pl.BlockSpec((BQ, NH * HD), lambda i, s: (jnp.minimum(i, last), 0)),
                pl.BlockSpec(
                    (1, BQ, NH * HD),
                    lambda i, s: (
                        jnp.minimum(i, last) // per_tok,
                        jnp.minimum(i, last) % per_tok,
                        0,
                    ),
                ),
                whole((NH, length, 128)),
                whole((NH, length, 128)),
            ],
            (sds((length, 576), f32),),
            (pl.BlockSpec((TOK, 576), lambda i, s: (jnp.maximum(i - nq, 0), 0)),),
            [
                pltpu.VMEM((NH, length, 128), f32),
                pltpu.VMEM((NH, length, 128), f32),
                pltpu.VMEM((NH, length, 128), f32),
            ],
            35,
            deps=[us_, vs],
        )[0]
        (uk2, us2), (vk2, vs2) = halves([(uk, us_got), (vk, vs_got)], 4, deps=[grads])
        us2_got, vs2_got = pp(us2, masks[2]), pp(vs2, masks[1])
        rel_tok = lambda n, s: s[1] ^ jnp.where(n < 2, n + 2, 3 - n)
        tok_block = lambda width: pl.BlockSpec((TOK, width), lambda n, s: (rel_tok(n, s), 0))
        in_shape = (2, D // 4, 576)
        g_send, g_one, g_own, in_keep, in_send, qgrad = call(
            mix_kernel,
            (nt,),
            sc,
            [grads, xh, inv, a, gain, avg] + in_p,
            [tok_block(576), tok_block(QK), tok_block(QK), tok_block(D), whole((8, QK)),
             whole((QK, QK))]
            + [ANY] * 4,
            (
                sds((2, TOK, D), bf16),
                sds((TOK, D), bf16),
                sds((TOK, D), bf16),
                sds(in_shape, bf16),
                sds(in_shape, bf16),
                sds((8, QK), f32),
            ),
            (
                pl.BlockSpec((1, TOK, D), lambda n, s: (jnp.minimum(n, 1), 0, 0)),
                whole((TOK, D)),
                whole((TOK, D)),
                whole(in_shape),
                whole(in_shape),
                whole((8, QK)),
            ),
            [pltpu.VMEM((D, 576), f32), pltpu.VMEM((D, 576), bf16), DMA((4,))],
            14,
            deps=[us2, vs2],
        )
        g_core = pp(g_send, 1)
        g_z = pp(add(g_one, g_core[1]).astype(bf16), 0, 1)

        in_got = pp(in_send, col_masks[0])
        if extra == 1:
            z_ins = [uk2[0], us2_got[0], vk2[0], vs2_got[0]]
        else:
            up = low_rows(add(uk2[0], us2_got[0]), low_bits).astype(bf16)
            down = low_rows(add(vk2[0], vs2_got[0]), low_bits).astype(bf16)
            z_ins = [up, jnp.zeros_like(up), down, jnp.zeros_like(down)]
        z_out = flat_call(
            z_parts_kernel, sc, z_ins, (sds((4, rows, 2 * D + 192), bf16),), us=4, deps=[g_core]
        )[0]
        z_got = [pp(z_out[r], 0, r) for r in (1, 2, 3)]
        (ik, is_), = halves([(in_keep, in_got)], 2, deps=[z_out])
        is_got = pp(is_, col_masks[1])

        qg_rows = qgrad[0].reshape(2, NH, HD).sum(axis=1) * jnp.array([0.125, 1.0], f32)[:, None]
        qg_rows = jnp.pad(qg_rows, ((0, 6), (0, 0)))
        hot_own = pl.BlockSpec((TOK, 128), lambda i, s: (s[1], 0))
        own_rows = pl.BlockSpec((TOK, D), lambda i, s: (s[1], 0))

        def tail_body(*refs):
            tail_kernel(n_dp, *refs)

        pk, ps = call(
            tail_body,
            (1,),
            sc,
            [g_own, g_core, g_z, gmid, x0, gx, patches, patches_in, hot_pos, small_b, qg_rows],
            [
                whole((TOK, D)),
                pl.BlockSpec((1, TOK, D), lambda i, s: (0, 0, 0)),
                whole((TOK, D)),
                whole((TOK, D)),
                whole((TOK, D)),
                whole((16, D)),
                own_rows,
                own_rows,
                hot_own,
                whole((8, D)),
                whole((8, HD)),
            ],
            (sds((4, SUB, D + SMALL), bf16), sds((4, SUB, D + SMALL), bf16)),
            (whole((4, SUB, D + SMALL)), whole((4, SUB, D + SMALL))),
            [pltpu.VMEM((D, D + SMALL), f32)],
            6,
            deps=[is_],
        )
        (pk1, ps1), = halves([(pk, pp(ps, masks[0]))], 2)
        ps1_got = pp(ps1, masks[1])
        if extra == 1:
            in_a, in_b = flat_call(
                in_parts_kernel, sc, [ik[0], is_got[0]], (sds((rows, 576), bf16),) * 2, us=2,
                deps=[ps1],
            )
        else:
            both = low_rows(add(ik[0], is_got[0]), col_low).astype(bf16).reshape(2, rows, 576)
            in_a = jnp.where(z1 == 1, both[1], both[0])
            in_b = jnp.where(z1 == 1, both[0], both[1])
        in_a = lax.ppermute(in_a, ("dp", "mp"), perm_a)
        in_b = lax.ppermute(in_b, ("dp", "mp"), back_b)
        (pk2, ps2), = halves([(pk1, ps1_got)], 2)
        ps2_got = pp(ps2, masks[2])
        s_up, s_down, s_out, s_in, s_head, sq = flat_call(
            share_kernel,
            sc,
            [z_out] + z_got + [in_a, in_b, gh, pp(gh, 0, 1)],
            (
                sds((rows, D), f32),
                sds((rows, D), f32),
                sds((192, rows), f32),
                sds((rows, 576), f32),
                sds((rows, CLASSES), f32),
                sds((8, 128), f32),
            ),
            us=4,
            deps=[ps2],
        )
        quarter = rows // 4
        if rows % 32 == 0:
            rel = flat_call(
                patch_parts_kernel, sc, [pk2, ps2_got], (sds((4, quarter, D + SMALL), bf16),),
                [pltpu.VMEM((rows, D + SMALL), f32)], 2, deps=[sq],
            )[0]
        else:
            rel = low_rows(add(pk2[0], ps2_got[0]), low_bits).astype(bf16)
            rel = rel.reshape(4, quarter, D + SMALL)
            rel = pick4([rel[n : n + 1] for n in range(4)], z, 0)
        q_got = [pp(rel[r], 0, r) for r in (1, 2, 3)]

        wide = jnp.arange(D + SMALL)
        extra_row = jnp.where((wide == buck + 1) & (g == 0), jnp.sum(loss[:, 0]), 0.0)
        extra_row = jnp.broadcast_to(extra_row[None, :], (8, D + SMALL))
        mine_q = flat_call(
            patch_sum_kernel, sc, [rel] + q_got + [sq, extra_row],
            (sds((quarter + 8, D + SMALL), f32),), us=2,
        )[0]
        around = [mine_q, pp(mine_q, 0, 1), pp(mine_q, 0, 2), pp(mine_q, 0, 3)]
        stats = [q[quarter : quarter + 1, :SMALL] for q in around]
        stats = (stats[0] + stats[1]) + (stats[2] + stats[3])
        stats = jnp.broadcast_to(stats, (8, SMALL))
        stats = stats + pp(stats, 1)
        m = 2
        while m < n_dp:
            stats = (stats + pp(stats, m)) + (pp(stats, 2 * m) + pp(stats, 3 * m))
            m *= 4
        share_patch = pick4([q[:quarter] for q in around], z, 0)

        shares = [s_in, s_out, s_up, s_down, share_patch, s_head]
        turned = [x.T if n // 3 == 3 else x for n, x in enumerate(state)]
        news = simple_call(
            update_kernel,
            [stats] + shares + turned,
            tuple([sds((8, 128), f32)] + [sds(s.shape, f32) for s in turned]),
            6,
        )
        top = news[0]
        outs = [x.T if n // 3 == 3 else x for n, x in enumerate(news[1:])]
        return (top[0, 1 : 1 + NB], counts, top[0, 0]) + tuple(outs)

    return local


def solution(mesh):
    shard = {
        "in": P("dp", "mp"),
        "out": P("mp", "dp"),
        "row": P("dp", None),
        "col": P(None, "dp"),
    }
    kinds = ["in", "out", "in", "out", "row", "col", "row", "col", "col"]
    triples = tuple(shard[k] for k in kinds for _ in range(3))
    in_specs = (P("dp", None),) + (P("dp"),) * 6 + triples
    out_specs = (P(), P(), P()) + triples
    return jax.shard_map(
        make_local(mesh.shape["dp"], mesh.shape["mp"]),
        mesh=mesh,
        in_specs=in_specs,
        out_specs=out_specs,
        check_vma=False,
    )
```

time: 605 us -> 483 us (0.80); the launches traced: 610 us -> 480 us
  local copies, waits for them, and re-layouts: 67.1 us -> 26.7 us
  starting transfers between devices: 120 us -> 84.7 us
  other arithmetic: 59 us -> 24.9 us
  Pallas kernels: 236 us -> 221 us
  between operations: 10.7 us -> 3.34 us
    ppermute x110 -> x68, starting transfers between devices: 108 us -> 71 us  [pp(): return lax.ppermute(x, ('dp', 'mp'), perm)]
    pallas_call x11 -> x25, Pallas kernels: 236 us -> 221 us  [the longest x22 209 us: call(): pl.pallas_call(without(kernel, 1 + len(ins), deps), out_shape=outs, grid_...]
    ppermute x7 -> x0, local copies, waits for them, and re-layouts: 12.2 us -> none  [pp(): return lax.ppermute(x, ('dp', 'mp'), perm)]
    sub x9 -> x0, other arithmetic: 8.69 us -> none  [local(): masters[index] - rate * (ratio + decay * masters[index])]
    another operation x21 -> x1, other arithmetic: 8.09 us -> 0.05 us
    slice x18 -> x7, local copies, waits for them, and re-layouts: 10.3 us -> 3.6 us  [the longest x1 1.19 us: local(): return (top[0, 1:1 + NB], counts, top[0, 0]) + tuple(outs)]
    unnamed x227 -> x140, local copies, waits for them, and re-layouts: 18.2 us -> 12.8 us
    convert_element_type x15 -> x8, other arithmetic: 15.4 us -> 10.2 us  [the longest x1 2.55 us: local(): kaux = jnp.where((ids64 < IMG) & match & kept[:, None], 1.0, jnp.where(id...]
  transfers between devices with their start and end apart: 116 -> 74, of which waited for: 36 -> 28; matrix products, arithmetic and copies ran while one was open for 15% -> 6% of each run, Pallas kernels for 33% -> 24%
where the time goes in v2:
time: 483 us; the launch traced here: 480 us
  Pallas kernels  221 us (46%)
  waiting for transfers between devices  120 us (25%)
  starting transfers between devices  84.7 us (18%)
  local copies, waits for them, and re-layouts  26.7 us (6%)
  other arithmetic  24.9 us (5%)
    pallas_call x22, Pallas kernels, call(): pl.pallas_call(without(kernel, 1 + len(ins), deps), out_shape=outs, grid_...  209 us
    ppermute x68, waiting for transfers between devices, pp(): return lax.ppermute(x, ('dp', 'mp'), perm)  117 us
    ppermute x68, starting transfers between devices, pp(): return lax.ppermute(x, ('dp', 'mp'), perm)  71 us
    unnamed x140, local copies, waits for them, and re-layouts  12.8 us
    pallas_call x3, Pallas kernels, simple_call(): pl.pallas_call(without(kernel, len(ins), deps), out_shape=outs, in_specs=...  11.2 us
  transfers between devices with their start and end apart: 74, of which 28 were waited for; matrix products, arithmetic and copies ran while one was open for 6% of the time, Pallas kernels for 24%

profile of v2, /device:TPU:0, one launch (start us, length us, event | category | flops | bytes accessed | tf_op | source)
XLA Modules:
  0.0 479.7 jit_solution(16545827218880948772)
XLA Ops:
  4.8 2.5 shard_map.571
  7.2 5.1 %collective-permute-start.11 = (bf16[96,192]{1,0:T(8,128)(2,1)}, bf16[96,192]{1,0:T(8,128)(2,1)S(1)}, u32[]{:S(2)}, u32[]{:S(2)}) collective-permute-start(bf16[96,192]{1,0:T(8,128)(2,1)} %get-tuple-element.129.refs_2_), channel_id=1, source_target_pairs={{0,3},{1,2},{2,1},{3,0},{4,7},{5,6},{6,5},{7,4},{8,11},{9,10},{10,... | collective-permute-start | bytes 110600 | tf_op jit(solution)/shard_map/ppermute | solution.py:805
  13.9 3.3 collective-permute-start.12
  21.2 3.0 collective-permute-start.1
  28.1 2.5 select_convert_fusion.refs_3_
  30.7 2.5 collective-permute-start.4
  35.1 4.0 collective-permute-done.9.refs_3_
  40.4 2.9 shard_map.572.refs_12_.rest_0_
  50.8 10.7 %shard_map.573 = (bf16[2048,768]{1,0:T(8,128)(2,1)}, f32[512,768]{1,0:T(8,128)}, f32[16,768]{1,0:T(8,128)}) custom-call(s32[24]{0:T(128)} %concatenate.89.refs_0_.sc, bf16[2048,768]{1,0:T(8,128)(2,1)} %refs_7_.1, bf16[2048,768]{1,0:T(8,128)(2,1)} %collective-permute-done.1.refs_2_.refs_8_, bf16[2048,128]{1,0:T(8,128)(2,1)} %fusion.2.refs_3_.refs_9_, ...), custom_call_target="tpu_custom_call" | custom-call | flops 11500000256 | bytes 1000000 | tf_op jit(solution)/shard_map/pallas_call | solution.py:737
  64.0 8.1 %collective-permute-done.18.refs_1_ = bf16[2,96,768]{2,1,0:T(8,128)(2,1)S(1)} collective-permute-done((bf16[2,96,768]{2,1,0:T(8,128)(2,1)S(1)}, bf16[2,96,768]{2,1,0:T(8,128)(2,1)S(1)}, u32[]{:S(2)}, u32[]{:S(2)}) %collective-permute-start.18) | collective-permute-done | bytes 294944 | tf_op jit(solution)/shard_map/ppermute | solution.py:805
  80.5 13.2 %shard_map.575 = (bf16[3,2048,128]{2,1,0:T(8,128)(2,1)}, bf16[3,2048,128]{2,1,0:T(8,128)(2,1)}, bf16[3,2048,128]{2,1,0:T(8,128)(2,1)}, f32[2048,384]{1,0:T(8,128)}, f32[2048,384]{1,0:T(8,128)}) custom-call(s32[24]{0:T(128)} %concatenate.89.refs_0_.sc, bf16[2048,768]{1,0:T(8,128)(2,1)} %get-tuple-element.130.refs_3_.refs_1_.refs_4_, ...), custom_call_target="tpu_custom_call" | custom-call | flops 11500000256 | bytes 1000000 | tf_op jit(solution)/shard_map/pallas_call | solution.py:737
  93.7 21.5 %shard_map.576 = (bf16[4,512,192]{2,1,0:T(8,128)(2,1)}, f32[2048,192]{1,0:T(8,128)}, bf16[3,2048,128]{2,1,0:T(8,128)(2,1)}) custom-call(s32[24]{0:T(128)} %concatenate.89.refs_0_.sc, bf16[3,2048,128]{2,1,0:T(8,128)(2,1)} %get-tuple-element.133.qx, bf16[3,2048,128]{2,1,0:T(8,128)(2,1)} %get-tuple-element.134.kx.refs_4_, ...), custom_call_target="tpu_custom_call" | custom-call | flops 23000000512 | bytes 1000000 | tf_op jit(solution)/shard_map/pallas_call | solution.py:737
  125.5 5.3 %collective-permute-done.22 = bf16[512,192]{1,0:T(8,128)(2,1)S(1)} collective-permute-done((bf16[512,192]{1,0:T(8,128)(2,1)S(1)}, bf16[512,192]{1,0:T(8,128)(2,1)S(1)}, u32[]{:S(2)}, u32[]{:S(2)}) %collective-permute-start.22) | collective-permute-done | bytes 196640 | tf_op jit(solution)/shard_map/ppermute | solution.py:805
  136.2 4.8 %collective-permute-done.32.rest_3_.rest_11_ = bf16[6,96,768]{2,1,0:T(8,128)(2,1)S(1)} collective-permute-done((bf16[6,96,768]{2,1,0:T(8,128)(2,1)S(1)}, bf16[6,96,768]{2,1,0:T(8,128)(2,1)S(1)}, u32[]{:S(2)}, u32[]{:S(2)}) %collective-permute-start.32) | collective-permute-done | bytes 884768 | tf_op jit(solution)/shard_map/ppermute | solution.py:805
  141.0 17.2 %collective-permute-done.31.rest_2_.rest_10_ = bf16[6,96,768]{2,1,0:T(8,128)(2,1)S(1)} collective-permute-done((bf16[6,96,768]{2,1,0:T(8,128)(2,1)S(1)}, bf16[6,96,768]{2,1,0:T(8,128)(2,1)S(1)}, u32[]{:S(2)}, u32[]{:S(2)}) %collective-permute-start.31) | collective-permute-done | bytes 884768 | tf_op jit(solution)/shard_map/ppermute | solution.py:805
  158.7 9.2 %shard_map.577 = (f32[512,768]{1,0:T(8,128)}, bf16[512,768]{1,0:T(8,128)(2,1)}, f32[512,768]{1,0:T(8,128)}, bf16[512,768]{1,0:T(8,128)(2,1)}, f32[512,768]{1,0:T(8,128)}) custom-call(s32[24]{0:T(128)} %concatenate.89.refs_0_.sc, bf16[512,768]{1,0:T(8,128)(2,1)} %maximum_select_fusion.2.o, f32[512,768]{1,0:T(8,128)} %get-tuple-element.139.x0.refs_5_, ...), custom_call_target="tpu_custom_call" | custom-call | flops 11500000256 | bytes 1000000 | tf_op jit(solution)/shard_map/pallas_call | solution.py:737
  169.8 14.4 %shard_map.578 = (f32[512,2304]{1,0:T(8,128)}, bf16[512,2304]{1,0:T(8,128)(2,1)}, f32[512,768]{1,0:T(8,128)}, f32[16,896]{1,0:T(8,128)}) custom-call(s32[24]{0:T(128)} %concatenate.89.refs_0_.sc, bf16[512,768]{1,0:T(8,128)(2,1)} %get-tuple-element.141.b, f32[512,768]{1,0:T(8,128)} %get-tuple-element.142.acc_in, f32[16,768]{1,0:T(8,128)} %get-tuple-element.131.gx.refs_6_, ...), custom_call_target="tpu_custom_call" | custom-call | flops 14949999616 | bytes 1000000 | tf_op jit(solution)/shard_map/pallas_call | solution.py:737
  191.6 5.2 %shard_map.579 = (f32[16,768]{1,0:T(8,128)}, f32[16,768]{1,0:T(8,128)}, f32[16,128]{1,0:T(8,128)}, f32[16,128]{1,0:T(8,128)}, bf16[4,96,512]{2,1,0:T(8,128)(2,1)}, /*index=5*/bf16[4,96,512]{2,1,0:T(8,128)(2,1)}) custom-call(s32[24]{0:T(128)} %concatenate.89.refs_0_.sc, f32[16,896]{1,0:T(8,128)} %copy-done.8, f32[16,896]{1,0:T(8,128)} %copy-done.62, ...), custom_call_target="tpu_custom_call" | custom-call | flops 5750000128 | bytes 1000000 | tf_op jit(solution)/shard_map/pallas_call | solution.py:737
  196.7 20.8 %shard_map.580 = (bf16[512,3072]{1,0:T(8,128)(2,1)}, bf16[512,768]{1,0:T(8,128)(2,1)}, bf16[512,768]{1,0:T(8,128)(2,1)}, f32[512,768]{1,0:T(8,128)}, bf16[512,768]{1,0:T(8,128)(2,1)}, /*index=5*/f32[8,768]{1,0:T(8,128)}) custom-call(s32[24]{0:T(128)} %concatenate.89.refs_0_.sc, f32[512,768]{1,0:T(8,128)} %get-tuple-element.140.u_a, ...), custom_call_target="tpu_custom_call" | custom-call | flops 23000000512 | bytes 1000000 | tf_op jit(solution)/shard_map/pallas_call | solution.py:737
  217.6 13.4 %shard_map.581 = (bf16[4,5,96,768]{3,2,1,0:T(8,128)(2,1)}, bf16[4,5,96,768]{3,2,1,0:T(8,128)(2,1)}, bf16[4,4,96,768]{3,2,1,0:T(8,128)(2,1)}, bf16[4,4,96,768]{3,2,1,0:T(8,128)(2,1)}) custom-call(s32[24]{0:T(128)} %concatenate.89.refs_0_.sc, bf16[512,768]{1,0:T(8,128)(2,1)} %get-tuple-element.151.gr, bf16[512,768]{1,0:T(8,128)(2,1)} %get-tuple-element.152.h_a, ...), custom_call_target="tpu_custom_call" | custom-call | flops 16099999744 | bytes 1000000 | tf_op jit(solution)/shard_map/pallas_call | solution.py:737
  234.8 7.0 %collective-permute-done.41 = bf16[512,192]{1,0:T(8,128)(2,1)S(1)} collective-permute-done((bf16[512,192]{1,0:T(8,128)(2,1)S(1)}, bf16[512,192]{1,0:T(8,128)(2,1)S(1)}, u32[]{:S(2)}, u32[]{:S(2)}) %collective-permute-start.41) | collective-permute-done | bytes 196640 | tf_op jit(solution)/shard_map/ppermute | solution.py:805
  242.0 4.1 collective-permute-done.39
  250.0 8.3 %shard_map.582 = (bf16[2,5,96,768]{3,2,1,0:T(8,128)(2,1)}, bf16[2,5,96,768]{3,2,1,0:T(8,128)(2,1)}, bf16[2,4,96,768]{3,2,1,0:T(8,128)(2,1)}, bf16[2,4,96,768]{3,2,1,0:T(8,128)(2,1)}) custom-call(s32[24]{0:T(128)} %concatenate.89.refs_0_.sc, bf16[4,5,96,768]{3,2,1,0:T(8,128)(2,1)} %get-tuple-element.156.refs_1_, bf16[4,5,96,768]{3,2,1,0:T(8,128)(2,1)} %copy-done.16, ...), custom_call_target="tpu_custom_call" | custom-call | flops 5750000128 | bytes 1000000 | tf_op jit(solution)/shard_map/pallas_call | solution.py:737
  260.0 35.0 %shard_map.583.refs_5_.refs_1_ = f32[2048,576]{1,0:T(8,128)} custom-call(s32[24]{0:T(128)} %concatenate.89.refs_0_.sc, bf16[3,2048,128]{2,1,0:T(8,128)(2,1)} %get-tuple-element.136.refs_1_, f32[2048,192]{1,0:T(8,128)} %get-tuple-element.137.refs_2_, bf16[4,512,192]{2,1,0:T(8,128)(2,1)} %maximum_select_fusion.1.refs_3_, ...), custom_call_target="tpu_custom_call" | custom-call | flops 40249999360 | bytes 1000000 | tf_op jit(solution)/shard_map/pallas_call | solution.py:737
  296.5 5.4 %shard_map.584 = (bf16[1,5,96,768]{3,2,1,0:T(8,128)(2,1)}, bf16[1,5,96,768]{3,2,1,0:T(8,128)(2,1)}, bf16[1,4,96,768]{3,2,1,0:T(8,128)(2,1)}, bf16[1,4,96,768]{3,2,1,0:T(8,128)(2,1)}) custom-call(s32[24]{0:T(128)} %concatenate.89.refs_0_.sc, bf16[2,5,96,768]{3,2,1,0:T(8,128)(2,1)} %get-tuple-element.164.refs_1_, bf16[2,5,96,768]{3,2,1,0:T(8,128)(2,1)} %copy-done.18, ...), custom_call_target="tpu_custom_call" | custom-call | flops 4600000000 | bytes 1000000 | tf_op jit(solution)/shard_map/pallas_call | solution.py:737
  301.9 16.6 %shard_map.585 = (bf16[2,512,768]{2,1,0:T(8,128)(2,1)}, bf16[512,768]{1,0:T(8,128)(2,1)}, bf16[512,768]{1,0:T(8,128)(2,1)}, bf16[2,192,576]{2,1,0:T(8,128)(2,1)}...) custom-call(s32[24]{0:T(128)} %concatenate.89.refs_0_.sc, f32[2048,576]{1,0:T(8,128)} %shard_map.583.refs_5_.refs_1_, ...), custom_call_target="tpu_custom_call" | custom-call | flops 16099999744 | bytes 1000000 | tf_op jit(solution)/shard_map/pallas_call | solution.py:737
  318.8 7.2 %collective-permute-done.60 = bf16[2,96,512]{2,1,0:T(8,128)(2,1)S(1)} collective-permute-done((bf16[2,96,512]{2,1,0:T(8,128)(2,1)S(1)}, bf16[2,96,512]{2,1,0:T(8,128)(2,1)S(1)}, u32[]{:S(2)}, u32[]{:S(2)}) %collective-permute-start.60) | collective-permute-done | bytes 196640 | tf_op jit(solution)/shard_map/ppermute | solution.py:805
  333.1 9.5 %collective-permute-done.50 = bf16[1,4,96,768]{3,2,1,0:T(8,128)(2,1)} collective-permute-done((bf16[1,4,96,768]{3,2,1,0:T(8,128)(2,1)}, bf16[1,4,96,768]{3,2,1,0:T(8,128)(2,1)}, u32[]{:S(2)}, u32[]{:S(2)}) %collective-permute-start.50) | collective-permute-done | bytes 589856 | tf_op jit(solution)/shard_map/ppermute | solution.py:805
  343.5 4.1 shard_map.586.refs_3_.refs_1_
  347.6 4.2 collective-permute-done.48.refs_2_
  352.6 3.1 shard_map.587
  356.6 7.4 %shard_map.588 = (bf16[4,96,896]{2,1,0:T(8,128)(2,1)}, bf16[4,96,896]{2,1,0:T(8,128)(2,1)}) custom-call(s32[24]{0:T(128)} %concatenate.89.refs_0_.sc, bf16[512,768]{1,0:T(8,128)(2,1)} %get-tuple-element.168.refs_1_, bf16[2,512,768]{2,1,0:T(8,128)(2,1)} %copy-done.3, bf16[512,768]{1,0:T(8,128)(2,1)} %copy-done.28, f32[512,768]{1,0:T(8,128)} %get-tuple-element.171.refs_4_, ...), custom_call_target="tpu_custom_call" | custom-call | flops 6899999744 | bytes 1000000 | tf_op jit(solution)/shard_map/pallas_call | solution.py:737
  366.0 3.3 collective-permute-done.61
  369.3 11.1 %collective-permute-start.62 = (bf16[96,512]{1,0:T(8,128)(2,1)S(1)}, bf16[96,512]{1,0:T(8,128)(2,1)S(1)}, u32[]{:S(2)}, u32[]{:S(2)}) collective-permute-start(bf16[96,512]{1,0:T(8,128)(2,1)S(1)} %fusion.6), channel_id=1, source_target_pairs={{0,2},{1,3},{2,0},{3,1},{4,6},{5,7},{6,4},{7,5},{8,10},{9,11},{10,... | collective-permute-start | bytes 294920 | tf_op jit(solution)/shard_map/ppermute | solution.py:805
  381.0 4.2 collective-permute-done.62
  386.8 4.4 shard_map.589
  391.8 2.7 collective-permute-start.56
  396.3 2.4 shard_map.591
  403.1 2.7 shard_map.590
  407.3 19.8 %collective-permute-done.55.refs_3_ = bf16[96,1728]{1,0:T(8,128)(2,1)S(1)} collective-permute-done((bf16[96,1728]{1,0:T(8,128)(2,1)S(1)}, bf16[96,1728]{1,0:T(8,128)(2,1)S(1)}, u32[]{:S(2)}, u32[]{:S(2)}) %collective-permute-start.55) | collective-permute-done | bytes 331808 | tf_op jit(solution)/shard_map/ppermute | solution.py:805
  427.2 2.6 collective-permute-done.59.refs_6_
  430.5 3.8 shard_map.592
  439.3 3.3 collective-permute-start.64
  445.7 2.5 shard_map.594
  453.5 2.5 collective-permute-done.69
  456.0 4.1 collective-permute-done.68
  463.4 2.7 collective-permute-start.73
  470.3 6.6 %shard_map.595 = (f32[8,128]{1,0:T(8,128)}, f32[96,576]{1,0:T(8,128)}, f32[96,576]{1,0:T(8,128)}, f32[96,576]{1,0:T(8,128)}, f32[192,96]{1,0:T(8,128)}, /*index=...) custom-call(f32[8,128]{1,0:T(8,128)} %add_add_fusion.stats, ...), custom_call_target="tpu_custom_call" | custom-call | flops 6899999744 | bytes 1000000 | tf_op jit(solution)/shard_map/pallas_call | solution.py:770
  (358 shorter events, 116.1 us)
Async XLA Ops:
  7.2 23.5 %collective-permute-start.11 = (bf16[96,192]{1,0:T(8,128)(2,1)}, bf16[96,192]{1,0:T(8,128)(2,1)S(1)}, u32[]{:S(2)}, u32[]{:S(2)}) collective-permute-start(bf16[96,192]{1,0:T(8,128)(2,1)} %get-tuple-element.129.refs_2_), channel_id=1, source_target_pairs={{0,3},{1,2},{2,1},{3,0},{4,7},{5,6},{6,5},{7,4},{8,11},{9,10},{10,... | collective-permute-start | bytes 110600 | tf_op jit(solution)/shard_map/ppermute | solution.py:805
  12.4 20.9 %collective-permute-start.10 = (bf16[96,192]{1,0:T(8,128)(2,1)}, bf16[96,192]{1,0:T(8,128)(2,1)S(1)}, u32[]{:S(2)}, u32[]{:S(2)}) collective-permute-start(bf16[96,192]{1,0:T(8,128)(2,1)} %get-tuple-element.129.refs_2_), channel_id=1, source_target_pairs={{0,2},{1,3},{2,0},{3,1},{4,6},{5,7},{6,4},{7,5},{8,10},{9,11},{10,... | collective-permute-start | bytes 110600 | tf_op jit(solution)/shard_map/ppermute | solution.py:805
  12.4 21.4 %collective-permute-start.13 = (bf16[96,576]{1,0:T(8,128)(2,1)}, bf16[96,576]{1,0:T(8,128)(2,1)S(1)}, u32[]{:S(2)}, u32[]{:S(2)}) collective-permute-start(bf16[96,576]{1,0:T(8,128)(2,1)} %get-tuple-element.132), channel_id=1, source_target_pairs={{0,0},{1,1},{2,4},{3,5},{4,2},{5,3},{6,6},{7,7},{8,8},{9,9},{10,12... | collective-permute-start | bytes 331784 | tf_op jit(solution)/shard_map/ppermute | solution.py:887
  13.9 21.1 %collective-permute-start.12 = (bf16[96,576]{1,0:T(8,128)(2,1)}, bf16[96,576]{1,0:T(8,128)(2,1)S(1)}, u32[]{:S(2)}, u32[]{:S(2)}) collective-permute-start(bf16[96,576]{1,0:T(8,128)(2,1)} %get-tuple-element.132), channel_id=1, source_target_pairs={{0,2},{1,3},{2,6},{3,7},{4,0},{5,1},{6,4},{7,5},{8,10},{9,11},{10,... | collective-permute-start | bytes 331784 | tf_op jit(solution)/shard_map/ppermute | solution.py:888
  21.2 29.0 %collective-permute-start.1 = (bf16[2048,768]{1,0:T(8,128)(2,1)}, bf16[2048,768]{1,0:T(8,128)(2,1)}, u32[]{:S(2)}, u32[]{:S(2)}) collective-permute-start(bf16[2048,768]{1,0:T(8,128)(2,1)} %refs_7_.1), channel_id=1, source_target_pairs={{0,4},{1,5},{6,2},{7,3},{8,12},{9,13},{14,10},{15,11},{16,20},{17,... | collective-permute-start | bytes 9437192 | tf_op jit(solution)/shard_map/ppermute | solution.py:862
  43.4 19.0 %collective-permute-start.19 = (bf16[2,96,768]{2,1,0:T(8,128)(2,1)S(1)}, bf16[2,96,768]{2,1,0:T(8,128)(2,1)S(1)}, u32[]{:S(2)}, u32[]{:S(2)}) collective-permute-start(bf16[2,96,768]{2,1,0:T(8,128)(2,1)S(1)} %copy-done.41), channel_id=1, source_target_pairs={{0,3},{1,2},{2,1},{3,0},{4,7},{5,6},{6,5},{7,4},{8,11},{9,10},{10,... | collective-permute-start | bytes 884744 | tf_op jit(solution)/shard_map/ppermute | solution.py:805
  44.6 27.5 %collective-permute-start.18 = (bf16[2,96,768]{2,1,0:T(8,128)(2,1)S(1)}, bf16[2,96,768]{2,1,0:T(8,128)(2,1)S(1)}, u32[]{:S(2)}, u32[]{:S(2)}) collective-permute-start(bf16[2,96,768]{2,1,0:T(8,128)(2,1)S(1)} %copy-done.41), channel_id=1, source_target_pairs={{0,2},{1,3},{2,0},{3,1},{4,6},{5,7},{6,4},{7,5},{8,10},{9,11},{10,... | collective-permute-start | bytes 884744 | tf_op jit(solution)/shard_map/ppermute | solution.py:805
  45.7 28.7 %collective-permute-start.17 = (bf16[2,96,768]{2,1,0:T(8,128)(2,1)S(1)}, bf16[2,96,768]{2,1,0:T(8,128)(2,1)S(1)}, u32[]{:S(2)}, u32[]{:S(2)}) collective-permute-start(bf16[2,96,768]{2,1,0:T(8,128)(2,1)S(1)} %copy-done.41), channel_id=1, source_target_pairs={{0,1},{1,0},{2,3},{3,2},{4,5},{5,4},{6,7},{7,6},{8,9},{9,8},{10,11... | collective-permute-start | bytes 884744 | tf_op jit(solution)/shard_map/ppermute | solution.py:805
  47.9 29.3 %collective-permute-start.16 = (bf16[192,576]{1,0:T(8,128)(2,1)S(1)}, bf16[192,576]{1,0:T(8,128)(2,1)S(1)}, u32[]{:S(2)}, u32[]{:S(2)}) collective-permute-start(bf16[192,576]{1,0:T(8,128)(2,1)S(1)} %maximum_select_fusion.10.refs_7_), channel_id=1, source_target_pairs={{0,24},{1,25},{2,26},{3,27},{4,28},{5,29},{6,30},{7,31},{8,16},{9,... | collective-permute-start | bytes 663560 | tf_op jit(solution)/shard_map/ppermute | solution.py:805
  50.2 29.0 %collective-permute-start.25 = (bf16[96,3328]{1,0:T(8,128)(2,1)}, bf16[96,3328]{1,0:T(8,128)(2,1)}, u32[]{:S(2)}, u32[]{:S(2)}) collective-permute-start(bf16[96,3328]{1,0:T(8,128)(2,1)} %shard_map.572.refs_12_.rest_0_), channel_id=1, source_target_pairs={{0,24},{1,25},{2,26},{3,27},{4,28},{5,29},{6,30},{7,31},{8,16},{9,... | collective-permute-start | bytes 1916936 | tf_op jit(solution)/shard_map/ppermute | solution.py:805
  62.5 15.4 %collective-permute-start.15 = (bf16[192,576]{1,0:T(8,128)(2,1)S(1)}, bf16[192,576]{1,0:T(8,128)(2,1)S(1)}, u32[]{:S(2)}, u32[]{:S(2)}) collective-permute-start(bf16[192,576]{1,0:T(8,128)(2,1)S(1)} %maximum_select_fusion.10.refs_7_), channel_id=1, source_target_pairs={{0,16},{1,17},{2,18},{3,19},{4,20},{5,21},{6,22},{7,23},{8,24},{9,... | collective-permute-start | bytes 663560 | tf_op jit(solution)/shard_map/ppermute | solution.py:805
  74.4 43.1 %collective-permute-start.26 = (bf16[96,3328]{1,0:T(8,128)(2,1)}, bf16[96,3328]{1,0:T(8,128)(2,1)S(1)}, u32[]{:S(2)}, u32[]{:S(2)}) collective-permute-start(bf16[96,3328]{1,0:T(8,128)(2,1)} %shard_map.572.refs_12_.rest_0_), channel_id=1, source_target_pairs={{0,4},{1,5},{2,6},{3,7},{4,0},{5,1},{6,2},{7,3},{8,12},{9,13},{10,... | collective-permute-start | bytes 1916936 | tf_op jit(solution)/shard_map/ppermute | solution.py:805
  77.2 40.4 %collective-permute-start.24 = (bf16[96,3328]{1,0:T(8,128)(2,1)}, bf16[96,3328]{1,0:T(8,128)(2,1)S(1)}, u32[]{:S(2)}, u32[]{:S(2)}) collective-permute-start(bf16[96,3328]{1,0:T(8,128)(2,1)} %shard_map.572.refs_12_.rest_0_), channel_id=1, source_target_pairs={{0,16},{1,17},{2,18},{3,19},{4,20},{5,21},{6,22},{7,23},{8,24},{9,... | collective-permute-start | bytes 1916936 | tf_op jit(solution)/shard_map/ppermute | solution.py:805
  77.8 41.3 %collective-permute-start.23 = (bf16[96,3328]{1,0:T(8,128)(2,1)}, bf16[96,3328]{1,0:T(8,128)(2,1)}, u32[]{:S(2)}, u32[]{:S(2)}) collective-permute-start(bf16[96,3328]{1,0:T(8,128)(2,1)} %shard_map.572.refs_12_.rest_0_), channel_id=1, source_target_pairs={{0,8},{1,9},{2,10},{3,11},{4,12},{5,13},{6,14},{7,15},{8,0},{9,1},... | collective-permute-start | bytes 1916936 | tf_op jit(solution)/shard_map/ppermute | solution.py:805
  79.3 41.8 %collective-permute-start.29 = (bf16[96,3328]{1,0:T(8,128)(2,1)}, bf16[96,3328]{1,0:T(8,128)(2,1)S(1)}, u32[]{:S(2)}, u32[]{:S(2)}) collective-permute-start(bf16[96,3328]{1,0:T(8,128)(2,1)} %collective-permute-done.25.rest_3_), channel_id=1, source_target_pairs={{0,4},{1,5},{2,6},{3,7},{4,0},{5,1},{6,2},{7,3},{8,12},{9,13},{10,... | collective-permute-start | bytes 1916936 | tf_op jit(solution)/shard_map/ppermute | solution.py:805
  117.5 23.5 %collective-permute-start.32 = (bf16[6,96,768]{2,1,0:T(8,128)(2,1)S(1)}, bf16[6,96,768]{2,1,0:T(8,128)(2,1)S(1)}, u32[]{:S(2)}, u32[]{:S(2)}) collective-permute-start(bf16[6,96,768]{2,1,0:T(8,128)(2,1)S(1)} %copy-done.20), channel_id=1, source_target_pairs={{0,24},{1,25},{2,26},{3,27},{4,28},{5,29},{6,30},{7,31},{8,16},{9,... | collective-permute-start | bytes 2654216 | tf_op jit(solution)/shard_map/ppermute | solution.py:805
  117.6 40.6 %collective-permute-start.31 = (bf16[6,96,768]{2,1,0:T(8,128)(2,1)S(1)}, bf16[6,96,768]{2,1,0:T(8,128)(2,1)S(1)}, u32[]{:S(2)}, u32[]{:S(2)}) collective-permute-start(bf16[6,96,768]{2,1,0:T(8,128)(2,1)S(1)} %copy-done.20), channel_id=1, source_target_pairs={{0,16},{1,17},{2,18},{3,19},{4,20},{5,21},{6,22},{7,23},{8,24},{9,... | collective-permute-start | bytes 2654216 | tf_op jit(solution)/shard_map/ppermute | solution.py:805
  119.1 39.1 %collective-permute-start.30 = (bf16[6,96,768]{2,1,0:T(8,128)(2,1)S(1)}, bf16[6,96,768]{2,1,0:T(8,128)(2,1)S(1)}, u32[]{:S(2)}, u32[]{:S(2)}) collective-permute-start(bf16[6,96,768]{2,1,0:T(8,128)(2,1)S(1)} %copy-done.20), channel_id=1, source_target_pairs={{0,8},{1,9},{2,10},{3,11},{4,12},{5,13},{6,14},{7,15},{8,0},{9,1},... | collective-permute-start | bytes 2654216 | tf_op jit(solution)/shard_map/ppermute | solution.py:805
  121.1 9.8 %collective-permute-start.22 = (bf16[512,192]{1,0:T(8,128)(2,1)S(1)}, bf16[512,192]{1,0:T(8,128)(2,1)S(1)}, u32[]{:S(2)}, u32[]{:S(2)}) collective-permute-start(bf16[512,192]{1,0:T(8,128)(2,1)S(1)} %get-tuple-element.241), channel_id=1, source_target_pairs={{0,1},{1,0},{2,3},{3,2},{4,5},{5,4},{6,7},{7,6},{8,9},{9,8},{10,11... | collective-permute-start | bytes 589832 | tf_op jit(solution)/shard_map/ppermute | solution.py:805
  130.9 27.9 %collective-permute-start.27 = (bf16[96,3328]{1,0:T(8,128)(2,1)}, bf16[96,3328]{1,0:T(8,128)(2,1)}, u32[]{:S(2)}, u32[]{:S(2)}) collective-permute-start(bf16[96,3328]{1,0:T(8,128)(2,1)} %collective-permute-done.23.rest_1_), channel_id=1, source_target_pairs={{0,4},{1,5},{2,6},{3,7},{4,0},{5,1},{6,2},{7,3},{8,12},{9,13},{10,... | collective-permute-start | bytes 1916936 | tf_op jit(solution)/shard_map/ppermute | solution.py:805
  135.4 32.7 %collective-permute-start.33 = (bf16[6,96,768]{2,1,0:T(8,128)(2,1)S(1)}, bf16[6,96,768]{2,1,0:T(8,128)(2,1)S(1)}, u32[]{:S(2)}, u32[]{:S(2)}) collective-permute-start(bf16[6,96,768]{2,1,0:T(8,128)(2,1)S(1)} %copy-done.20), channel_id=1, source_target_pairs={{0,4},{1,5},{2,6},{3,7},{4,0},{5,1},{6,2},{7,3},{8,12},{9,13},{10,... | collective-permute-start | bytes 2654216 | tf_op jit(solution)/shard_map/ppermute | solution.py:805
  141.0 27.0 %collective-permute-start.36 = (bf16[6,96,768]{2,1,0:T(8,128)(2,1)S(1)}, bf16[6,96,768]{2,1,0:T(8,128)(2,1)S(1)}, u32[]{:S(2)}, u32[]{:S(2)}) collective-permute-start(bf16[6,96,768]{2,1,0:T(8,128)(2,1)S(1)} %collective-permute-done.32.rest_3_.rest_11_), channel_id=1, source_target_pairs={{0,4},{1,5},{2,6},{3,7},{4,0},{5,1},{6,2},{7,3},{8,12},{9,13},{10,... | collective-permute-start | bytes 2654216 | tf_op jit(solution)/shard_map/ppermute | solution.py:805
  158.2 9.8 %collective-permute-start.35 = (bf16[6,96,768]{2,1,0:T(8,128)(2,1)S(1)}, bf16[6,96,768]{2,1,0:T(8,128)(2,1)S(1)}, u32[]{:S(2)}, u32[]{:S(2)}) collective-permute-start(bf16[6,96,768]{2,1,0:T(8,128)(2,1)S(1)} %collective-permute-done.31.rest_2_.rest_10_), channel_id=1, source_target_pairs={{0,4},{1,5},{2,6},{3,7},{4,0},{5,1},{6,2},{7,3},{8,12},{9,13},{10,... | collective-permute-start | bytes 2654216 | tf_op jit(solution)/shard_map/ppermute | solution.py:805
  158.2 9.8 %collective-permute-start.34 = (bf16[6,96,768]{2,1,0:T(8,128)(2,1)S(1)}, bf16[6,96,768]{2,1,0:T(8,128)(2,1)S(1)}, u32[]{:S(2)}, u32[]{:S(2)}) collective-permute-start(bf16[6,96,768]{2,1,0:T(8,128)(2,1)S(1)} %collective-permute-done.30.rest_1_.rest_9_), channel_id=1, source_target_pairs={{0,4},{1,5},{2,6},{3,7},{4,0},{5,1},{6,2},{7,3},{8,12},{9,13},{10,... | collective-permute-start | bytes 2654216 | tf_op jit(solution)/shard_map/ppermute | solution.py:805
  231.0 16.7 %collective-permute-start.42 = (bf16[4,5,96,768]{3,2,1,0:T(8,128)(2,1)}, bf16[4,5,96,768]{3,2,1,0:T(8,128)(2,1)S(1)}, u32[]{:S(2)}, u32[]{:S(2)}) collective-permute-start(bf16[4,5,96,768]{3,2,1,0:T(8,128)(2,1)} %get-tuple-element.157), channel_id=1, source_target_pairs={{0,4},{1,5},{2,6},{3,7},{4,0},{5,1},{6,2},{7,3},{8,12},{9,13},{10,... | collective-permute-start | bytes 8847368 | tf_op jit(solution)/shard_map/ppermute | solution.py:805
  231.1 16.6 %collective-permute-start.43 = (bf16[4,4,96,768]{3,2,1,0:T(8,128)(2,1)}, bf16[4,4,96,768]{3,2,1,0:T(8,128)(2,1)S(1)}, u32[]{:S(2)}, u32[]{:S(2)}) collective-permute-start(bf16[4,4,96,768]{3,2,1,0:T(8,128)(2,1)} %get-tuple-element.159), channel_id=1, source_target_pairs={{0,4},{1,5},{2,6},{3,7},{4,0},{5,1},{6,2},{7,3},{8,12},{9,13},{10,... | collective-permute-start | bytes 7077896 | tf_op jit(solution)/shard_map/ppermute | solution.py:805
  232.6 9.2 %collective-permute-start.41 = (bf16[512,192]{1,0:T(8,128)(2,1)S(1)}, bf16[512,192]{1,0:T(8,128)(2,1)S(1)}, u32[]{:S(2)}, u32[]{:S(2)}) collective-permute-start(bf16[512,192]{1,0:T(8,128)(2,1)S(1)} %get-tuple-element.237), channel_id=1, source_target_pairs={{0,1},{1,0},{2,3},{3,2},{4,5},{5,4},{6,7},{7,6},{8,9},{9,8},{10,11... | collective-permute-start | bytes 589832 | tf_op jit(solution)/shard_map/ppermute | solution.py:805
  234.6 11.5 %collective-permute-start.39 = (bf16[512,192]{1,0:T(8,128)(2,1)S(1)}, bf16[512,192]{1,0:T(8,128)(2,1)S(1)}, u32[]{:S(2)}, u32[]{:S(2)}) collective-permute-start(bf16[512,192]{1,0:T(8,128)(2,1)S(1)} %get-tuple-element.235), channel_id=1, source_target_pairs={{0,5},{1,4},{2,7},{3,6},{4,1},{5,0},{6,3},{7,2},{8,13},{9,12},{10,... | collective-permute-start | bytes 589832 | tf_op jit(solution)/shard_map/ppermute | solution.py:805
  234.6 11.5 %collective-permute-start.40 = (bf16[512,192]{1,0:T(8,128)(2,1)S(1)}, bf16[512,192]{1,0:T(8,128)(2,1)S(1)}, u32[]{:S(2)}, u32[]{:S(2)}) collective-permute-start(bf16[512,192]{1,0:T(8,128)(2,1)S(1)} %get-tuple-element.238), channel_id=1, source_target_pairs={{0,4},{1,5},{2,6},{3,7},{4,0},{5,1},{6,2},{7,3},{8,12},{9,13},{10,... | collective-permute-start | bytes 589832 | tf_op jit(solution)/shard_map/ppermute | solution.py:805
  258.4 36.6 %collective-permute-start.45 = (bf16[2,4,96,768]{3,2,1,0:T(8,128)(2,1)}, bf16[2,4,96,768]{3,2,1,0:T(8,128)(2,1)S(1)}, u32[]{:S(2)}, u32[]{:S(2)}) collective-permute-start(bf16[2,4,96,768]{3,2,1,0:T(8,128)(2,1)} %get-tuple-element.161.refs_7_), channel_id=1, source_target_pairs={{0,16},{1,17},{2,18},{3,19},{4,20},{5,21},{6,22},{7,23},{8,24},{9,... | collective-permute-start | bytes 3538952 | tf_op jit(solution)/shard_map/ppermute | solution.py:805
  259.3 35.7 %collective-permute-start.44 = (bf16[2,5,96,768]{3,2,1,0:T(8,128)(2,1)}, bf16[2,5,96,768]{3,2,1,0:T(8,128)(2,1)S(1)}, u32[]{:S(2)}, u32[]{:S(2)}) collective-permute-start(bf16[2,5,96,768]{3,2,1,0:T(8,128)(2,1)} %get-tuple-element.160.refs_6_), channel_id=1, source_target_pairs={{0,8},{1,9},{2,10},{3,11},{4,12},{5,13},{6,14},{7,15},{8,0},{9,1},... | collective-permute-start | bytes 4423688 | tf_op jit(solution)/shard_map/ppermute | solution.py:805
  318.5 10.5 %collective-permute-start.46 = (bf16[2,512,768]{2,1,0:T(8,128)(2,1)}, bf16[2,512,768]{2,1,0:T(8,128)(2,1)S(1)}, u32[]{:S(2)}, u32[]{:S(2)}) collective-permute-start(bf16[2,512,768]{2,1,0:T(8,128)(2,1)} %get-tuple-element.169), channel_id=1, source_target_pairs={{0,4},{1,5},{2,6},{3,7},{4,0},{5,1},{6,2},{7,3},{8,12},{9,13},{10,... | collective-permute-start | bytes 4718600 | tf_op jit(solution)/shard_map/ppermute | solution.py:805
  318.7 23.9 %collective-permute-start.49 = (bf16[1,5,96,768]{3,2,1,0:T(8,128)(2,1)S(1)}, bf16[1,5,96,768]{3,2,1,0:T(8,128)(2,1)S(1)}, u32[]{:S(2)}, u32[]{:S(2)}) collective-permute-start(bf16[1,5,96,768]{3,2,1,0:T(8,128)(2,1)S(1)} %copy-done.29), channel_id=1, source_target_pairs={{0,16},{1,17},{2,18},{3,19},{4,20},{5,21},{6,22},{7,23},{8,24},{9,... | collective-permute-start | bytes 2211848 | tf_op jit(solution)/shard_map/ppermute | solution.py:805
  326.0 16.6 %collective-permute-start.50 = (bf16[1,4,96,768]{3,2,1,0:T(8,128)(2,1)}, bf16[1,4,96,768]{3,2,1,0:T(8,128)(2,1)}, u32[]{:S(2)}, u32[]{:S(2)}) collective-permute-start(bf16[1,4,96,768]{3,2,1,0:T(8,128)(2,1)} %get-tuple-element.167.refs_12_), channel_id=1, source_target_pairs={{0,8},{1,9},{2,10},{3,11},{4,12},{5,13},{6,14},{7,15},{8,0},{9,1},... | collective-permute-start | bytes 1769480 | tf_op jit(solution)/shard_map/ppermute | solution.py:805
  327.2 24.6 %collective-permute-start.48 = (bf16[2,192,576]{2,1,0:T(8,128)(2,1)}, bf16[2,192,576]{2,1,0:T(8,128)(2,1)S(1)}, u32[]{:S(2)}, u32[]{:S(2)}) collective-permute-start(bf16[2,192,576]{2,1,0:T(8,128)(2,1)} %get-tuple-element.175), channel_id=1, source_target_pairs={{0,8},{1,9},{2,10},{3,11},{4,12},{5,13},{6,14},{7,15},{8,0},{9,1},... | collective-permute-start | bytes 1327112 | tf_op jit(solution)/shard_map/ppermute | solution.py:805
  330.9 24.8 %collective-permute-start.47 = (bf16[512,768]{1,0:T(8,128)(2,1)S(1)}, bf16[512,768]{1,0:T(8,128)(2,1)S(1)}, u32[]{:S(2)}, u32[]{:S(2)}) collective-permute-start(bf16[512,768]{1,0:T(8,128)(2,1)S(1)} %fusion), channel_id=1, source_target_pairs={{0,1},{1,0},{2,3},{3,2},{4,5},{5,4},{6,7},{7,6},{8,9},{9,8},{10,11... | collective-permute-start | bytes 2359304 | tf_op jit(solution)/shard_map/ppermute | solution.py:805
  363.9 21.9 %collective-permute-start.51 = (bf16[4,96,896]{2,1,0:T(8,128)(2,1)}, bf16[4,96,896]{2,1,0:T(8,128)(2,1)S(1)}, u32[]{:S(2)}, u32[]{:S(2)}) collective-permute-start(bf16[4,96,896]{2,1,0:T(8,128)(2,1)} %get-tuple-element.180), channel_id=1, source_target_pairs={{0,4},{1,5},{2,6},{3,7},{4,0},{5,1},{6,2},{7,3},{8,12},{9,13},{10,... | collective-permute-start | bytes 2064392 | tf_op jit(solution)/shard_map/ppermute | solution.py:805
  369.3 15.9 %collective-permute-start.62 = (bf16[96,512]{1,0:T(8,128)(2,1)S(1)}, bf16[96,512]{1,0:T(8,128)(2,1)S(1)}, u32[]{:S(2)}, u32[]{:S(2)}) collective-permute-start(bf16[96,512]{1,0:T(8,128)(2,1)S(1)} %fusion.6), channel_id=1, source_target_pairs={{0,2},{1,3},{2,0},{3,1},{4,6},{5,7},{6,4},{7,5},{8,10},{9,11},{10,... | collective-permute-start | bytes 294920 | tf_op jit(solution)/shard_map/ppermute | solution.py:805
  385.2 13.5 %collective-permute-start.63 = (f32[96,512]{1,0:T(8,128)S(1)}, f32[96,512]{1,0:T(8,128)S(1)}, u32[]{:S(2)}, u32[]{:S(2)}) collective-permute-start(f32[96,512]{1,0:T(8,128)S(1)} %convert_add_fusion.2.refs_7_), channel_id=1, source_target_pairs={{0,1},{1,0},{2,3},{3,2},{4,5},{5,4},{6,7},{7,6},{8,9},{9,8},{10,11... | collective-permute-start | bytes 589832 | tf_op jit(solution)/shard_map/ppermute | solution.py:805
  385.3 10.0 %collective-permute-start.57 = (bf16[1,192,576]{2,1,0:T(8,128)(2,1)S(1)}, bf16[1,192,576]{2,1,0:T(8,128)(2,1)S(1)}, u32[]{:S(2)}, u32[]{:S(2)}) collective-permute-start(bf16[1,192,576]{2,1,0:T(8,128)(2,1)S(1)} %copy-done.48), channel_id=1, source_target_pairs={{0,16},{1,17},{2,18},{3,19},{4,20},{5,21},{6,22},{7,23},{8,24},{9,... | collective-permute-start | bytes 663560 | tf_op jit(solution)/shard_map/ppermute | solution.py:805
  391.1 9.8 %collective-permute-start.52 = (bf16[2,96,896]{2,1,0:T(8,128)(2,1)}, bf16[2,96,896]{2,1,0:T(8,128)(2,1)S(1)}, u32[]{:S(2)}, u32[]{:S(2)}) collective-permute-start(bf16[2,96,896]{2,1,0:T(8,128)(2,1)} %get-tuple-element.182.refs_3_), channel_id=1, source_target_pairs={{0,8},{1,9},{2,10},{3,11},{4,12},{5,13},{6,14},{7,15},{8,0},{9,1},... | collective-permute-start | bytes 1032200 | tf_op jit(solution)/shard_map/ppermute | solution.py:805
  391.8 13.9 %collective-permute-start.56 = (bf16[96,1728]{1,0:T(8,128)(2,1)S(1)}, bf16[96,1728]{1,0:T(8,128)(2,1)S(1)}, u32[]{:S(2)}, u32[]{:S(2)}) collective-permute-start(bf16[96,1728]{1,0:T(8,128)(2,1)S(1)} %get-tuple-element.232), channel_id=1, source_target_pairs={{0,3},{1,2},{2,1},{3,0},{4,7},{5,6},{6,5},{7,4},{8,11},{9,10},{10,... | collective-permute-start | bytes 995336 | tf_op jit(solution)/shard_map/ppermute | solution.py:805
  394.5 32.6 %collective-permute-start.55 = (bf16[96,1728]{1,0:T(8,128)(2,1)S(1)}, bf16[96,1728]{1,0:T(8,128)(2,1)S(1)}, u32[]{:S(2)}, u32[]{:S(2)}) collective-permute-start(bf16[96,1728]{1,0:T(8,128)(2,1)S(1)} %get-tuple-element.233), channel_id=1, source_target_pairs={{0,2},{1,3},{2,0},{3,1},{4,6},{5,7},{6,4},{7,5},{8,10},{9,11},{10,... | collective-permute-start | bytes 995336 | tf_op jit(solution)/shard_map/ppermute | solution.py:805
  395.3 31.9 %collective-permute-start.54 = (bf16[96,1728]{1,0:T(8,128)(2,1)S(1)}, bf16[96,1728]{1,0:T(8,128)(2,1)S(1)}, u32[]{:S(2)}, u32[]{:S(2)}) collective-permute-start(bf16[96,1728]{1,0:T(8,128)(2,1)S(1)} %get-tuple-element.234), channel_id=1, source_target_pairs={{0,1},{1,0},{2,3},{3,2},{4,5},{5,4},{6,7},{7,6},{8,9},{9,8},{10,11... | collective-permute-start | bytes 995336 | tf_op jit(solution)/shard_map/ppermute | solution.py:805
  398.7 28.4 %collective-permute-start.58 = (bf16[96,576]{1,0:T(8,128)(2,1)}, bf16[96,576]{1,0:T(8,128)(2,1)S(1)}, u32[]{:S(2)}, u32[]{:S(2)}) collective-permute-start(bf16[96,576]{1,0:T(8,128)(2,1)} %get-tuple-element.186), channel_id=1, source_target_pairs={{0,0},{1,1},{2,4},{3,5},{4,2},{5,3},{6,6},{7,7},{8,8},{9,9},{10,12... | collective-permute-start | bytes 331784 | tf_op jit(solution)/shard_map/ppermute | solution.py:1341
  400.9 28.9 %collective-permute-start.59 = (bf16[96,576]{1,0:T(8,128)(2,1)}, bf16[96,576]{1,0:T(8,128)(2,1)S(1)}, u32[]{:S(2)}, u32[]{:S(2)}) collective-permute-start(bf16[96,576]{1,0:T(8,128)(2,1)} %get-tuple-element.187), channel_id=1, source_target_pairs={{0,4},{1,5},{2,0},{3,1},{4,6},{5,7},{6,2},{7,3},{8,12},{9,13},{10,... | collective-permute-start | bytes 331784 | tf_op jit(solution)/shard_map/ppermute | solution.py:1342
  405.7 28.5 %collective-permute-start.53 = (bf16[1,96,896]{2,1,0:T(8,128)(2,1)}, bf16[1,96,896]{2,1,0:T(8,128)(2,1)S(1)}, u32[]{:S(2)}, u32[]{:S(2)}) collective-permute-start(bf16[1,96,896]{2,1,0:T(8,128)(2,1)} %get-tuple-element.184.refs_9_), channel_id=1, source_target_pairs={{0,16},{1,17},{2,18},{3,19},{4,20},{5,21},{6,22},{7,23},{8,24},{9,... | collective-permute-start | bytes 516104 | tf_op jit(solution)/shard_map/ppermute | solution.py:805
  450.2 9.9 %collective-permute-start.68 = (f32[32,896]{1,0:T(8,128)}, f32[32,896]{1,0:T(8,128)S(1)}, u32[]{:S(2)}, u32[]{:S(2)}) collective-permute-start(f32[32,896]{1,0:T(8,128)} %shard_map.594), channel_id=1, source_target_pairs={{0,2},{1,3},{2,0},{3,1},{4,6},{5,7},{6,4},{7,5},{8,10},{9,11},{10,... | collective-permute-start | bytes 344072 | tf_op jit(solution)/shard_map/ppermute | solution.py:805
  (96 other events, 807.1 us)
